TPU v7x, 256 devices: a whole 4x4x8 slice. The times are simulated.
256 devices in a mesh: dp: 32 (over y, x, core), expert: 8 (over z).
Axes of the slice: x: 4, y: 4, z: 8, core: 2. Of those that a mesh axis runs over, the one named last changes fastest.
Arguments:
- hidden_in: bfloat16 [32768, 2048], P(('dp', 'expert')), may hold values from -6 to 6
- resid_in: bfloat16 [32768, 2048], P(('dp', 'expert')), may hold values from -12 to 12
- route_ids: int32 [32768, 2], P(('dp', 'expert')), may hold values from 0 to 7, all different within a row; in each aligned block of 128 rows (0 to 127, 128 to 255, ...) at most 48 rows name the same one
- route_weight: float32 [32768, 2], P(('dp', 'expert')), may hold values from 0.05 to 0.6
- returns: float32 [32768], P(('dp', 'expert')), may hold values from -40 to 50
- run_moments: float32 [2], replicated, may hold values from 0.5 to 2
- gate_w: bfloat16 [8, 2048, 768], P('expert'), may hold values from -0.125 to 0.125
- up_w: bfloat16 [8, 2048, 768], P('expert'), may hold values from -0.125 to 0.125
- down_w: bfloat16 [8, 768, 2048], P('expert'), may hold values from -0.21875 to 0.21875
- value_w: bfloat16 [2048, 256], replicated
Outputs:
- grad_hidden: bfloat16 [32768, 2048], P(('dp', 'expert'))
- grad_route: float32 [32768, 2], P(('dp', 'expert'))
- grad_gate: float32 [8, 2048, 768], P('expert', 'dp')
- grad_up: float32 [8, 2048, 768], P('expert', 'dp')
- grad_down: float32 [8, 768, 2048], P('expert', None, 'dp')
- grad_value: float32 [2048, 256], P(('dp', 'expert'))
Inputs may be any that keep to these rules, and one draw needn't show every extreme that they name: `route_ids`: each token names 2 different experts. Among the routes of one device no expert is named more than 48 times, and in every draw some device names some expert exactly 48 times.
All inputs are finite; a program needn't handle non-finite values.
Results may differ from a plain program's by a relative error of at most 0.024.
Values may be sent and summed in bfloat16 or wider, within the bound.
No kernel may reach another device: no remote copies, remote signals or barrier semaphores. Data moves between devices by JAX's collectives and lax.ppermute only.
A program may use at most 128 MiB of HBM per device.

v0:
```python
import math

import jax
import jax.numpy as jnp
from jax import lax
from jax.sharding import PartitionSpec as P

support_edge = 4.0
smoothing = 0.75


def soft_targets(returns, mean_value, var_value, bin_count):
    scaled = jnp.clip(
        (returns - mean_value) / jnp.sqrt(var_value + 1e-06), -support_edge, support_edge
    )
    bin_edges = -support_edge + 2.0 * support_edge / bin_count * jnp.arange(bin_count + 1).astype(
        jnp.float32
    )
    bin_sigma = smoothing * 2.0 * support_edge / bin_count
    cumulative = jax.scipy.special.erf(
        (bin_edges[None, :] - scaled[:, None]) / (math.sqrt(2.0) * bin_sigma)
    )
    bin_mass = cumulative[:, 1:] - cumulative[:, :-1]
    return bin_mass / (cumulative[:, -1:] - cumulative[:, :1])


def contract_rows(left, right):
    return lax.dot_general(
        left, right, (((0,), (0,)), ((), ())), preferred_element_type=jnp.float32
    )


def contract_cols(left, right):
    return lax.dot_general(
        left, right, (((1,), (1,)), ((), ())), preferred_element_type=jnp.float32
    )


def per_device(
    hidden_in,
    resid_in,
    route_ids,
    route_weight,
    returns,
    run_moments,
    gate_w,
    up_w,
    down_w,
    value_w,
):
    groups = lax.axis_size("expert")
    devices = lax.axis_size(("dp", "expert"))
    tok_rows, model_width = hidden_in.shape
    routes = route_ids.shape[1]
    slot_cap = 3 * tok_rows * routes // (2 * groups)
    bin_count = value_w.shape[1]
    total_sum, total_square = lax.psum(
        (jnp.sum(returns), jnp.sum(returns * returns)), ("dp", "expert")
    )
    row_count = float(tok_rows * devices)
    batch_mean = total_sum / row_count
    batch_var = total_square / row_count - batch_mean * batch_mean
    mean_value = 0.5 * (run_moments[0] + batch_mean)
    var_value = 0.5 * (run_moments[1] + batch_var) + 0.25 * (batch_mean - run_moments[0]) ** 2
    targets = soft_targets(returns, mean_value, var_value, bin_count)
    flat_ids = route_ids.reshape(-1)
    onehot = (flat_ids[:, None] == jnp.arange(groups, dtype=jnp.int32)[None, :]).astype(jnp.int32)
    position = jnp.sum((jnp.cumsum(onehot, axis=0) - onehot) * onehot, axis=1)
    slot_index = flat_ids * slot_cap + position
    slot_total = groups * slot_cap
    route_order = jnp.arange(flat_ids.shape[0], dtype=jnp.int32)
    slot_route = jnp.zeros((slot_total,), jnp.int32).at[slot_index].set(route_order)
    slot_live = (jnp.zeros((slot_total,), jnp.int32).at[slot_index].set(1) > 0)[:, None]
    zero_value = jnp.zeros((), jnp.bfloat16)
    outgoing = jnp.where(slot_live, hidden_in[slot_route // routes], zero_value).reshape(
        groups, slot_cap, model_width
    )
    in_rows = lax.all_to_all(outgoing, "expert", split_axis=0, concat_axis=0, tiled=True).reshape(
        slot_total, model_width
    )
    gate_pre = jnp.dot(in_rows, gate_w[0], preferred_element_type=jnp.float32)
    up_pre = jnp.dot(in_rows, up_w[0], preferred_element_type=jnp.float32)
    gate_sig = jax.nn.sigmoid(gate_pre)
    activation = (gate_pre * gate_sig * up_pre).astype(jnp.bfloat16)
    expert_out = jnp.dot(activation, down_w[0], preferred_element_type=jnp.float32).astype(
        jnp.bfloat16
    )
    returned = lax.all_to_all(
        expert_out.reshape(groups, slot_cap, model_width),
        "expert",
        split_axis=0,
        concat_axis=0,
        tiled=True,
    )
    route_out = returned.reshape(slot_total, model_width)[slot_index].reshape(
        tok_rows, routes, model_width
    )
    stream = resid_in.astype(jnp.float32)
    for route in range(routes):
        stream = stream + route_weight[:, route : route + 1] * route_out[:, route].astype(
            jnp.float32
        )
    features = stream.astype(jnp.bfloat16)
    logits = jnp.dot(features, value_w, preferred_element_type=jnp.float32)
    softmax_p = jax.nn.softmax(logits, axis=-1)
    logit_grad = (softmax_p - targets).astype(jnp.bfloat16)
    feature_grad = contract_cols(logit_grad, value_w)
    grad_route = jnp.stack(
        [
            jnp.sum(route_out[:, route].astype(jnp.float32) * feature_grad, axis=1)
            for route in range(routes)
        ],
        axis=1,
    )
    route_grad = (
        (route_weight[:, :, None] * feature_grad[:, None, :])
        .astype(jnp.bfloat16)
        .reshape(tok_rows * routes, model_width)
    )
    outgoing_grad = jnp.where(slot_live, route_grad[slot_route], zero_value).reshape(
        groups, slot_cap, model_width
    )
    grad_rows = lax.all_to_all(
        outgoing_grad, "expert", split_axis=0, concat_axis=0, tiled=True
    ).reshape(slot_total, model_width)
    act_grad = contract_cols(grad_rows, down_w[0])
    gate_grad = (act_grad * up_pre * gate_sig * (1.0 + gate_pre * (1.0 - gate_sig))).astype(
        jnp.bfloat16
    )
    up_grad = (act_grad * gate_pre * gate_sig).astype(jnp.bfloat16)
    input_grad = (contract_cols(gate_grad, gate_w[0]) + contract_cols(up_grad, up_w[0])).astype(
        jnp.bfloat16
    )
    returned_grad = lax.all_to_all(
        input_grad.reshape(groups, slot_cap, model_width),
        "expert",
        split_axis=0,
        concat_axis=0,
        tiled=True,
    )
    route_back = returned_grad.reshape(slot_total, model_width)[slot_index].reshape(
        tok_rows, routes, model_width
    )
    grad_hidden = jnp.sum(route_back.astype(jnp.float32), axis=1).astype(jnp.bfloat16)
    grad_gate = lax.psum_scatter(
        contract_rows(in_rows, gate_grad).astype(jnp.bfloat16),
        "dp",
        scatter_dimension=0,
        tiled=True,
    ).astype(jnp.float32)
    grad_up = lax.psum_scatter(
        contract_rows(in_rows, up_grad).astype(jnp.bfloat16), "dp", scatter_dimension=0, tiled=True
    ).astype(jnp.float32)
    down_shard = lax.psum_scatter(
        contract_rows(grad_rows, activation).astype(jnp.bfloat16),
        "dp",
        scatter_dimension=0,
        tiled=True,
    ).astype(jnp.float32)
    grad_down = down_shard.T
    head_rows = model_width // devices
    head_total = lax.psum(contract_rows(features, logit_grad), ("dp", "expert"))
    grad_value = lax.dynamic_slice_in_dim(
        head_total, lax.axis_index(("dp", "expert")) * head_rows, head_rows, 0
    )
    return (grad_hidden, grad_route, grad_gate[None], grad_up[None], grad_down[None], grad_value)


def solution(mesh):
    in_specs = (
        P(("dp", "expert"), None),
        P(("dp", "expert"), None),
        P(("dp", "expert"), None),
        P(("dp", "expert"), None),
        P(("dp", "expert")),
        P(),
        P("expert", None, None),
        P("expert", None, None),
        P("expert", None, None),
        P(),
    )
    out_specs = (
        P(("dp", "expert"), None),
        P(("dp", "expert"), None),
        P("expert", "dp", None),
        P("expert", "dp", None),
        P("expert", None, "dp"),
        P(("dp", "expert"), None),
    )
    return jax.shard_map(
        per_device, mesh=mesh, in_specs=in_specs, out_specs=out_specs, check_vma=False
    )
```

profile of v0, /device:TPU:24, one launch (start us, length us, event | category | flops | bytes accessed | tf_op | source)
XLA Modules:
  0.0 526.4 jit_solution(10191027066324917693)
XLA Ops:
  14.2 6.2 %gather_fusion = bf16[384,2048]{1,0:T(8,128)(2,1)} fusion(bf16[128,2048]{1,0:T(8,128)(2,1)} %param.10, s32[1024]{0:T(1024)S(1)} %get-tuple-element.28), kind=kCustom, calls=%fused_computation | custom fusion | bytes 3147264 | tf_op jit(solution)/shard_map/gather | solution.py:75
  22.0 48.5 %all_to_all.20 = bf16[8,48,2048]{2,1,0:T(8,128)(2,1)S(1)} all-to-all(bf16[8,48,2048]{2,1,0:T(8,128)(2,1)S(1)} %broadcast_select_fusion.1), channel_id=1, replica_groups=mesh['dp'=32,'expert'=8] {'expert'}, dimensions={0} | all-to-all | bytes 3145728 | tf_op jit(solution)/shard_map/all_to_all | solution.py:78
  78.0 4.4 all-to-all-start.1
  83.0 79.0 %all-reduce = (f32[]{:T(128)}, f32[]{:T(128)}) all-reduce(f32[]{:T(128)} %get-tuple-element.9, f32[]{:T(128)} %get-tuple-element.8), channel_id=1, replica_groups=mesh['dp'=32,'expert'=8] {'dp','expert'}, use_global_device_ids=true, to_apply=%region_10.11 | all-reduce | flops 2 | bytes 16 | tf_op jit(solution)/shard_map/psum | solution.py:57
  167.7 4.9 gather_fusion.1
  175.2 3.2 fusion.37
  183.7 3.7 mul.139
  187.4 2.7 multiply_convert_fusion
  190.1 6.4 %gather_fusion.2 = bf16[384,2048]{1,0:T(8,128)(2,1)} fusion(bf16[256,2048]{1,0:T(8,128)(2,1)} %multiply_convert_fusion, s32[1024]{0:T(1024)S(1)} %get-tuple-element.27), kind=kCustom, calls=%fused_computation.2 | custom fusion | bytes 3147264 | tf_op jit(solution)/shard_map/gather | solution.py:120
  196.6 2.7 broadcast_select_fusion
  199.3 6.0 %all-to-all-start.2 = ((bf16[8,48,2048]{2,1,0:T(8,128)(2,1)}), bf16[8,48,2048]{2,1,0:T(8,128)(2,1)}, u32[]{:S(2)}, u32[]{:S(2)}) async-start(bf16[8,48,2048]{2,1,0:T(8,128)(2,1)} %broadcast_select_fusion), calls=%async_computation.2 | async-start | bytes 3145728 | tf_op jit(solution)/shard_map/all_to_all | solution.py:123
  205.4 3.0 fusion.40
  208.7 37.5 %all-to-all-done.2 = bf16[8,48,2048]{2,1,0:T(8,128)(2,1)} async-done(((bf16[8,48,2048]{2,1,0:T(8,128)(2,1)}), bf16[8,48,2048]{2,1,0:T(8,128)(2,1)}, u32[]{:S(2)}, u32[]{:S(2)}) %all-to-all-start.2) | async-done | bytes 1572896 | tf_op jit(solution)/shard_map/all_to_all | solution.py:123
  246.2 5.1 convolution_convert_fusion
  251.4 4.8 multiply_convert_fusion.2
  256.9 3.5 convolution_convert_fusion.2
  260.5 5.1 convolution_convert_fusion.1
  265.7 3.7 fusion.4
  269.5 2.6 add_convert_fusion
  272.1 4.6 all-to-all-start.3
  277.2 203.7 %all-reduce.3.cloned.1.call-done = f32[2048,256]{1,0:T(8,128)} async-done(((f32[2048,256]{1,0:T(8,128)}), f32[2048,256]{1,0:T(8,128)}) %all-reduce.3.cloned.1.call-update) | async-done | bytes 2097168 | tf_op jit(solution)/shard_map/psum | solution.py:162
  482.2 4.9 gather_fusion.3
  489.7 4.6 reduce_sum.73
  497.4 19.8 %reduce-scatter.6.cloned.1.call-done = bf16[64,768]{1,0:T(8,128)(2,1)} async-done(((bf16[2048,768]{1,0:T(8,128)(2,1)}), bf16[64,768]{1,0:T(8,128)(2,1)}) %reduce-scatter.6.cloned.1.call-update) | async-done | bytes 98320 | tf_op jit(solution)/shard_map/reduce_scatter | solution.py:151
  (91 shorter events, 35.1 us)
Async XLA Ops:
  8.0 67.4 %copy-start = (bf16[1,768,2048]{2,1,0:T(8,128)(2,1)S(1)}, bf16[1,768,2048]{2,1,0:T(8,128)(2,1)}, u32[]{:S(2)}) copy-start(bf16[1,768,2048]{2,1,0:T(8,128)(2,1)} %param.18) | copy-start | bytes 9437188
  22.0 48.5 %copy-start.10 = (bf16[1,2048,768]{2,1,0:T(8,128)(2,1)S(1)}, bf16[1,2048,768]{2,1,0:T(8,128)(2,1)}, u32[]{:S(2)}) copy-start(bf16[1,2048,768]{2,1,0:T(8,128)(2,1)} %param.16) | copy-start | bytes 9437188
  70.5 1.4 copy-start.2
  70.5 2.5 copy-start.9
  73.0 2.4 copy-start.15
  75.4 2.6 copy-start.14
  78.0 4.5 copy-start.8
  78.0 86.0 %copy-start.7 = (f32[2]{0:T(128)S(1)}, f32[2]{0:T(128)}, u32[]{:S(2)}) copy-start(f32[2]{0:T(128)} %param.15) | copy-start | bytes 28
  78.0 89.2 %copy-start.6 = (f32[128,2]{0,1:T(2,128)S(1)}, f32[128,2]{0,1:T(2,128)}, u32[]{:S(2)}) copy-start(f32[128,2]{0,1:T(2,128)} %param.13) | copy-start | bytes 3076
  78.0 89.7 %all-to-all-start.1 = ((bf16[8,48,2048]{2,1,0:T(8,128)(2,1)}), bf16[8,48,2048]{2,1,0:T(8,128)(2,1)}, u32[]{:S(2)}, u32[]{:S(2)}) async-start(bf16[8,48,2048]{2,1,0:T(8,128)(2,1)} %bitcast.97), calls=%async_computation.1 | async-start | bytes 3145728 | tf_op jit(solution)/shard_map/all_to_all | solution.py:88
  175.2 3.2 copy-start.5
  178.4 1.2 copy-start.4
  179.6 1.5 copy-start.1
  199.3 46.9 %all-to-all-start.2 = ((bf16[8,48,2048]{2,1,0:T(8,128)(2,1)}), bf16[8,48,2048]{2,1,0:T(8,128)(2,1)}, u32[]{:S(2)}, u32[]{:S(2)}) async-start(bf16[8,48,2048]{2,1,0:T(8,128)(2,1)} %broadcast_select_fusion), calls=%async_computation.2 | async-start | bytes 3145728 | tf_op jit(solution)/shard_map/all_to_all | solution.py:123
  205.4 275.5 %all-reduce.3.cloned.1.call-start = ((), (), s32[]{:S(2)}) async-start(), calls=%async_computation.10 | async-start | bytes 4194304 | tf_op jit(solution)/shard_map/psum | solution.py:162
  208.4 285.8 %reduce-scatter.8.cloned.1.call-start = ((), (), s32[]{:S(2)}) async-start(), calls=%async_computation.9 | async-start | bytes 3244032 | tf_op jit(solution)/shard_map/reduce_scatter | solution.py:154
  251.3 244.6 %reduce-scatter.4.cloned.1.call-start = ((), (), s32[]{:S(2)}) async-start(), calls=%async_computation.7 | async-start | bytes 3244032 | tf_op jit(solution)/shard_map/reduce_scatter | solution.py:145
  251.3 5.6 %copy-start.3 = (bf16[8,48,2048]{2,1,0:T(8,128)(2,1)S(1)}, bf16[8,48,2048]{2,1,0:T(8,128)(2,1)}, u32[]{:S(2)}) copy-start(bf16[8,48,2048]{2,1,0:T(8,128)(2,1)} %copy-done.2) | copy-start | bytes 4718596
  256.1 0.8 copy-start.12
  260.5 256.7 %reduce-scatter.6.cloned.1.call-start = ((), (), s32[]{:S(2)}) async-start(), calls=%async_computation.8 | async-start | bytes 3244032 | tf_op jit(solution)/shard_map/reduce_scatter | solution.py:151
  265.7 3.8 copy-start.11
  265.7 3.8 copy-start.13
  272.1 210.1 %all-to-all-start.3 = ((bf16[8,48,2048]{2,1,0:T(8,128)(2,1)}), bf16[8,48,2048]{2,1,0:T(8,128)(2,1)}, u32[]{:S(2)}, u32[]{:S(2)}) async-start(bf16[8,48,2048]{2,1,0:T(8,128)(2,1)} %bitcast.98), calls=%async_computation.3 | async-start | bytes 3145728 | tf_op jit(solution)/shard_map/all_to_all | solution.py:134
Sparse Core Ops, SparseCore 0:
  212.4 268.4 all-reduce.2
Sparse Core Ops, SparseCore 1:
  251.4 82.5 reduce-scatter.7
  338.2 87.3 reduce-scatter.3
  429.4 87.8 reduce-scatter.5
where the time goes:
time: 528 us; the launch traced here: 526 us
  waiting for transfers between devices  261 us (49%)
  blocking collectives  127 us (24%)
  local copies, waits for them, and re-layouts  45.7 us (9%)
  matrix products  35.5 us (7%)
  other arithmetic  20.6 us (4%)
  between operations  20.6 us (4%)
  starting transfers between devices  15.4 us (3%)
    psum x1, waiting for transfers between devices, per_device(): head_total = lax.psum(contract_rows(features, logit_grad), ('dp', 'expert'))  204 us
    psum x1, blocking collectives, per_device(): lax.psum((jnp.sum(returns), jnp.sum(returns * returns)), ('dp', 'expert'))  79 us
    all_to_all x1, blocking collectives, per_device(): lax.all_to_all(outgoing, 'expert', split_axis=0, concat_axis=0, tiled=True)  48.5 us
    all_to_all x1, waiting for transfers between devices, per_device(): lax.all_to_all(outgoing_grad, 'expert', split_axis=0, concat_axis=0, tile...  37.5 us
    reduce_scatter x1, waiting for transfers between devices, per_device(): lax.psum_scatter(contract_rows(in_rows, up_grad).astype(jnp.bfloat16), 'd...  19.8 us
    dot_general x4, matrix products, contract_rows(): lax.dot_general(left, right, (((0,), (0,)), ((), ())), preferred_element_...  16.7 us
    dot_general x4, matrix products, contract_cols(): lax.dot_general(left, right, (((1,), (1,)), ((), ())), preferred_element_...  12 us
  transfers between devices with their start and end apart: 7, of which 3 were waited for; matrix products, arithmetic and copies ran while one was open for 9% of the time, Pallas kernels for 0%

commit v1 on v0

v1 whole, which is shorter than its diff:
```python
import math

import jax
import jax.numpy as jnp
from jax import lax
from jax.experimental import pallas as pl
from jax.experimental.pallas import tpu as pltpu
from jax.sharding import Mesh, PartitionSpec as P

support_edge = 4.0
smoothing = 0.75
ALL = ("y", "x", "core", "expert")
BF16 = jnp.bfloat16
F32 = jnp.float32
STAT_ROWS = 16
MIB = 1024 * 1024
VMEM_BYTES = 56 * MIB


def dot(left, right, left_dim=1, right_dim=0):
    return lax.dot_general(
        left, right, (((left_dim,), (right_dim,)), ((), ())), preferred_element_type=F32
    )


def params():
    return pltpu.CompilerParams(vmem_limit_bytes=VMEM_BYTES)


def cost(flops, bytes_accessed):
    return pl.CostEstimate(flops=flops, bytes_accessed=bytes_accessed, transcendentals=0)


def whole(shape):
    return pl.BlockSpec(shape, lambda *_: (0,) * len(shape))


def pick(array, index, axis):
    return lax.dynamic_index_in_dim(array, index, axis, keepdims=False)


def swap_cores(array):
    return lax.ppermute(array, "core", [(0, 1), (1, 0)])


def send(arrays, axis_name):
    size = lax.axis_size(axis_name)
    came = {
        shift: lax.ppermute(
            arrays[shift], axis_name, [(k, (k + shift) % size) for k in range(size)]
        )
        for shift in sorted(range(1, size), key=lambda shift: -min(shift, size - shift))
    }
    return [came[shift] for shift in range(1, size)]


def summed(refs):
    total = refs[0][...]
    for ref in refs[1:]:
        total = total + ref[...].astype(F32)
    return total


def slots_kernel(groups, cap, ids_ref, hidden_ref, out_ref, slot_ref, any_ref):
    routes, tok_rows = ids_ref.shape
    ids = ids_ref[...]
    expert = lax.broadcasted_iota(jnp.int32, (8 * pl.cdiv(groups, 8), tok_rows), 0)
    named = [ids[k : k + 1, :] == expert for k in range(routes)]
    counts = sum(jnp.where(n, 1.0, 0.0) for n in named).astype(BF16)
    row = lax.broadcasted_iota(jnp.int32, (tok_rows, tok_rows), 0)
    col = lax.broadcasted_iota(jnp.int32, (tok_rows, tok_rows), 1)
    before = dot(counts, jnp.where(row < col, 1.0, 0.0).astype(BF16))
    slot_ids = lax.broadcasted_iota(jnp.int32, (groups * cap, tok_rows), 0)
    placed = jnp.zeros((groups * cap, tok_rows), F32)
    for k in range(routes):
        position = jnp.sum(jnp.where(named[k], before, 0.0), axis=0, keepdims=True)
        slot = ids[k : k + 1, :] * cap + position.astype(jnp.int32)
        placed = placed + jnp.where(slot_ids == slot, 1.0, 0.0)
        slot_ref[k : k + 1, :] = slot
    placed = placed.astype(BF16)
    any_ref[...] = placed
    width = hidden_ref.shape[1]
    step = min(512, width)
    for at in range(0, width, step):
        out_ref[:, at : at + step] = dot(placed, hidden_ref[:, at : at + step]).astype(BF16)


def front_kernel(
    cap, x_ref, gate_ref, up_ref, mix_ref, stat_ref, *refs
):
    act_ref, one_ref, two_ref, z_ref, acc = refs[-5:]
    step = pl.program_id(0)
    x = x_ref[...]
    gate = dot(x, gate_ref[...])
    up = dot(x, up_ref[...])
    sig = jax.nn.sigmoid(gate)
    act = (gate * sig * up).astype(BF16)
    act_ref[...] = act
    one_ref[...] = up * sig * (1.0 + gate * (1.0 - sig))
    two_ref[...] = gate * sig
    part = dot(act, mix_ref[...])

    @pl.when(step == 0)
    def _():
        acc[...] = part

    @pl.when(step > 0)
    def _():
        acc[...] += part

    @pl.when(step == pl.num_programs(0) - 1)
    def _():
        total = acc[...].astype(BF16)
        shape = (STAT_ROWS, z_ref.shape[2])
        lane = lax.broadcasted_iota(jnp.int32, shape, 1)
        stat = jnp.where(lane < shape[1] // 2, stat_ref[0], stat_ref[1])
        high = stat.astype(BF16).astype(F32)
        middle = (stat - high).astype(BF16).astype(F32)
        low = stat - high - middle
        row = lax.broadcasted_iota(jnp.int32, stat.shape, 0)
        rows = jnp.where(
            row == 0, high, jnp.where(row == 1, middle, jnp.where(row == 2, low, 0.0))
        ).astype(BF16)
        for group in range(z_ref.shape[0]):
            z_ref[group, :cap, :] = total[group * cap : (group + 1) * cap]
            z_ref[group, cap:, :] = rows


def head_kernel(
    cap, token_count, moments_ref, back_ref, slot_ref, weight_ref, resid_ref, returns_ref, *refs
):
    out_ref, grad_ref, route_ref = refs[-3:]
    groups, _, bins = back_ref.shape
    routes, tok_rows = slot_ref.shape
    stat = jnp.sum(jnp.sum(back_ref[:, cap:, :].astype(F32), axis=0), axis=0, keepdims=True)
    half = bins // 2
    batch_mean = stat[:, 0:1] / token_count
    batch_var = stat[:, half : half + 1] / token_count - batch_mean * batch_mean
    run_mean, run_var = moments_ref[0], moments_ref[1]
    mean_value = 0.5 * (run_mean + batch_mean)
    var_value = 0.5 * (run_var + batch_var) + 0.25 * (batch_mean - run_mean) ** 2
    scaled = jnp.clip(
        (returns_ref[...] - mean_value) / jnp.sqrt(var_value + 1e-06), -support_edge, support_edge
    )
    width = 2.0 * support_edge / bins
    scale = math.sqrt(2.0) * smoothing * width
    edge = lax.broadcasted_iota(jnp.int32, (tok_rows, bins), 1).astype(F32) * width - support_edge
    lower = lax.erf((edge - scaled) / scale)
    upper = lax.erf((edge + width - scaled) / scale)
    targets = (upper - lower) / (upper[:, bins - 1 :] - lower[:, :1])

    back = jnp.concatenate([back_ref[group, :cap, :] for group in range(groups)], axis=0)
    slot_ids = lax.broadcasted_iota(jnp.int32, (groups * cap, tok_rows), 0)
    placed, token_logits = [], []
    logits = resid_ref[...]
    for k in range(routes):
        placed.append(jnp.where(slot_ids == slot_ref[k : k + 1, :], 1.0, 0.0).astype(BF16))
        token_logits.append(dot(placed[k], back, 0, 0))
        logits = logits + weight_ref[:, k : k + 1] * token_logits[k]
    power = jnp.exp(logits - jnp.max(logits, axis=1, keepdims=True))
    probs = power / jnp.sum(power, axis=1, keepdims=True)
    grad = (probs - targets).astype(BF16)
    grad_ref[...] = grad
    grad_f = grad.astype(F32)
    total = jnp.zeros((groups * cap, bins), F32)
    which = lax.broadcasted_iota(jnp.int32, (tok_rows, routes), 1)
    route = jnp.zeros((tok_rows, routes), F32)
    for k in range(routes):
        weighted = (weight_ref[:, k : k + 1] * grad_f).astype(BF16)
        total = total + dot(placed[k], weighted)
        sums = jnp.sum(token_logits[k] * grad_f, axis=1, keepdims=True)
        route = jnp.where(which == k, sums, route)
    out_ref[...] = total.astype(BF16)
    route_ref[...] = route


def back_kernel(grad_ref, mix_ref, act_ref, one_ref, two_ref, gate_ref, up_ref, *refs):
    input_ref, pair_ref, inner_ref = refs[-3:]
    ff = one_ref.shape[1]

    @pl.when(pl.program_id(0) == 0)
    def _():
        grad = grad_ref[...]
        act_grad = dot(grad, mix_ref[...], 1, 1)
        pair_ref[:, :ff] = (act_grad * one_ref[...]).astype(BF16)
        pair_ref[:, ff:] = (act_grad * two_ref[...]).astype(BF16)
        inner_ref[...] = dot(act_ref[...], grad, 0, 0).astype(BF16)

    input_ref[...] = (
        dot(pair_ref[:, :ff], gate_ref[...], 1, 1) + dot(pair_ref[:, ff:], up_ref[...], 1, 1)
    ).astype(BF16)


def parts_kernel(
    shifts, coord_ref, rows_x, rows_x2, rows_y, rows_y2, value_x, value_y, resid_x, resid_x2,
    down_x, pair_ref, pair2_ref, inner_ref, inner2_ref, grad_ref, grad2_ref, *refs,
):
    del coord_ref
    outs, inner = refs[:-1], refs[-1]
    step = pl.program_id(0)
    each = len(outs) // (2 * len(shifts))
    ff, bins = inner.shape
    cut = ff - 2 * bins

    @pl.when(step == 0)
    def _():
        inner[...] = (inner_ref[...].astype(F32) + inner2_ref[...].astype(F32)).astype(BF16)

    def flat(ref):
        return ref[...].reshape(ref.shape[0] * ref.shape[1] * ref.shape[2], ref.shape[3])

    def write(place, at, value):
        half = len(outs) // 2
        for number in range(len(shifts)):

            def put():
                targets = outs[place * half + number * each : place * half + (number + 1) * each]
                begin = 0
                for out in targets:
                    low, high = max(at, begin), min(at + value.shape[1], begin + out.shape[2])
                    if low < high:
                        part = value[:, low - at : high - at]
                        out[:, :, low - begin : high - begin] = part.reshape(
                            out.shape[:2] + (high - low,)
                        ).astype(out.dtype)
                    begin += out.shape[2]

            if len(shifts) == 1:
                put()
            else:
                pl.when(step == number)(put)

    write(0, 0, dot(flat(rows_x), pair_ref[:, :ff]) + dot(flat(rows_x2), pair2_ref[:, :ff]))
    write(0, ff, dot(flat(value_x), inner[:cut, :], 1, 1))
    write(
        0,
        ff + cut,
        dot(flat(resid_x), grad_ref[...])
        + dot(flat(resid_x2), grad2_ref[...])
        + dot(flat(down_x), inner[...]),
    )
    write(1, 0, dot(flat(rows_y), pair_ref[:, ff:]) + dot(flat(rows_y2), pair2_ref[:, ff:]))
    write(1, ff, dot(flat(value_y), inner[cut:, :], 1, 1))


def fold_kernel(*refs):
    half = len(refs) // 3
    for number in range(half):
        block, came, out = refs[number], refs[half + number], refs[2 * half + number]
        columns = came.shape[2]
        at = 0 if number % 2 == 0 else columns
        out[:, :, columns - at : 2 * columns - at] = block[:, :, columns - at : 2 * columns - at]
        out[:, :, at : at + columns] = (
            block[:, :, at : at + columns].astype(F32) + came[...].astype(F32)
        ).astype(BF16)


def middle_kernel(side_x, side_y, coord_ref, placed_ref, rows_ref, *refs):
    refs = list(refs)
    firsts = [refs.pop(0) for _ in range(3)]
    seconds = [refs.pop(0) for _ in range(3)]
    hidden_ref, head_ref = refs.pop(0), refs.pop(0)
    first_outs = [refs.pop(0) for _ in range(side_y)]
    second_outs = [refs.pop(0) for _ in range(side_x)]
    first_full, second_full = refs
    columns = first_outs[0].shape[1]
    first_full[...] = summed(firsts)
    second_full[...] = summed(seconds)
    for shift, out in enumerate(first_outs):
        out[...] = first_full[lax.rem(coord_ref[1] + shift, side_y), :, :columns].astype(out.dtype)
    for shift, out in enumerate(second_outs):
        out[...] = second_full[lax.rem(coord_ref[0] + shift, side_x)].astype(out.dtype)
    head_ref[...] = first_full[:, :, columns:]
    hidden_ref[...] = dot(placed_ref[...], rows_ref[...], 0, 0).astype(BF16)


def last_kernel(side_x, side_y, head_ref, *refs):
    firsts, seconds = refs[:side_y], refs[side_y : side_y + side_x]
    gate_ref, up_ref, down_ref, value_ref = refs[side_y + side_x :]
    ff = gate_ref.shape[1]
    first, second = summed(firsts), summed(seconds)
    gate_ref[...] = first[:, :ff]
    up_ref[...] = second[:, :ff]
    cut = first.shape[1] - ff
    down_ref[:, :cut] = first[:, ff:]
    down_ref[:, cut:] = second[:, ff:]
    value_ref[...] = jnp.sum(head_ref[...], axis=0)


def per_shift(count, shape):
    return tuple(jax.ShapeDtypeStruct(shape, BF16 if shift else F32) for shift in range(count))


def per_device(
    hidden_in,
    resid_in,
    route_ids,
    route_weight,
    returns,
    run_moments,
    gate_w,
    up_w,
    down_w,
    value_w,
):
    groups = lax.axis_size("expert")
    side_y, side_x = lax.axis_size("y"), lax.axis_size("x")
    core = lax.axis_index("core")
    tok_rows, width = hidden_in.shape
    routes = route_ids.shape[1]
    cap = 3 * tok_rows * routes // (2 * groups)
    slot_total = groups * cap
    bins = value_w.shape[1]
    gate_w, up_w, down_w = gate_w[0], up_w[0], down_w[0]
    ff = gate_w.shape[1]
    own_rows = width // (side_y * side_x * 2)
    token_count = float(tok_rows * groups * side_y * side_x * 2)
    sds = jax.ShapeDtypeStruct
    anywhere = pl.BlockSpec(memory_space=pl.ANY)
    smem = pl.BlockSpec(memory_space=pltpu.SMEM)
    vmem = pl.BlockSpec(memory_space=pltpu.VMEM)

    def core_half(array):
        blocks = array.reshape(side_y * side_x, 2, own_rows, array.shape[1])
        mine = pick(blocks, core, 1).reshape(width // 2, array.shape[1])
        other = pick(blocks, 1 - core, 1).reshape(width // 2, array.shape[1])
        return mine, other

    def exchange(blocks):
        return lax.all_to_all(blocks, "expert", 0, 0, tiled=True)

    def exchange_rows(rows):
        return exchange(rows.reshape(groups, cap, rows.shape[1])).reshape(rows.shape)

    outgoing, slots, placed_any = pl.pallas_call(
        lambda *refs: slots_kernel(groups, cap, *refs),
        out_shape=(
            sds((slot_total, width), BF16),
            sds((routes, tok_rows), jnp.int32),
            sds((slot_total, tok_rows), BF16),
        ),
        compiler_params=params(),
        cost_estimate=cost(2 * tok_rows * slot_total * width, 2 * width * (slot_total + tok_rows)),
        name="slots",
    )(route_ids.T, hidden_in)
    in_rows = exchange_rows(outgoing)

    with jax.named_scope("moments"):
        sums = jnp.stack([jnp.sum(returns), jnp.sum(returns * returns)])
        for axis_name in ("x", "y", "core"):
            sums = lax.psum(sums, axis_name)

    with jax.named_scope("weights_only"):
        mix = dot(down_w, value_w).astype(BF16)
        resid_logits = dot(resid_in, value_w)
        value_mine, _ = core_half(value_w)
        down_mine, _ = core_half(down_w.T)
        resid_mine, resid_other = core_half(resid_in.T)
        resid_peer = swap_cores(resid_other)

    steps = 3
    part = ff // steps
    act, one, two, route_logits = pl.pallas_call(
        lambda *refs: front_kernel(cap, *refs),
        grid=(steps,),
        in_specs=[
            whole((slot_total, width)),
            pl.BlockSpec((width, part), lambda j: (0, j)),
            pl.BlockSpec((width, part), lambda j: (0, j)),
            pl.BlockSpec((part, bins), lambda j: (j, 0)),
            smem,
        ]
        + [anywhere] * 4,
        out_specs=[
            pl.BlockSpec((slot_total, part), lambda j: (0, j)),
            pl.BlockSpec((slot_total, part), lambda j: (0, j)),
            pl.BlockSpec((slot_total, part), lambda j: (0, j)),
            whole((groups, cap + STAT_ROWS, bins)),
        ],
        out_shape=(
            sds((slot_total, ff), BF16),
            sds((slot_total, ff), F32),
            sds((slot_total, ff), F32),
            sds((groups, cap + STAT_ROWS, bins), BF16),
        ),
        scratch_shapes=[pltpu.VMEM((slot_total, bins), F32)],
        compiler_params=params(),
        cost_estimate=cost(4 * slot_total * width * ff, 4 * width * ff),
        name="front",
    )(in_rows, gate_w, up_w, mix, sums, value_mine, down_mine, resid_mine, resid_peer)
    back_logits = exchange(route_logits)
    with jax.named_scope("turned"):
        rows_mine, rows_other = core_half(in_rows.T)
        rows_peer = swap_cores(rows_other)

    out_grad, logit_grad, grad_route = pl.pallas_call(
        lambda *refs: head_kernel(cap, token_count, *refs),
        in_specs=[smem]
        + [vmem] * 5
        + [anywhere] * 2,
        out_shape=(
            sds((slot_total, bins), BF16),
            sds((tok_rows, bins), BF16),
            sds((tok_rows, routes), F32),
        ),
        compiler_params=params(),
        cost_estimate=cost(8 * tok_rows * slot_total * bins, 4 * slot_total * bins),
        name="head",
    )(
        run_moments, back_logits, slots, route_weight, resid_logits, returns.reshape(tok_rows, 1),
        rows_mine, rows_other,
    )
    row_grad = exchange_rows(out_grad)
    grad_peer = swap_cores(logit_grad)

    strip = min(512, width)
    input_grad, pair, inner = pl.pallas_call(
        back_kernel,
        grid=(width // strip,),
        in_specs=[
            whole((slot_total, bins)),
            whole((ff, bins)),
            whole((slot_total, ff)),
            whole((slot_total, ff)),
            whole((slot_total, ff)),
            pl.BlockSpec((strip, ff), lambda i: (i, 0)),
            pl.BlockSpec((strip, ff), lambda i: (i, 0)),
            anywhere,
            anywhere,
        ],
        out_specs=[
            pl.BlockSpec((slot_total, strip), lambda i: (0, i)),
            whole((slot_total, 2 * ff)),
            whole((ff, bins)),
        ],
        out_shape=(
            sds((slot_total, width), BF16),
            sds((slot_total, 2 * ff), BF16),
            sds((ff, bins), BF16),
        ),
        compiler_params=params(),
        cost_estimate=cost(4 * slot_total * width * ff, 4 * width * ff),
        name="back",
    )(row_grad, mix, act, one, two, gate_w, up_w, rows_peer, grad_peer)
    back_grad = exchange_rows(input_grad)
    inner_peer = swap_cores(inner)
    pair_peer = swap_cores(pair)

    half = width // 2
    coords = jnp.stack([lax.axis_index("x"), lax.axis_index("y")]).astype(jnp.int32)
    def parts(shifts, out_shape):
        pattern = {(2,): lambda step: 2, (1, 3, 0): lambda step: lax.rem(2 * step + 1, 5)}[shifts]

        def tall(depth):
            return pl.BlockSpec(
                (side_y, 1, own_rows, depth),
                lambda step, at: (0, lax.rem(at[0] + pattern(step), side_x), 0, 0),
            )

        def wide(depth):
            return pl.BlockSpec(
                (1, side_x, own_rows, depth),
                lambda step, at: (lax.rem(at[1] + pattern(step), side_y), 0, 0, 0),
            )

        return pl.pallas_call(
            lambda *refs: parts_kernel(shifts, *refs),
            grid_spec=pltpu.PrefetchScalarGridSpec(
                num_scalar_prefetch=1,
                grid=(len(shifts),),
                in_specs=[
                    tall(slot_total),
                    tall(slot_total),
                    wide(slot_total),
                    wide(slot_total),
                    tall(bins),
                    wide(bins),
                    tall(tok_rows),
                    tall(tok_rows),
                    tall(ff),
                    whole((slot_total, 2 * ff)),
                    whole((slot_total, 2 * ff)),
                    whole((ff, bins)),
                    whole((ff, bins)),
                    whole((tok_rows, bins)),
                    whole((tok_rows, bins)),
                ],
                out_specs=[whole(out.shape) for out in out_shape],
                scratch_shapes=[pltpu.VMEM((ff, bins), BF16)],
            ),
            out_shape=out_shape,
            compiler_params=params(),
            cost_estimate=cost(len(shifts) * half * slot_total * 2 * ff, len(shifts) * 4 * MIB),
            name="parts%d" % len(shifts),
        )(
            coords,
            *[
                rows.reshape(side_y, side_x, own_rows, rows.shape[1])
                for rows in (
                    rows_mine, rows_peer, rows_mine, rows_peer, value_mine, value_mine, resid_mine,
                    resid_peer, down_mine,
                )
            ],
            pair,
            pair_peer,
            inner,
            inner_peer,
            logit_grad,
            grad_peer,
        )

    def step_on(array, axis_name, shift):
        size = lax.axis_size(axis_name)
        return lax.ppermute(array, axis_name, [(k, (k + shift) % size) for k in range(size)])

    cut = ff - 2 * bins
    first_columns, second_columns = ff + cut, 2 * ff - cut
    columns = first_columns + bins
    block = (side_y, own_rows, columns)
    far = sds((side_y, own_rows, columns // 2), BF16)
    x_up, x_down, y_up, y_down = parts((2,), (far,) * 4)
    came = (
        step_on(x_up, "x", 1),
        step_on(x_down, "x", -1),
        step_on(y_up, "y", 1),
        step_on(y_down, "y", -1),
    )
    near, own = sds(block, BF16), sds(block, F32)
    x_up, x_down, x_own, y_up, y_down, y_own = parts(
        (1, 3, 0), (near, near, own, near, near, own)
    )
    x_up, x_down, y_up, y_down = pl.pallas_call(
        fold_kernel,
        out_shape=(near,) * 4,
        compiler_params=params(),
        cost_estimate=cost(0, 24 * side_y * own_rows * columns),
        name="fold",
    )(x_up, x_down, y_up, y_down, *came)
    firsts = (x_own, step_on(x_up, "x", 1), step_on(x_down, "x", -1))
    seconds = (y_own, step_on(y_up, "y", 1), step_on(y_down, "y", -1))

    grad_hidden, head, *halves = pl.pallas_call(
        lambda *refs: middle_kernel(side_x, side_y, *refs),
        in_specs=[smem] + [vmem] * 8,
        out_shape=(
            sds((tok_rows, width), BF16),
            sds((side_y, own_rows, bins), F32),
        )
        + per_shift(side_y, (own_rows, first_columns))
        + per_shift(side_x, (own_rows, second_columns)),
        scratch_shapes=[pltpu.VMEM(block, F32), pltpu.VMEM(block, F32)],
        compiler_params=params(),
        cost_estimate=cost(2 * tok_rows * slot_total * width, 2 * width * (slot_total + tok_rows)),
        name="middle",
    )(coords, placed_any, back_grad, *firsts, *seconds)
    firsts, seconds = halves[:side_y], halves[side_y:]
    shares = head.reshape(side_y * groups, own_rows // groups, bins)
    shares = lax.all_to_all(shares, ("y", "expert"), 0, 0, tiled=True)
    first_came, second_came = send(firsts, "y"), send(seconds, "x")
    grad_gate, grad_up, grad_down, grad_value = pl.pallas_call(
        lambda *refs: last_kernel(side_x, side_y, *refs),
        out_shape=(
            sds((own_rows, ff), F32),
            sds((own_rows, ff), F32),
            sds((own_rows, ff), F32),
            sds(shares.shape[1:], F32),
        ),
        compiler_params=params(),
        cost_estimate=cost(0, 24 * own_rows * ff),
        name="last",
    )(shares, firsts[0], *first_came, seconds[0], *second_came)
    return (grad_hidden, grad_route, grad_gate[None], grad_up[None], grad_down.T[None], grad_value)


def solution(mesh):
    pair = 2
    plane = mesh.shape["dp"] // pair
    side = math.isqrt(plane)
    grid = Mesh(mesh.devices.reshape(plane // side, side, pair, mesh.shape["expert"]), ALL)
    rows = P(ALL, None)
    dp = ("y", "x", "core")
    in_specs = (
        rows,
        rows,
        rows,
        rows,
        P(ALL),
        P(),
        P("expert", None, None),
        P("expert", None, None),
        P("expert", None, None),
        P(),
    )
    out_specs = (
        rows,
        rows,
        P("expert", dp, None),
        P("expert", dp, None),
        P("expert", None, dp),
        rows,
    )
    return jax.shard_map(
        per_device, mesh=grid, in_specs=in_specs, out_specs=out_specs, check_vma=False
    )
```

time: 528 us -> 199 us (0.38)
  waiting for transfers between devices: 261 us -> 43.1 us
  blocking collectives: 127 us -> 21 us
  Pallas kernels: 0 us -> 51.8 us
  starting transfers between devices: 15.4 us -> 52.3 us
  matrix products: 35.5 us -> 3.75 us
  local copies, waits for them, and re-layouts: 45.7 us -> 21.1 us
  between operations: 20.6 us -> 0.91 us
  other arithmetic: 20.6 us -> 2.58 us
    psum x1 -> x0, waiting for transfers between devices: 204 us -> none  [per_device(): head_total = lax.psum(contract_rows(features, logit_grad), ('dp', 'expert'))]
    psum x1 -> x3, blocking collectives: 79 us -> 21 us  [per_device(): sums = lax.psum(sums, axis_name)]
    pallas_call x0 -> x9, Pallas kernels: none -> 51.8 us  [the longest x2 19.1 us: parts(): pl.pallas_call(lambda *refs: parts_kernel(shifts, *refs), grid_spec=pltpu...]
    all_to_all x1 -> x0, blocking collectives: 48.5 us -> none  [per_device(): lax.all_to_all(outgoing, 'expert', split_axis=0, concat_axis=0, tiled=True)]
    dot_general x12 -> x2, matrix products: 35.5 us -> 3.75 us  [dot(): lax.dot_general(left, right, (((left_dim,), (right_dim,)), ((), ())), pre...]
    ppermute x0 -> x19, waiting for transfers between devices: none -> 24.1 us  [the longest x8 15.5 us: step_on(): lax.ppermute(array, axis_name, [(k, (k + shift) % size) for k in range(si...]
    ppermute x0 -> x19, starting transfers between devices: none -> 22.8 us  [the longest x8 14.3 us: step_on(): lax.ppermute(array, axis_name, [(k, (k + shift) % size) for k in range(si...]
    gather x4 -> x0, local copies, waits for them, and re-layouts: 22.5 us -> none  [the longest x1 6.43 us: per_device(): route_grad[slot_route]]
  transfers between devices with their start and end apart: 7 -> 24, of which waited for: 3 -> 12; matrix products, arithmetic and copies ran while one was open for 9% -> 11% of each run, Pallas kernels for 0% -> 13%
where the time goes in v1:
time: 199 us; the launch traced here: 197 us
  starting transfers between devices  52.3 us (26%)
  Pallas kernels  51.8 us (26%)
  waiting for transfers between devices  43.1 us (22%)
  local copies, waits for them, and re-layouts  21.1 us (11%)
  blocking collectives  21 us (11%)
  matrix products  3.75 us (2%)
  other arithmetic  2.58 us (1%)
    psum x3, blocking collectives, per_device(): sums = lax.psum(sums, axis_name)  21 us
    all_to_all x4, starting transfers between devices, exchange(): return lax.all_to_all(blocks, 'expert', 0, 0, tiled=True)  19.8 us
    pallas_call x2, Pallas kernels, parts(): pl.pallas_call(lambda *refs: parts_kernel(shifts, *refs), grid_spec=pltpu...  19.1 us
    all_to_all x4, waiting for transfers between devices, exchange(): return lax.all_to_all(blocks, 'expert', 0, 0, tiled=True)  19 us
    ppermute x8, waiting for transfers between devices, step_on(): lax.ppermute(array, axis_name, [(k, (k + shift) % size) for k in range(si...  15.5 us
    ppermute x8, starting transfers between devices, step_on(): lax.ppermute(array, axis_name, [(k, (k + shift) % size) for k in range(si...  14.3 us
    unnamed x62, local copies, waits for them, and re-layouts  13.2 us
    all_to_all x1, starting transfers between devices, per_device(): shares = lax.all_to_all(shares, ('y', 'expert'), 0, 0, tiled=True)  9.78 us
  transfers between devices with their start and end apart: 24, of which 12 were waited for; matrix products, arithmetic and copies ran while one was open for 11% of the time, Pallas kernels for 13%

profile of v1, /device:TPU:24, one launch (start us, length us, event | category | flops | bytes accessed | tf_op | source)
XLA Modules:
  0.0 196.6 jit_solution(17766844060788553613)
XLA Ops:
  0.6 3.0 %slots.1 = (bf16[384,2048]{1,0:T(8,128)(2,1)}, s32[2,128]{1,0:T(2,128)}, bf16[384,128]{1,0:T(8,128)(2,1)}) custom-call(s32[2,128]{1,0:T(2,128)} %bitcast.100, bf16[128,2048]{1,0:T(8,128)(2,1)} %refs_1_.1), custom_call_target="tpu_custom_call" | custom-call | flops 201326592 | bytes 2097152 | tf_op jit(solution)/shard_map/slots/pallas_call | solution.py:335
  3.7 8.6 %all-to-all-start = ((bf16[8,48,2048]{2,1,0:T(8,128)(2,1)}), bf16[8,48,2048]{2,1,0:T(8,128)(2,1)S(1)}, u32[]{:S(2)}, u32[]{:S(2)}) async-start(bf16[8,48,2048]{2,1,0:T(8,128)(2,1)} %bitcast.91), calls=%async_computation | async-start | bytes 3145728 | tf_op jit(solution)/shard_map/all_to_all | solution.py:330
  14.3 10.5 %psum.21 = f32[2]{0:T(128)S(1)} all-reduce(f32[2]{0:T(128)S(1)} %pad_maximum_fusion), channel_id=1, replica_groups=mesh['y'=4,'x'=4,'core'=2,'expert'=8] {'x'}, use_global_device_ids=true, to_apply=%region_2.0 | all-reduce | flops 2 | bytes 16 | tf_op jit(solution)/shard_map/moments/psum | solution.py:351
  24.7 7.5 %psum.22 = f32[2]{0:T(128)S(1)} all-reduce(f32[2]{0:T(128)S(1)} %psum.21), channel_id=1, replica_groups=mesh['y'=4,'x'=4,'core'=2,'expert'=8] {'y'}, use_global_device_ids=true, to_apply=%region_3.0 | all-reduce | flops 2 | bytes 16 | tf_op jit(solution)/shard_map/moments/psum | solution.py:351
  34.3 3.1 %psum.23.refs_4_ = f32[2]{0:T(128)} all-reduce(f32[2]{0:T(128)S(1)} %psum.22), channel_id=1, replica_groups=mesh['y'=4,'x'=4,'core'=2,'expert'=8] {'core'}, use_global_device_ids=true, to_apply=%region_4.0 | all-reduce | flops 2 | bytes 16 | tf_op jit(solution)/shard_map/moments/psum | solution.py:351
  37.4 4.6 %copy.25 = bf16[1,768,2048]{1,2,0:T(8,128)(2,1)} copy(bf16[1,768,2048]{2,1,0:T(8,128)(2,1)} %param.18) | data formatting | bytes 6291456 | tf_op args[8]
  42.9 2.9 %constant_dynamic-slice_fusion.4 = bf16[16,1,64,768]{3,2,1,0:T(8,128)(2,1)} fusion(bf16[16,2,64,768]{3,2,1,0:T(8,128)(2,1)} %bitcast.79, s32[]{:T(128)S(6)} %select_n.14), kind=kLoop, calls=%fused_computation.7 | loop fusion | bytes 3145732 | tf_op jit(solution)/shard_map/weights_only/jit(dynamic_index_in_dim)/dynamic_slice | solution.py:39
  47.5 4.8 %all-to-all-done = bf16[8,48,2048]{2,1,0:T(8,128)(2,1)S(1)} async-done(((bf16[8,48,2048]{2,1,0:T(8,128)(2,1)}), bf16[8,48,2048]{2,1,0:T(8,128)(2,1)S(1)}, u32[]{:S(2)}, u32[]{:S(2)}) %all-to-all-start) | async-done | bytes 1572896 | tf_op jit(solution)/shard_map/all_to_all | solution.py:330
  54.6 8.2 %front.1 = (bf16[384,768]{1,0:T(8,128)(2,1)}, f32[384,768]{1,0:T(8,128)}, f32[384,768]{1,0:T(8,128)}, bf16[8,64,256]{2,1,0:T(8,128)(2,1)}) custom-call(bf16[384,2048]{1,0:T(8,128)(2,1)} %bitcast.74, bf16[2048,768]{1,0:T(8,128)(2,1)} %bitcast.75, bf16[2048,768]{1,0:T(8,128)(2,1)} %bitcast.77, bf16[768,256]{1,0:T(8,128)(2,1)} %fusion.2.refs_3_.mix_ref, ...), custom_call_target="tpu_custom_call" | custom-call | flops 2415919104 | bytes 6291456 | tf_op jit(solution)/shard_map/front/pallas_call | solution.py:363
  62.8 4.1 %all-to-all-start.1 = ((bf16[8,64,256]{2,1,0:T(8,128)(2,1)}), bf16[8,64,256]{2,1,0:T(8,128)(2,1)}, u32[]{:S(2)}, u32[]{:S(2)}) async-start(bf16[8,64,256]{2,1,0:T(8,128)(2,1)} %get-tuple-element.49), calls=%async_computation.1 | async-start | bytes 524288 | tf_op jit(solution)/shard_map/all_to_all | solution.py:330
  71.6 6.1 %all-to-all-done.1.refs_1_ = bf16[8,64,256]{2,1,0:T(8,128)(2,1)} async-done(((bf16[8,64,256]{2,1,0:T(8,128)(2,1)}), bf16[8,64,256]{2,1,0:T(8,128)(2,1)}, u32[]{:S(2)}, u32[]{:S(2)}) %all-to-all-start.1) | async-done | bytes 262176 | tf_op jit(solution)/shard_map/all_to_all | solution.py:330
  80.2 3.4 %all-to-all-start.2 = ((bf16[8,48,256]{2,1,0:T(8,128)(2,1)}), bf16[8,48,256]{2,1,0:T(8,128)(2,1)S(1)}, u32[]{:S(2)}, u32[]{:S(2)}) async-start(bf16[8,48,256]{2,1,0:T(8,128)(2,1)} %bitcast.95), calls=%async_computation.2 | async-start | bytes 393216 | tf_op jit(solution)/shard_map/all_to_all | solution.py:330
  85.2 8.1 %all-to-all-done.2 = bf16[8,48,256]{2,1,0:T(8,128)(2,1)S(1)} async-done(((bf16[8,48,256]{2,1,0:T(8,128)(2,1)}), bf16[8,48,256]{2,1,0:T(8,128)(2,1)S(1)}, u32[]{:S(2)}, u32[]{:S(2)}) %all-to-all-start.2) | async-done | bytes 196640 | tf_op jit(solution)/shard_map/all_to_all | solution.py:330
  94.0 8.0 %back.1 = (bf16[384,2048]{1,0:T(8,128)(2,1)}, bf16[384,1536]{1,0:T(8,128)(2,1)}, bf16[768,256]{1,0:T(8,128)(2,1)}) custom-call(bf16[384,256]{1,0:T(8,128)(2,1)} %bitcast.92, bf16[768,256]{1,0:T(8,128)(2,1)} %fusion.2.refs_3_.mix_ref, bf16[384,768]{1,0:T(8,128)(2,1)} %get-tuple-element.52.act_ref, f32[384,768]{1,0:T(8,128)} %get-tuple-element.53.one_ref, ...), custom_call_target="tpu_custom_call" | custom-call | flops 2415919104 | bytes 6291456 | tf_op jit(solution)/shard_map/back/pallas_call | solution.py:417
  102.0 3.7 %all-to-all-start.3 = ((bf16[8,48,2048]{2,1,0:T(8,128)(2,1)}), bf16[8,48,2048]{2,1,0:T(8,128)(2,1)S(1)}, u32[]{:S(2)}, u32[]{:S(2)}) async-start(bf16[8,48,2048]{2,1,0:T(8,128)(2,1)} %bitcast.90), calls=%async_computation.3 | async-start | bytes 3145728 | tf_op jit(solution)/shard_map/all_to_all | solution.py:330
  109.9 5.3 %parts1.1 = (bf16[4,64,640]{2,1,0:T(8,128)(2,1)}, bf16[4,64,640]{2,1,0:T(8,128)(2,1)}, bf16[4,64,640]{2,1,0:T(8,128)(2,1)}, bf16[4,64,640]{2,1,0:T(8,128)(2,1)}) custom-call(s32[2]{0:T(128)} %pad_add_fusion.refs_0_, bf16[4,4,64,384]{3,2,1,0:T(8,128)(2,1)} %bitcast.57, bf16[4,4,64,384]{3,2,1,0:T(8,128)(2,1)} %bitcast.64, bf16[4,4,64,384]{3,2,1,0:T(8,128)(2,1)} %bitcast.58, ...), custom_call_target="tpu_custom_call" | custom-call | flops 603979776 | bytes 4194304 | tf_op jit(solution)/shard_map/parts1/pallas_call | solution.py:466
  118.4 4.5 %collective-permute-start.7 = (bf16[4,64,640]{2,1,0:T(8,128)(2,1)}, bf16[4,64,640]{2,1,0:T(8,128)(2,1)S(1)}, u32[]{:S(2)}, u32[]{:S(2)}) collective-permute-start(bf16[4,64,640]{2,1,0:T(8,128)(2,1)} %get-tuple-element.66), channel_id=1, source_target_pairs={{0,64},{64,128},{128,192},{192,0},{1,65},{65,129},{129,193},{193,1... | collective-permute-start | bytes 983048 | tf_op jit(solution)/shard_map/ppermute | solution.py:514
  123.0 13.9 %parts3.1 = (bf16[4,64,1280]{2,1,0:T(8,128)(2,1)}, bf16[4,64,1280]{2,1,0:T(8,128)(2,1)}, f32[4,64,1280]{2,1,0:T(8,128)}, bf16[4,64,1280]{2,1,0:T(8,128)(2,1)}, b...) custom-call(s32[2]{0:T(128)} %pad_add_fusion.refs_0_, bf16[4,4,64,384]{3,2,1,0:T(8,128)(2,1)} %bitcast.59, ...), custom_call_target="tpu_custom_call" | custom-call | flops 1811939328 | bytes 12582912 | tf_op jit(solution)/shard_map/parts3/pallas_call | solution.py:466
  137.9 3.7 %fold.1 = (bf16[4,64,1280]{2,1,0:T(8,128)(2,1)}, bf16[4,64,1280]{2,1,0:T(8,128)(2,1)}, bf16[4,64,1280]{2,1,0:T(8,128)(2,1)}, bf16[4,64,1280]{2,1,0:T(8,128)(2,1)}) custom-call(bf16[4,64,1280]{2,1,0:T(8,128)(2,1)} %get-tuple-element.60.refs_0_, bf16[4,64,1280]{2,1,0:T(8,128)(2,1)} %get-tuple-element.61.refs_1_, ...), custom_call_target="tpu_custom_call" | custom-call | bytes 7864320 | tf_op jit(solution)/shard_map/fold/pallas_call | solution.py:532
  141.6 3.2 %collective-permute-start.10 = (bf16[4,64,1280]{2,1,0:T(8,128)(2,1)}, bf16[4,64,1280]{2,1,0:T(8,128)(2,1)S(1)}, u32[]{:S(2)}, u32[]{:S(2)}) collective-permute-start(bf16[4,64,1280]{2,1,0:T(8,128)(2,1)} %get-tuple-element.69), channel_id=1, source_target_pairs={{0,48},{16,0},{32,16},{48,32},{1,49},{17,1},{33,17},{49,33},{2,50}... | collective-permute-start | bytes 1966088 | tf_op jit(solution)/shard_map/ppermute | solution.py:514
  144.9 3.2 %collective-permute-start.11 = (bf16[4,64,1280]{2,1,0:T(8,128)(2,1)}, bf16[4,64,1280]{2,1,0:T(8,128)(2,1)S(1)}, u32[]{:S(2)}, u32[]{:S(2)}) collective-permute-start(bf16[4,64,1280]{2,1,0:T(8,128)(2,1)} %get-tuple-element.71), channel_id=1, source_target_pairs={{0,64},{64,128},{128,192},{192,0},{1,65},{65,129},{129,193},{193,1... | collective-permute-start | bytes 1966088 | tf_op jit(solution)/shard_map/ppermute | solution.py:514
  148.1 10.9 %collective-permute-done.9.refs_4_ = bf16[4,64,1280]{2,1,0:T(8,128)(2,1)S(1)} collective-permute-done((bf16[4,64,1280]{2,1,0:T(8,128)(2,1)}, bf16[4,64,1280]{2,1,0:T(8,128)(2,1)S(1)}, u32[]{:S(2)}, u32[]{:S(2)}) %collective-permute-start.9) | collective-permute-done | bytes 655392 | tf_op jit(solution)/shard_map/ppermute | solution.py:514
  165.7 5.0 %middle.1 = (bf16[128,2048]{1,0:T(8,128)(2,1)}, f32[4,64,256]{2,1,0:T(8,128)}, f32[64,1024]{1,0:T(8,128)}, bf16[64,1024]{1,0:T(8,128)(2,1)}, bf16[64,1024]{1,0:T...) custom-call(s32[2]{0:T(128)} %pad_add_fusion.refs_0_, ...), custom_call_target="tpu_custom_call" | custom-call | flops 201326592 | bytes 2097152 | tf_op jit(solution)/shard_map/middle/pallas_call | solution.py:542
  170.7 9.8 %all-to-all-start.4 = ((f32[32,8,256]{2,1,0:T(8,128)}), f32[32,8,256]{2,1,0:T(8,128)S(1)}, u32[]{:S(2)}, u32[]{:S(2)}) async-start(f32[32,8,256]{2,1,0:T(8,128)} %bitcast.94), calls=%async_computation.4 | async-start | bytes 524288 | tf_op jit(solution)/shard_map/all_to_all | solution.py:558
  (109 shorter events, 49.7 us)
Async XLA Ops:
  3.7 48.6 %all-to-all-start = ((bf16[8,48,2048]{2,1,0:T(8,128)(2,1)}), bf16[8,48,2048]{2,1,0:T(8,128)(2,1)S(1)}, u32[]{:S(2)}, u32[]{:S(2)}) async-start(bf16[8,48,2048]{2,1,0:T(8,128)(2,1)} %bitcast.91), calls=%async_computation | async-start | bytes 3145728 | tf_op jit(solution)/shard_map/all_to_all | solution.py:330
  34.3 19.7 %collective-permute-start = (bf16[1024,128]{1,0:T(8,128)(2,1)S(1)}, bf16[1024,128]{1,0:T(8,128)(2,1)S(1)}, u32[]{:S(2)}, u32[]{:S(2)}) collective-permute-start(bf16[1024,128]{1,0:T(8,128)(2,1)S(1)} %bitcast.93), channel_id=1, source_target_pairs={{0,8},{8,0},{1,9},{9,1},{2,10},{10,2},{3,11},{11,3},{4,12},{12,4},... | collective-permute-start | bytes 786440 | tf_op jit(solution)/shard_map/weights_only/ppermute | solution.py:43
  62.8 14.9 %all-to-all-start.1 = ((bf16[8,64,256]{2,1,0:T(8,128)(2,1)}), bf16[8,64,256]{2,1,0:T(8,128)(2,1)}, u32[]{:S(2)}, u32[]{:S(2)}) async-start(bf16[8,64,256]{2,1,0:T(8,128)(2,1)} %get-tuple-element.49), calls=%async_computation.1 | async-start | bytes 524288 | tf_op jit(solution)/shard_map/all_to_all | solution.py:330
  68.0 17.2 %collective-permute-start.1 = (bf16[1024,384]{1,0:T(8,128)(2,1)S(1)}, bf16[1024,384]{1,0:T(8,128)(2,1)S(1)}, u32[]{:S(2)}, u32[]{:S(2)}) collective-permute-start(bf16[1024,384]{1,0:T(8,128)(2,1)S(1)} %bitcast.85), channel_id=1, source_target_pairs={{0,8},{8,0},{1,9},{9,1},{2,10},{10,2},{3,11},{11,3},{4,12},{12,4},... | collective-permute-start | bytes 2359304 | tf_op jit(solution)/shard_map/turned/ppermute | solution.py:43
  80.2 13.1 %all-to-all-start.2 = ((bf16[8,48,256]{2,1,0:T(8,128)(2,1)}), bf16[8,48,256]{2,1,0:T(8,128)(2,1)S(1)}, u32[]{:S(2)}, u32[]{:S(2)}) async-start(bf16[8,48,256]{2,1,0:T(8,128)(2,1)} %bitcast.95), calls=%async_computation.2 | async-start | bytes 393216 | tf_op jit(solution)/shard_map/all_to_all | solution.py:330
  83.6 1.6 collective-permute-start.2
  102.0 62.5 %all-to-all-start.3 = ((bf16[8,48,2048]{2,1,0:T(8,128)(2,1)}), bf16[8,48,2048]{2,1,0:T(8,128)(2,1)S(1)}, u32[]{:S(2)}, u32[]{:S(2)}) async-start(bf16[8,48,2048]{2,1,0:T(8,128)(2,1)} %bitcast.90), calls=%async_computation.3 | async-start | bytes 3145728 | tf_op jit(solution)/shard_map/all_to_all | solution.py:330
  105.7 3.8 %collective-permute-start.3 = (bf16[384,1536]{1,0:T(8,128)(2,1)}, bf16[384,1536]{1,0:T(8,128)(2,1)}, u32[]{:S(2)}, u32[]{:S(2)}) collective-permute-start(bf16[384,1536]{1,0:T(8,128)(2,1)} %get-tuple-element.57.refs_10_), channel_id=1, source_target_pairs={{0,8},{8,0},{1,9},{9,1},{2,10},{10,2},{3,11},{11,3},{4,12},{12,4},... | collective-permute-start | bytes 3538952 | tf_op jit(solution)/shard_map/ppermute | solution.py:43
  105.8 3.4 %collective-permute-start.4 = (bf16[768,256]{1,0:T(8,128)(2,1)S(1)}, bf16[768,256]{1,0:T(8,128)(2,1)S(1)}, u32[]{:S(2)}, u32[]{:S(2)}) collective-permute-start(bf16[768,256]{1,0:T(8,128)(2,1)S(1)} %copy-done.8), channel_id=1, source_target_pairs={{0,8},{8,0},{1,9},{9,1},{2,10},{10,2},{3,11},{11,3},{4,12},{12,4},... | collective-permute-start | bytes 1179656 | tf_op jit(solution)/shard_map/ppermute | solution.py:43
  115.2 21.7 %collective-permute-start.5 = (bf16[4,64,640]{2,1,0:T(8,128)(2,1)}, bf16[4,64,640]{2,1,0:T(8,128)(2,1)S(1)}, u32[]{:S(2)}, u32[]{:S(2)}) collective-permute-start(bf16[4,64,640]{2,1,0:T(8,128)(2,1)} %get-tuple-element.64), channel_id=1, source_target_pairs={{0,16},{16,32},{32,48},{48,0},{1,17},{17,33},{33,49},{49,1},{2,18}... | collective-permute-start | bytes 983048 | tf_op jit(solution)/shard_map/ppermute | solution.py:514
  116.3 20.6 %collective-permute-start.6 = (bf16[4,64,640]{2,1,0:T(8,128)(2,1)}, bf16[4,64,640]{2,1,0:T(8,128)(2,1)S(1)}, u32[]{:S(2)}, u32[]{:S(2)}) collective-permute-start(bf16[4,64,640]{2,1,0:T(8,128)(2,1)} %get-tuple-element.65), channel_id=1, source_target_pairs={{0,48},{16,0},{32,16},{48,32},{1,49},{17,1},{33,17},{49,33},{2,50}... | collective-permute-start | bytes 983048 | tf_op jit(solution)/shard_map/ppermute | solution.py:514
  118.4 18.5 %collective-permute-start.7 = (bf16[4,64,640]{2,1,0:T(8,128)(2,1)}, bf16[4,64,640]{2,1,0:T(8,128)(2,1)S(1)}, u32[]{:S(2)}, u32[]{:S(2)}) collective-permute-start(bf16[4,64,640]{2,1,0:T(8,128)(2,1)} %get-tuple-element.66), channel_id=1, source_target_pairs={{0,64},{64,128},{128,192},{192,0},{1,65},{65,129},{129,193},{193,1... | collective-permute-start | bytes 983048 | tf_op jit(solution)/shard_map/ppermute | solution.py:514
  123.0 13.9 %collective-permute-start.8 = (bf16[4,64,640]{2,1,0:T(8,128)(2,1)}, bf16[4,64,640]{2,1,0:T(8,128)(2,1)S(1)}, u32[]{:S(2)}, u32[]{:S(2)}) collective-permute-start(bf16[4,64,640]{2,1,0:T(8,128)(2,1)} %get-tuple-element.67), channel_id=1, source_target_pairs={{0,192},{64,0},{128,64},{192,128},{1,193},{65,1},{129,65},{193,129... | collective-permute-start | bytes 983048 | tf_op jit(solution)/shard_map/ppermute | solution.py:514
  141.6 17.3 %collective-permute-start.9 = (bf16[4,64,1280]{2,1,0:T(8,128)(2,1)}, bf16[4,64,1280]{2,1,0:T(8,128)(2,1)S(1)}, u32[]{:S(2)}, u32[]{:S(2)}) collective-permute-start(bf16[4,64,1280]{2,1,0:T(8,128)(2,1)} %get-tuple-element.68), channel_id=1, source_target_pairs={{0,16},{16,32},{32,48},{48,0},{1,17},{17,33},{33,49},{49,1},{2,18}... | collective-permute-start | bytes 1966088 | tf_op jit(solution)/shard_map/ppermute | solution.py:514
  141.6 17.4 %collective-permute-start.10 = (bf16[4,64,1280]{2,1,0:T(8,128)(2,1)}, bf16[4,64,1280]{2,1,0:T(8,128)(2,1)S(1)}, u32[]{:S(2)}, u32[]{:S(2)}) collective-permute-start(bf16[4,64,1280]{2,1,0:T(8,128)(2,1)} %get-tuple-element.69), channel_id=1, source_target_pairs={{0,48},{16,0},{32,16},{48,32},{1,49},{17,1},{33,17},{49,33},{2,50}... | collective-permute-start | bytes 1966088 | tf_op jit(solution)/shard_map/ppermute | solution.py:514
  144.9 16.2 %collective-permute-start.11 = (bf16[4,64,1280]{2,1,0:T(8,128)(2,1)}, bf16[4,64,1280]{2,1,0:T(8,128)(2,1)S(1)}, u32[]{:S(2)}, u32[]{:S(2)}) collective-permute-start(bf16[4,64,1280]{2,1,0:T(8,128)(2,1)} %get-tuple-element.71), channel_id=1, source_target_pairs={{0,64},{64,128},{128,192},{192,0},{1,65},{65,129},{129,193},{193,1... | collective-permute-start | bytes 1966088 | tf_op jit(solution)/shard_map/ppermute | solution.py:514
  148.1 16.3 %collective-permute-start.12 = (bf16[4,64,1280]{2,1,0:T(8,128)(2,1)}, bf16[4,64,1280]{2,1,0:T(8,128)(2,1)}, u32[]{:S(2)}, u32[]{:S(2)}) collective-permute-start(bf16[4,64,1280]{2,1,0:T(8,128)(2,1)} %get-tuple-element.72), channel_id=1, source_target_pairs={{0,192},{64,0},{128,64},{192,128},{1,193},{65,1},{129,65},{193,129... | collective-permute-start | bytes 1966088 | tf_op jit(solution)/shard_map/ppermute | solution.py:514
  170.7 22.8 %all-to-all-start.4 = ((f32[32,8,256]{2,1,0:T(8,128)}), f32[32,8,256]{2,1,0:T(8,128)S(1)}, u32[]{:S(2)}, u32[]{:S(2)}) async-start(f32[32,8,256]{2,1,0:T(8,128)} %bitcast.94), calls=%async_computation.4 | async-start | bytes 524288 | tf_op jit(solution)/shard_map/all_to_all | solution.py:558
  180.5 6.6 %collective-permute-start.13 = (bf16[64,1024]{1,0:T(8,128)(2,1)}, bf16[64,1024]{1,0:T(8,128)(2,1)S(1)}, u32[]{:S(2)}, u32[]{:S(2)}) collective-permute-start(bf16[64,1024]{1,0:T(8,128)(2,1)} %get-tuple-element.77), channel_id=1, source_target_pairs={{0,64},{64,128},{128,192},{192,0},{1,65},{65,129},{129,193},{193,1... | collective-permute-start | bytes 393224 | tf_op jit(solution)/shard_map/ppermute | solution.py:49
  180.7 12.7 %collective-permute-start.16 = (bf16[64,1280]{1,0:T(8,128)(2,1)}, bf16[64,1280]{1,0:T(8,128)(2,1)S(1)}, u32[]{:S(2)}, u32[]{:S(2)}) collective-permute-start(bf16[64,1280]{1,0:T(8,128)(2,1)} %get-tuple-element.81), channel_id=1, source_target_pairs={{0,16},{16,32},{32,48},{48,0},{1,17},{17,33},{33,49},{49,1},{2,18}... | collective-permute-start | bytes 491528 | tf_op jit(solution)/shard_map/ppermute | solution.py:49
  180.7 12.7 %collective-permute-start.17 = (bf16[64,1280]{1,0:T(8,128)(2,1)}, bf16[64,1280]{1,0:T(8,128)(2,1)S(1)}, u32[]{:S(2)}, u32[]{:S(2)}) collective-permute-start(bf16[64,1280]{1,0:T(8,128)(2,1)} %get-tuple-element.82), channel_id=1, source_target_pairs={{0,32},{16,48},{32,0},{48,16},{1,33},{17,49},{33,1},{49,17},{2,34}... | collective-permute-start | bytes 491528 | tf_op jit(solution)/shard_map/ppermute | solution.py:49
  182.5 11.0 %collective-permute-start.18 = (bf16[64,1280]{1,0:T(8,128)(2,1)}, bf16[64,1280]{1,0:T(8,128)(2,1)S(1)}, u32[]{:S(2)}, u32[]{:S(2)}) collective-permute-start(bf16[64,1280]{1,0:T(8,128)(2,1)} %get-tuple-element.83), channel_id=1, source_target_pairs={{0,48},{16,0},{32,16},{48,32},{1,49},{17,1},{33,17},{49,33},{2,50}... | collective-permute-start | bytes 491528 | tf_op jit(solution)/shard_map/ppermute | solution.py:49
  184.0 6.9 %collective-permute-start.14 = (bf16[64,1024]{1,0:T(8,128)(2,1)}, bf16[64,1024]{1,0:T(8,128)(2,1)S(1)}, u32[]{:S(2)}, u32[]{:S(2)}) collective-permute-start(bf16[64,1024]{1,0:T(8,128)(2,1)} %get-tuple-element.78), channel_id=1, source_target_pairs={{0,128},{64,192},{128,0},{192,64},{1,129},{65,193},{129,1},{193,65... | collective-permute-start | bytes 393224 | tf_op jit(solution)/shard_map/ppermute | solution.py:49
  187.1 6.4 %collective-permute-start.15 = (bf16[64,1024]{1,0:T(8,128)(2,1)}, bf16[64,1024]{1,0:T(8,128)(2,1)S(1)}, u32[]{:S(2)}, u32[]{:S(2)}) collective-permute-start(bf16[64,1024]{1,0:T(8,128)(2,1)} %get-tuple-element.79), channel_id=1, source_target_pairs={{0,192},{64,0},{128,64},{192,128},{1,193},{65,1},{129,65},{193,129... | collective-permute-start | bytes 393224 | tf_op jit(solution)/shard_map/ppermute | solution.py:49
  (29 other events, 148.9 us)

commit v2 on v1

--- a/solution.py
+++ b/solution.py
@@ -55,7 +55,7 @@
 
 
 def summed(refs):
-    total = refs[0][...]
+    total = refs[0][...].astype(F32)
     for ref in refs[1:]:
         total = total + ref[...].astype(F32)
     return total
@@ -174,117 +174,144 @@
     route_ref[...] = route
 
 
-def back_kernel(grad_ref, mix_ref, act_ref, one_ref, two_ref, gate_ref, up_ref, *refs):
-    input_ref, pair_ref, inner_ref = refs[-3:]
+def back_kernel(grad_ref, mix_ref, one_ref, two_ref, gate_ref, up_ref, *refs):
+    input_ref, pair_ref = refs[-2:]
     ff = one_ref.shape[1]
 
     @pl.when(pl.program_id(0) == 0)
     def _():
-        grad = grad_ref[...]
-        act_grad = dot(grad, mix_ref[...], 1, 1)
+        act_grad = dot(grad_ref[...], mix_ref[...], 1, 1)
         pair_ref[:, :ff] = (act_grad * one_ref[...]).astype(BF16)
         pair_ref[:, ff:] = (act_grad * two_ref[...]).astype(BF16)
-        inner_ref[...] = dot(act_ref[...], grad, 0, 0).astype(BF16)
 
     input_ref[...] = (
         dot(pair_ref[:, :ff], gate_ref[...], 1, 1) + dot(pair_ref[:, ff:], up_ref[...], 1, 1)
     ).astype(BF16)
 
 
-def parts_kernel(
-    shifts, coord_ref, rows_x, rows_x2, rows_y, rows_y2, value_x, value_y, resid_x, resid_x2,
-    down_x, pair_ref, pair2_ref, inner_ref, inner2_ref, grad_ref, grad2_ref, *refs,
+def far_kernel(
+    coord_ref, rows_x, rows_x2, resid_x, resid_x2, down_x, rows_y, rows_y2, value_y, pair_ref,
+    grad_ref, grad2_ref, row_grad, row_grad2, mix_ref, one2_ref, two2_ref, act_ref, act2_ref,
+    first_ref, second_ref, pair2_ref, inner_ref,
+):
+    ff = act_ref.shape[1]
+    act_grad = dot(row_grad2[...], mix_ref[...], 1, 1)
+    pair2_ref[:, :ff] = (act_grad * one2_ref[...]).astype(BF16)
+    pair2_ref[:, ff:] = (act_grad * two2_ref[...]).astype(BF16)
+    inner_ref[...] = (
+        dot(act_ref[...], row_grad[...], 0, 0) + dot(act2_ref[...], row_grad2[...], 0, 0)
+    ).astype(BF16)
+    gates, ups = slice(None, ff), slice(ff, None)
+    x_kernel(
+        1, coord_ref, rows_x, rows_x2, resid_x, resid_x2, down_x, pair_ref.at[:, gates],
+        pair2_ref.at[:, gates], inner_ref, grad_ref, grad2_ref, first_ref,
+    )
+    y_kernel(
+        1, coord_ref, rows_y, rows_y2, value_y, pair_ref.at[:, ups], pair2_ref.at[:, ups],
+        inner_ref, second_ref,
+    )
+
+
+def own_kernel(
+    coord_ref, rows_x, rows_x2, resid_x, resid_x2, down_x, rows_y, rows_y2, value_y, pair_ref,
+    pair2_ref, inner_ref, grad_ref, grad2_ref, token, first_ref, second_ref,
+):
+    del token
+    ff = inner_ref.shape[0]
+    gates, ups = slice(None, ff), slice(ff, None)
+    x_kernel(
+        1, coord_ref, rows_x, rows_x2, resid_x, resid_x2, down_x, pair_ref.at[:, gates],
+        pair2_ref.at[:, gates], inner_ref, grad_ref, grad2_ref, first_ref,
+    )
+    y_kernel(
+        1, coord_ref, rows_y, rows_y2, value_y, pair_ref.at[:, ups], pair2_ref.at[:, ups],
+        inner_ref, second_ref,
+    )
+
+
+def flat(ref):
+    return ref[...].reshape(ref.shape[0] * ref.shape[1] * ref.shape[2], ref.shape[3])
+
+
+def write(outs, at, value):
+    for number, out in enumerate(outs):
+
+        def put():
+            shape = out.shape[:2] + (value.shape[1],)
+            out[:, :, at : at + value.shape[1]] = value.reshape(shape).astype(out.dtype)
+
+        if len(outs) == 1:
+            put()
+        else:
+            pl.when(pl.program_id(0) == number)(put)
+
+
+def x_kernel(
+    count, coord_ref, rows_x, rows_x2, resid_x, resid_x2, down_x, pair_ref, pair2_ref, inner_ref,
+    grad_ref, grad2_ref, *outs,
 ):
     del coord_ref
-    outs, inner = refs[:-1], refs[-1]
-    step = pl.program_id(0)
-    each = len(outs) // (2 * len(shifts))
-    ff, bins = inner.shape
-    cut = ff - 2 * bins
-
-    @pl.when(step == 0)
-    def _():
-        inner[...] = (inner_ref[...].astype(F32) + inner2_ref[...].astype(F32)).astype(BF16)
-
-    def flat(ref):
-        return ref[...].reshape(ref.shape[0] * ref.shape[1] * ref.shape[2], ref.shape[3])
-
-    def write(place, at, value):
-        half = len(outs) // 2
-        for number in range(len(shifts)):
-
-            def put():
-                targets = outs[place * half + number * each : place * half + (number + 1) * each]
-                begin = 0
-                for out in targets:
-                    low, high = max(at, begin), min(at + value.shape[1], begin + out.shape[2])
-                    if low < high:
-                        part = value[:, low - at : high - at]
-                        out[:, :, low - begin : high - begin] = part.reshape(
-                            out.shape[:2] + (high - low,)
-                        ).astype(out.dtype)
-                    begin += out.shape[2]
-
-            if len(shifts) == 1:
-                put()
-            else:
-                pl.when(step == number)(put)
-
-    write(0, 0, dot(flat(rows_x), pair_ref[:, :ff]) + dot(flat(rows_x2), pair2_ref[:, :ff]))
-    write(0, ff, dot(flat(value_x), inner[:cut, :], 1, 1))
+    outs = outs[-count:]
+    write(outs, 0, dot(flat(rows_x), pair_ref[...]) + dot(flat(rows_x2), pair2_ref[...]))
     write(
-        0,
-        ff + cut,
+        outs,
+        pair_ref.shape[1],
         dot(flat(resid_x), grad_ref[...])
         + dot(flat(resid_x2), grad2_ref[...])
-        + dot(flat(down_x), inner[...]),
-    )
-    write(1, 0, dot(flat(rows_y), pair_ref[:, ff:]) + dot(flat(rows_y2), pair2_ref[:, ff:]))
-    write(1, ff, dot(flat(value_y), inner[cut:, :], 1, 1))
-
-
-def fold_kernel(*refs):
-    half = len(refs) // 3
-    for number in range(half):
-        block, came, out = refs[number], refs[half + number], refs[2 * half + number]
-        columns = came.shape[2]
-        at = 0 if number % 2 == 0 else columns
-        out[:, :, columns - at : 2 * columns - at] = block[:, :, columns - at : 2 * columns - at]
-        out[:, :, at : at + columns] = (
-            block[:, :, at : at + columns].astype(F32) + came[...].astype(F32)
-        ).astype(BF16)
-
-
-def middle_kernel(side_x, side_y, coord_ref, placed_ref, rows_ref, *refs):
-    refs = list(refs)
-    firsts = [refs.pop(0) for _ in range(3)]
-    seconds = [refs.pop(0) for _ in range(3)]
-    hidden_ref, head_ref = refs.pop(0), refs.pop(0)
-    first_outs = [refs.pop(0) for _ in range(side_y)]
-    second_outs = [refs.pop(0) for _ in range(side_x)]
-    first_full, second_full = refs
-    columns = first_outs[0].shape[1]
-    first_full[...] = summed(firsts)
-    second_full[...] = summed(seconds)
-    for shift, out in enumerate(first_outs):
-        out[...] = first_full[lax.rem(coord_ref[1] + shift, side_y), :, :columns].astype(out.dtype)
-    for shift, out in enumerate(second_outs):
-        out[...] = second_full[lax.rem(coord_ref[0] + shift, side_x)].astype(out.dtype)
-    head_ref[...] = first_full[:, :, columns:]
-    hidden_ref[...] = dot(placed_ref[...], rows_ref[...], 0, 0).astype(BF16)
+        + dot(flat(down_x), inner_ref[...]),
+    )
+
+
+def y_kernel(
+    count, coord_ref, rows_y, rows_y2, value_y, pair_ref, pair2_ref, inner_ref, *outs
+):
+    del coord_ref
+    outs = outs[-count:]
+    write(outs, 0, dot(flat(rows_y), pair_ref[...]) + dot(flat(rows_y2), pair2_ref[...]))
+    write(outs, pair_ref.shape[1], dot(flat(value_y), inner_ref[...], 1, 1))
+
+
+def first_kernel(coord_ref, *refs):
+    full, head_ref, outs = refs[-1], refs[-6], refs[-5:-1]
+    columns = outs[0].shape[1]
+    full[...] = summed(refs[:4])
+    head_ref[...] = full[:, :, columns:]
+    for shift, out in enumerate(outs):
+        at = lax.rem(coord_ref[1] + shift, full.shape[0])
+        out[...] = full[at, :, :columns].astype(out.dtype)
+
+
+def second_kernel(coord_ref, *refs):
+    full, outs = refs[-1], refs[-5:-1]
+    full[...] = summed(refs[:4])
+    for shift, out in enumerate(outs):
+        out[...] = full[lax.rem(coord_ref[0] + shift, full.shape[0])].astype(out.dtype)
+
+
+def hidden_kernel(placed_ref, rows_ref, head_ref, out_ref, pass_ref):
+    out_ref[...] = dot(placed_ref[...], rows_ref[...], 0, 0).astype(BF16)
+    pass_ref[...] = head_ref[...]
 
 
 def last_kernel(side_x, side_y, head_ref, *refs):
     firsts, seconds = refs[:side_y], refs[side_y : side_y + side_x]
     gate_ref, up_ref, down_ref, value_ref = refs[side_y + side_x :]
     ff = gate_ref.shape[1]
-    first, second = summed(firsts), summed(seconds)
-    gate_ref[...] = first[:, :ff]
+    gate_ref[...] = summed(firsts)
+    second = summed(seconds)
     up_ref[...] = second[:, :ff]
-    cut = first.shape[1] - ff
-    down_ref[:, :cut] = first[:, ff:]
-    down_ref[:, cut:] = second[:, ff:]
+    down_ref[...] = second[:, ff:]
     value_ref[...] = jnp.sum(head_ref[...], axis=0)
+
+
+def turn_kernel(core_ref, rows_ref, token, mine_ref, other_ref):
+    del token
+    own = mine_ref.shape[1]
+    for at in range(mine_ref.shape[0]):
+        turned = rows_ref[:, 2 * own * at : 2 * own * (at + 1)].T
+        low, high = turned[:own], turned[own:]
+        mine_ref[at] = jnp.where(core_ref[0] == 0, low, high)
+        other_ref[at] = jnp.where(core_ref[0] == 0, high, low)
 
 
 def per_shift(count, shape):
@@ -320,6 +347,8 @@
     smem = pl.BlockSpec(memory_space=pltpu.SMEM)
     vmem = pl.BlockSpec(memory_space=pltpu.VMEM)
 
+    coords = jnp.stack([lax.axis_index("x"), lax.axis_index("y")]).astype(jnp.int32)
+
     def core_half(array):
         blocks = array.reshape(side_y * side_x, 2, own_rows, array.shape[1])
         mine = pick(blocks, core, 1).reshape(width // 2, array.shape[1])
@@ -358,7 +387,7 @@
         resid_mine, resid_other = core_half(resid_in.T)
         resid_peer = swap_cores(resid_other)
 
-    steps = 3
+    steps = 1
     part = ff // steps
     act, one, two, route_logits = pl.pallas_call(
         lambda *refs: front_kernel(cap, *refs),
@@ -390,14 +419,31 @@
     )(in_rows, gate_w, up_w, mix, sums, value_mine, down_mine, resid_mine, resid_peer)
     back_logits = exchange(route_logits)
     with jax.named_scope("turned"):
-        rows_mine, rows_other = core_half(in_rows.T)
-        rows_peer = swap_cores(rows_other)
+        chips = side_y * side_x
+        rows_mine, rows_other = pl.pallas_call(
+            turn_kernel,
+            grid=(4,),
+            in_specs=[
+                smem,
+                pl.BlockSpec((slot_total, width // 4), lambda i: (0, i)),
+                anywhere,
+            ],
+            out_specs=[pl.BlockSpec((chips // 4, own_rows, slot_total), lambda i: (i, 0, 0))] * 2,
+            out_shape=(sds((chips, own_rows, slot_total), BF16),) * 2,
+            compiler_params=params(),
+            cost_estimate=cost(0, 4 * slot_total * width),
+            name="turn",
+        )(core.astype(jnp.int32)[None], in_rows, act)
+        rows_mine = rows_mine.reshape(width // 2, slot_total)
+        rows_peer = swap_cores(rows_other).reshape(width // 2, slot_total)
+        act_peer, one_peer, two_peer = swap_cores(act), swap_cores(one), swap_cores(two)
 
     out_grad, logit_grad, grad_route = pl.pallas_call(
         lambda *refs: head_kernel(cap, token_count, *refs),
         in_specs=[smem]
         + [vmem] * 5
-        + [anywhere] * 2,
+        + [anywhere] * 2
+        + [smem],
         out_shape=(
             sds((slot_total, bins), BF16),
             sds((tok_rows, bins), BF16),
@@ -408,13 +454,15 @@
         name="head",
     )(
         run_moments, back_logits, slots, route_weight, resid_logits, returns.reshape(tok_rows, 1),
-        rows_mine, rows_other,
+        rows_mine, rows_other, coords,
     )
     row_grad = exchange_rows(out_grad)
     grad_peer = swap_cores(logit_grad)
 
-    strip = min(512, width)
-    input_grad, pair, inner = pl.pallas_call(
+    row_grad_peer = swap_cores(row_grad)
+
+    strip = min(1024, width)
+    input_grad, pair = pl.pallas_call(
         back_kernel,
         grid=(width // strip,),
         in_specs=[
@@ -422,141 +470,156 @@
             whole((ff, bins)),
             whole((slot_total, ff)),
             whole((slot_total, ff)),
-            whole((slot_total, ff)),
             pl.BlockSpec((strip, ff), lambda i: (i, 0)),
             pl.BlockSpec((strip, ff), lambda i: (i, 0)),
-            anywhere,
-            anywhere,
-        ],
+        ]
+        + [anywhere] * 5,
         out_specs=[
             pl.BlockSpec((slot_total, strip), lambda i: (0, i)),
             whole((slot_total, 2 * ff)),
-            whole((ff, bins)),
         ],
         out_shape=(
             sds((slot_total, width), BF16),
             sds((slot_total, 2 * ff), BF16),
-            sds((ff, bins), BF16),
         ),
         compiler_params=params(),
         cost_estimate=cost(4 * slot_total * width * ff, 4 * width * ff),
         name="back",
-    )(row_grad, mix, act, one, two, gate_w, up_w, rows_peer, grad_peer)
+    )(
+        row_grad, mix, one, two, gate_w, up_w, rows_peer, grad_peer, act_peer, one_peer, two_peer
+    )
     back_grad = exchange_rows(input_grad)
-    inner_peer = swap_cores(inner)
-    pair_peer = swap_cores(pair)
 
     half = width // 2
-    coords = jnp.stack([lax.axis_index("x"), lax.axis_index("y")]).astype(jnp.int32)
-    def parts(shifts, out_shape):
-        pattern = {(2,): lambda step: 2, (1, 3, 0): lambda step: lax.rem(2 * step + 1, 5)}[shifts]
+    first_block, second_block = (side_y, own_rows, ff + bins), (side_x, own_rows, 2 * ff)
+
+    def parts(kernel, shifts, blocked, shared, outs, name):
+        def shift_of(step):
+            return shifts[0] if len(shifts) == 1 else shifts[0] + step * (shifts[1] - shifts[0])
 
         def tall(depth):
             return pl.BlockSpec(
                 (side_y, 1, own_rows, depth),
-                lambda step, at: (0, lax.rem(at[0] + pattern(step), side_x), 0, 0),
+                lambda step, at: (0, lax.rem(at[0] + shift_of(step), side_x), 0, 0),
             )
 
         def wide(depth):
             return pl.BlockSpec(
                 (1, side_x, own_rows, depth),
-                lambda step, at: (lax.rem(at[1] + pattern(step), side_y), 0, 0, 0),
+                lambda step, at: (lax.rem(at[1] + shift_of(step), side_y), 0, 0, 0),
             )
 
+        makes = {"x": tall, "y": wide}
         return pl.pallas_call(
-            lambda *refs: parts_kernel(shifts, *refs),
+            kernel,
             grid_spec=pltpu.PrefetchScalarGridSpec(
                 num_scalar_prefetch=1,
                 grid=(len(shifts),),
-                in_specs=[
-                    tall(slot_total),
-                    tall(slot_total),
-                    wide(slot_total),
-                    wide(slot_total),
-                    tall(bins),
-                    wide(bins),
-                    tall(tok_rows),
-                    tall(tok_rows),
-                    tall(ff),
-                    whole((slot_total, 2 * ff)),
-                    whole((slot_total, 2 * ff)),
-                    whole((ff, bins)),
-                    whole((ff, bins)),
-                    whole((tok_rows, bins)),
-                    whole((tok_rows, bins)),
-                ],
-                out_specs=[whole(out.shape) for out in out_shape],
-                scratch_shapes=[pltpu.VMEM((ff, bins), BF16)],
+                in_specs=[makes[along](rows.shape[1]) for along, rows in blocked]
+                + [whole(item.shape) if spec is None else spec for spec, item in shared],
+                out_specs=[whole(out.shape) for out in outs],
             ),
-            out_shape=out_shape,
+            out_shape=outs,
             compiler_params=params(),
-            cost_estimate=cost(len(shifts) * half * slot_total * 2 * ff, len(shifts) * 4 * MIB),
-            name="parts%d" % len(shifts),
+            cost_estimate=cost(len(shifts) * half * slot_total * ff, len(shifts) * 3 * MIB),
+            name=name,
         )(
             coords,
-            *[
-                rows.reshape(side_y, side_x, own_rows, rows.shape[1])
-                for rows in (
-                    rows_mine, rows_peer, rows_mine, rows_peer, value_mine, value_mine, resid_mine,
-                    resid_peer, down_mine,
-                )
-            ],
-            pair,
-            pair_peer,
-            inner,
-            inner_peer,
-            logit_grad,
-            grad_peer,
+            *[rows.reshape(side_y, side_x, own_rows, rows.shape[1]) for _, rows in blocked],
+            *[item for _, item in shared],
         )
 
     def step_on(array, axis_name, shift):
         size = lax.axis_size(axis_name)
         return lax.ppermute(array, axis_name, [(k, (k + shift) % size) for k in range(size)])
 
-    cut = ff - 2 * bins
-    first_columns, second_columns = ff + cut, 2 * ff - cut
-    columns = first_columns + bins
-    block = (side_y, own_rows, columns)
-    far = sds((side_y, own_rows, columns // 2), BF16)
-    x_up, x_down, y_up, y_down = parts((2,), (far,) * 4)
-    came = (
-        step_on(x_up, "x", 1),
-        step_on(x_down, "x", -1),
-        step_on(y_up, "y", 1),
-        step_on(y_down, "y", -1),
-    )
-    near, own = sds(block, BF16), sds(block, F32)
-    x_up, x_down, x_own, y_up, y_down, y_own = parts(
-        (1, 3, 0), (near, near, own, near, near, own)
-    )
-    x_up, x_down, y_up, y_down = pl.pallas_call(
-        fold_kernel,
-        out_shape=(near,) * 4,
-        compiler_params=params(),
-        cost_estimate=cost(0, 24 * side_y * own_rows * columns),
-        name="fold",
-    )(x_up, x_down, y_up, y_down, *came)
-    firsts = (x_own, step_on(x_up, "x", 1), step_on(x_down, "x", -1))
-    seconds = (y_own, step_on(y_up, "y", 1), step_on(y_down, "y", -1))
-
-    grad_hidden, head, *halves = pl.pallas_call(
-        lambda *refs: middle_kernel(side_x, side_y, *refs),
-        in_specs=[smem] + [vmem] * 8,
-        out_shape=(
-            sds((tok_rows, width), BF16),
-            sds((side_y, own_rows, bins), F32),
-        )
-        + per_shift(side_y, (own_rows, first_columns))
-        + per_shift(side_x, (own_rows, second_columns)),
-        scratch_shapes=[pltpu.VMEM(block, F32), pltpu.VMEM(block, F32)],
+    x_rows = [("x", r) for r in (rows_mine, rows_peer, resid_mine, resid_peer, down_mine)]
+    y_rows = [("y", r) for r in (rows_mine, rows_peer, value_mine)]
+    first_out, second_out = sds(first_block, BF16), sds(second_block, BF16)
+    first_far, second_far, pair_peer, inner = parts(
+        far_kernel,
+        (2,),
+        x_rows + y_rows,
+        [
+            (None, item)
+            for item in (
+                pair, logit_grad, grad_peer, row_grad, row_grad_peer, mix, one_peer, two_peer,
+                act, act_peer,
+            )
+        ],
+        [first_out, second_out, sds(pair.shape, BF16), sds((ff, bins), BF16)],
+        "far",
+    )
+    gate_spec = pl.BlockSpec((slot_total, ff), lambda *_: (0, 0))
+    up_spec = pl.BlockSpec((slot_total, ff), lambda *_: (0, 1))
+
+    firsts = [step_on(first_far, "x", 2)]
+    seconds = [step_on(second_far, "y", 2)]
+    first_up, first_down = parts(
+        lambda *refs: x_kernel(2, *refs),
+        (1, 3),
+        x_rows,
+        [
+            (gate_spec, pair), (gate_spec, pair_peer), (None, inner), (None, logit_grad),
+            (None, grad_peer),
+        ],
+        [first_out] * 2,
+        "x_near",
+    )
+    firsts += [step_on(first_up, "x", 1), step_on(first_down, "x", 3)]
+    first_own, second_own = parts(
+        own_kernel,
+        (0,),
+        x_rows + y_rows,
+        [
+            (None, pair), (None, pair_peer), (None, inner), (None, logit_grad), (None, grad_peer),
+            (anywhere, first_up),
+        ],
+        [first_out, second_out],
+        "own",
+    )
+    second_up, second_down = parts(
+        lambda *refs: y_kernel(2, *refs),
+        (1, 3),
+        y_rows,
+        [
+            (up_spec, pair), (up_spec, pair_peer), (None, inner), (anywhere, seconds[0]),
+            (anywhere, second_own),
+        ],
+        [second_out] * 2,
+        "y_near",
+    )
+    seconds += [step_on(second_up, "y", 1), step_on(second_down, "y", 3)]
+
+    head, *firsts = pl.pallas_call(
+        first_kernel,
+        in_specs=[smem] + [vmem] * 4,
+        out_shape=(sds((side_y, own_rows, bins), F32),) + per_shift(side_y, (own_rows, ff)),
+        scratch_shapes=[pltpu.VMEM(first_block, F32)],
+        compiler_params=params(),
+        cost_estimate=cost(0, 12 * side_y * own_rows * ff),
+        name="first",
+    )(coords, first_own, *firsts)
+    first_came = send(firsts, "y")
+    seconds = pl.pallas_call(
+        second_kernel,
+        in_specs=[smem] + [vmem] * 4,
+        out_shape=per_shift(side_x, (own_rows, 2 * ff)),
+        scratch_shapes=[pltpu.VMEM(second_block, F32)],
+        compiler_params=params(),
+        cost_estimate=cost(0, 24 * side_y * own_rows * ff),
+        name="second",
+    )(coords, second_own, *seconds)
+    second_came = send(seconds, "x")
+    grad_hidden, head = pl.pallas_call(
+        hidden_kernel,
+        out_shape=(sds((tok_rows, width), BF16), sds(head.shape, F32)),
         compiler_params=params(),
         cost_estimate=cost(2 * tok_rows * slot_total * width, 2 * width * (slot_total + tok_rows)),
-        name="middle",
-    )(coords, placed_any, back_grad, *firsts, *seconds)
-    firsts, seconds = halves[:side_y], halves[side_y:]
+        name="hidden",
+    )(placed_any, back_grad, head)
     shares = head.reshape(side_y * groups, own_rows // groups, bins)
     shares = lax.all_to_all(shares, ("y", "expert"), 0, 0, tiled=True)
-    first_came, second_came = send(firsts, "y"), send(seconds, "x")
     grad_gate, grad_up, grad_down, grad_value = pl.pallas_call(
         lambda *refs: last_kernel(side_x, side_y, *refs),
         out_shape=(

time: 199 us -> 187 us (0.940)
  waiting for transfers between devices: 43.1 us -> 32.9 us
  Pallas kernels: 51.8 us -> 59.4 us
  starting transfers between devices: 52.3 us -> 47 us
    ppermute x8 -> x6, waiting for transfers between devices: 15.5 us -> 5.79 us  [step_on(): lax.ppermute(array, axis_name, [(k, (k + shift) % size) for k in range(si...]
    pallas_call x4 -> x8, Pallas kernels: 27.8 us -> 36.8 us  [the longest x4 24 us: parts(): pl.pallas_call(kernel, grid_spec=pltpu.PrefetchScalarGridSpec(num_scalar_...]
    ppermute x8 -> x6, starting transfers between devices: 14.3 us -> 8.3 us  [step_on(): lax.ppermute(array, axis_name, [(k, (k + shift) % size) for k in range(si...]
    ppermute x5 -> x7, waiting for transfers between devices: 4.08 us -> 2.89 us  [swap_cores(): return lax.ppermute(array, 'core', [(0, 1), (1, 0)])]
    unnamed x62 -> x64, local copies, waits for them, and re-layouts: 13.2 us -> 14.4 us
    dynamic_slice x4 -> x3, local copies, waits for them, and re-layouts: 5.53 us -> 4.46 us  [pick(): return lax.dynamic_index_in_dim(array, index, axis, keepdims=False)]
  transfers between devices with their start and end apart: 24 -> 24, of which waited for: 12 -> 9; matrix products, arithmetic and copies ran while one was open for 11% -> 10% of each run, Pallas kernels for 13% -> 21%
where the time goes in v2:
time: 187 us; the launch traced here: 186 us
  Pallas kernels  59.4 us (32%)
  starting transfers between devices  47 us (25%)
  waiting for transfers between devices  32.9 us (18%)
  blocking collectives  21 us (11%)
  local copies, waits for them, and re-layouts  19.6 us (10%)
  matrix products  2.71 us (1%)
  other arithmetic  2.58 us (1%)
    pallas_call x4, Pallas kernels, parts(): pl.pallas_call(kernel, grid_spec=pltpu.PrefetchScalarGridSpec(num_scalar_...  24 us
    psum x3, blocking collectives, per_device(): sums = lax.psum(sums, axis_name)  21 us
    all_to_all x4, starting transfers between devices, exchange(): return lax.all_to_all(blocks, 'expert', 0, 0, tiled=True)  19.8 us
    all_to_all x4, waiting for transfers between devices, exchange(): return lax.all_to_all(blocks, 'expert', 0, 0, tiled=True)  19 us
    unnamed x64, local copies, waits for them, and re-layouts  14.4 us
    all_to_all x1, starting transfers between devices, per_device(): shares = lax.all_to_all(shares, ('y', 'expert'), 0, 0, tiled=True)  10.2 us
    ppermute x6, starting transfers between devices, step_on(): lax.ppermute(array, axis_name, [(k, (k + shift) % size) for k in range(si...  8.3 us
    pallas_call x1, Pallas kernels, per_device(): pl.pallas_call(lambda *refs: front_kernel(cap, *refs), grid=(steps,), in_...  7.9 us
  transfers between devices with their start and end apart: 24, of which 9 were waited for; matrix products, arithmetic and copies ran while one was open for 10% of the time, Pallas kernels for 21%

profile of v2, /device:TPU:24, one launch (start us, length us, event | category | flops | bytes accessed | tf_op | source)
XLA Modules:
  0.0 186.1 jit_solution(817094922911667262)
XLA Ops:
  0.6 3.0 %slots.1 = (bf16[384,2048]{1,0:T(8,128)(2,1)}, s32[2,128]{1,0:T(2,128)}, bf16[384,128]{1,0:T(8,128)(2,1)}) custom-call(s32[2,128]{1,0:T(2,128)} %bitcast.104, bf16[128,2048]{1,0:T(8,128)(2,1)} %refs_1_.1), custom_call_target="tpu_custom_call" | custom-call | flops 201326592 | bytes 2097152 | tf_op jit(solution)/shard_map/slots/pallas_call | solution.py:364
  3.7 8.6 %all-to-all-start = ((bf16[8,48,2048]{2,1,0:T(8,128)(2,1)}), bf16[8,48,2048]{2,1,0:T(8,128)(2,1)S(1)}, u32[]{:S(2)}, u32[]{:S(2)}) async-start(bf16[8,48,2048]{2,1,0:T(8,128)(2,1)} %bitcast.96), calls=%async_computation | async-start | bytes 3145728 | tf_op jit(solution)/shard_map/all_to_all | solution.py:359
  14.3 10.5 %psum.21 = f32[2]{0:T(128)S(1)} all-reduce(f32[2]{0:T(128)S(1)} %pad_maximum_fusion), channel_id=1, replica_groups=mesh['y'=4,'x'=4,'core'=2,'expert'=8] {'x'}, use_global_device_ids=true, to_apply=%region_2.0 | all-reduce | flops 2 | bytes 16 | tf_op jit(solution)/shard_map/moments/psum | solution.py:380
  24.7 7.5 %psum.22 = f32[2]{0:T(128)S(1)} all-reduce(f32[2]{0:T(128)S(1)} %psum.21), channel_id=1, replica_groups=mesh['y'=4,'x'=4,'core'=2,'expert'=8] {'y'}, use_global_device_ids=true, to_apply=%region_3.0 | all-reduce | flops 2 | bytes 16 | tf_op jit(solution)/shard_map/moments/psum | solution.py:380
  34.3 3.1 %psum.23.refs_4_ = f32[2]{0:T(128)} all-reduce(f32[2]{0:T(128)S(1)} %psum.22), channel_id=1, replica_groups=mesh['y'=4,'x'=4,'core'=2,'expert'=8] {'core'}, use_global_device_ids=true, to_apply=%region_4.0 | all-reduce | flops 2 | bytes 16 | tf_op jit(solution)/shard_map/moments/psum | solution.py:380
  37.4 4.7 %copy.23 = bf16[1,768,2048]{1,2,0:T(8,128)(2,1)} copy(bf16[1,768,2048]{2,1,0:T(8,128)(2,1)} %param.18) | data formatting | bytes 6291456 | tf_op args[8]
  42.9 2.9 %constant_dynamic-slice_fusion.2 = bf16[16,1,64,768]{3,2,1,0:T(8,128)(2,1)} fusion(bf16[16,2,64,768]{3,2,1,0:T(8,128)(2,1)} %bitcast.82, s32[]{:T(128)S(6)} %select_n.11), kind=kLoop, calls=%fused_computation.5 | loop fusion | bytes 3145732 | tf_op jit(solution)/shard_map/weights_only/jit(dynamic_index_in_dim)/dynamic_slice | solution.py:39
  47.5 4.7 %all-to-all-done = bf16[8,48,2048]{2,1,0:T(8,128)(2,1)S(1)} async-done(((bf16[8,48,2048]{2,1,0:T(8,128)(2,1)}), bf16[8,48,2048]{2,1,0:T(8,128)(2,1)S(1)}, u32[]{:S(2)}, u32[]{:S(2)}) %all-to-all-start) | async-done | bytes 1572896 | tf_op jit(solution)/shard_map/all_to_all | solution.py:359
  53.4 7.9 %front.1 = (bf16[384,768]{1,0:T(8,128)(2,1)}, f32[384,768]{1,0:T(8,128)}, f32[384,768]{1,0:T(8,128)}, bf16[8,64,256]{2,1,0:T(8,128)(2,1)}) custom-call(bf16[384,2048]{1,0:T(8,128)(2,1)} %bitcast.72, bf16[2048,768]{1,0:T(8,128)(2,1)} %bitcast.78, bf16[2048,768]{1,0:T(8,128)(2,1)} %bitcast.80, bf16[768,256]{1,0:T(8,128)(2,1)} %fusion.2.refs_3_.mix_ref, ...), custom_call_target="tpu_custom_call" | custom-call | flops 2415919104 | bytes 6291456 | tf_op jit(solution)/shard_map/front/pallas_call | solution.py:392
  61.9 4.1 %all-to-all-start.1 = ((bf16[8,64,256]{2,1,0:T(8,128)(2,1)}), bf16[8,64,256]{2,1,0:T(8,128)(2,1)}, u32[]{:S(2)}, u32[]{:S(2)}) async-start(bf16[8,64,256]{2,1,0:T(8,128)(2,1)} %get-tuple-element.47), calls=%async_computation.1 | async-start | bytes 524288 | tf_op jit(solution)/shard_map/all_to_all | solution.py:359
  66.0 3.8 %turn.1 = (bf16[16,64,384]{2,1,0:T(8,128)(2,1)}, bf16[16,64,384]{2,1,0:T(8,128)(2,1)}) custom-call(s32[1]{0:T(128)} %bitcast.19.core_ref, bf16[384,2048]{1,0:T(8,128)(2,1)} %bitcast.73, bf16[384,768]{1,0:T(8,128)(2,1)} %get-tuple-element.49.token.act_ref), custom_call_target="tpu_custom_call" | custom-call | bytes 3145728 | tf_op jit(solution)/shard_map/turned/turn/pallas_call | solution.py:423
  73.3 5.0 %all-to-all-done.1.refs_1_ = bf16[8,64,256]{2,1,0:T(8,128)(2,1)} async-done(((bf16[8,64,256]{2,1,0:T(8,128)(2,1)}), bf16[8,64,256]{2,1,0:T(8,128)(2,1)}, u32[]{:S(2)}, u32[]{:S(2)}) %all-to-all-start.1) | async-done | bytes 262176 | tf_op jit(solution)/shard_map/all_to_all | solution.py:359
  80.9 3.4 %all-to-all-start.2 = ((bf16[8,48,256]{2,1,0:T(8,128)(2,1)}), bf16[8,48,256]{2,1,0:T(8,128)(2,1)S(1)}, u32[]{:S(2)}, u32[]{:S(2)}) async-start(bf16[8,48,256]{2,1,0:T(8,128)(2,1)} %bitcast.99), calls=%async_computation.2 | async-start | bytes 393216 | tf_op jit(solution)/shard_map/all_to_all | solution.py:359
  85.8 9.3 %all-to-all-done.2 = bf16[8,48,256]{2,1,0:T(8,128)(2,1)S(1)} async-done(((bf16[8,48,256]{2,1,0:T(8,128)(2,1)}), bf16[8,48,256]{2,1,0:T(8,128)(2,1)S(1)}, u32[]{:S(2)}, u32[]{:S(2)}) %all-to-all-start.2) | async-done | bytes 196640 | tf_op jit(solution)/shard_map/all_to_all | solution.py:359
  96.2 6.9 %back.1 = (bf16[384,2048]{1,0:T(8,128)(2,1)}, bf16[384,1536]{1,0:T(8,128)(2,1)}) custom-call(bf16[384,256]{1,0:T(8,128)(2,1)} %bitcast.92, bf16[768,256]{1,0:T(8,128)(2,1)} %fusion.2.refs_3_.mix_ref, f32[384,768]{1,0:T(8,128)} %get-tuple-element.53.one_ref, f32[384,768]{1,0:T(8,128)} %get-tuple-element.54.two_ref, bf16[2048,768]{1,0:T(8,128)(2,1)} %bitcast.79, ...), custom_call_target="tpu_custom_call" | custom-call | flops 2415919104 | bytes 6291456 | tf_op jit(solution)/shard_map/back/pallas_call | solution.py:465
  103.1 3.7 %all-to-all-start.3 = ((bf16[8,48,2048]{2,1,0:T(8,128)(2,1)}), bf16[8,48,2048]{2,1,0:T(8,128)(2,1)S(1)}, u32[]{:S(2)}, u32[]{:S(2)}) async-start(bf16[8,48,2048]{2,1,0:T(8,128)(2,1)} %bitcast.95), calls=%async_computation.3 | async-start | bytes 3145728 | tf_op jit(solution)/shard_map/all_to_all | solution.py:359
  109.2 6.9 %far.1 = (bf16[4,64,1024]{2,1,0:T(8,128)(2,1)}, bf16[4,64,1536]{2,1,0:T(8,128)(2,1)}, bf16[384,1536]{1,0:T(8,128)(2,1)}, bf16[768,256]{1,0:T(8,128)(2,1)}) custom-call(s32[2]{0:T(128)} %pad_add_fusion.refs_8_.coord_ref.refs_0_, bf16[4,4,64,384]{3,2,1,0:T(8,128)(2,1)} %bitcast.59, bf16[4,4,64,384]{3,2,1,0:T(8,128)(2,1)} %bitcast.66, ...), custom_call_target="tpu_custom_call" | custom-call | flops 301989888 | bytes 3145728 | tf_op jit(solution)/shard_map/far/pallas_call | solution.py:513
  117.3 3.0 %collective-permute-start.7 = (bf16[4,64,1024]{2,1,0:T(8,128)(2,1)}, bf16[4,64,1024]{2,1,0:T(8,128)(2,1)S(1)}, u32[]{:S(2)}, u32[]{:S(2)}) collective-permute-start(bf16[4,64,1024]{2,1,0:T(8,128)(2,1)} %get-tuple-element.62), channel_id=1, source_target_pairs={{0,32},{16,48},{32,0},{48,16},{1,33},{17,49},{33,1},{49,17},{2,34}... | collective-permute-start | bytes 1572872 | tf_op jit(solution)/shard_map/ppermute | solution.py:534
  120.4 6.1 %x_near.1 = (bf16[4,64,1024]{2,1,0:T(8,128)(2,1)}, bf16[4,64,1024]{2,1,0:T(8,128)(2,1)}) custom-call(s32[2]{0:T(128)} %pad_add_fusion.refs_8_.coord_ref.refs_0_, bf16[4,4,64,384]{3,2,1,0:T(8,128)(2,1)} %bitcast.61, bf16[4,4,64,384]{3,2,1,0:T(8,128)(2,1)} %bitcast.68, bf16[4,4,64,128]{3,2,1,0:T(8,128)(2,1)} %bitcast.85, bf16[4,4,64,128]{3,2,1,0:T(8,128)(2,1)} %bitcast.89, ...), custom_call_target="tpu_custom_call" | custom-call | flops 603979776 | bytes 6291456 | tf_op jit(solution)/shard_map/x_near/pallas_call | solution.py:513
  128.5 5.2 %own.1 = (bf16[4,64,1024]{2,1,0:T(8,128)(2,1)}, bf16[4,64,1536]{2,1,0:T(8,128)(2,1)}) custom-call(s32[2]{0:T(128)} %pad_add_fusion.refs_8_.coord_ref.refs_0_, bf16[4,4,64,384]{3,2,1,0:T(8,128)(2,1)} %bitcast.62, bf16[4,4,64,384]{3,2,1,0:T(8,128)(2,1)} %bitcast.69, bf16[4,4,64,128]{3,2,1,0:T(8,128)(2,1)} %bitcast.86, bf16[4,4,64,128]{3,2,1,0:T(8,128)(2,1)} %bitcast.90, ...), custom_call_target="tpu_custom_call" | custom-call | flops 301989888 | bytes 3145728 | tf_op jit(solution)/shard_map/own/pallas_call | solution.py:513
  133.6 3.8 %collective-permute-done.13.refs_7_.refs_1_ = bf16[4,64,1536]{2,1,0:T(8,128)(2,1)S(1)} collective-permute-done((bf16[4,64,1536]{2,1,0:T(8,128)(2,1)}, bf16[4,64,1536]{2,1,0:T(8,128)(2,1)S(1)}, u32[]{:S(2)}, u32[]{:S(2)}) %collective-permute-start.13) | collective-permute-done | bytes 786464 | tf_op jit(solution)/shard_map/ppermute | solution.py:534
  138.3 5.8 %y_near.1 = (bf16[4,64,1536]{2,1,0:T(8,128)(2,1)}, bf16[4,64,1536]{2,1,0:T(8,128)(2,1)}) custom-call(s32[2]{0:T(128)} %pad_add_fusion.refs_8_.coord_ref.refs_0_, bf16[4,4,64,384]{3,2,1,0:T(8,128)(2,1)} %bitcast.64, bf16[4,4,64,384]{3,2,1,0:T(8,128)(2,1)} %bitcast.71, bf16[4,4,64,256]{3,2,1,0:T(8,128)(2,1)} %bitcast.77, ...), custom_call_target="tpu_custom_call" | custom-call | flops 603979776 | bytes 6291456 | tf_op jit(solution)/shard_map/y_near/pallas_call | solution.py:513
  154.0 10.2 %all-to-all-start.4 = ((f32[32,8,256]{2,1,0:T(8,128)}), f32[32,8,256]{2,1,0:T(8,128)S(1)}, u32[]{:S(2)}, u32[]{:S(2)}) async-start(f32[32,8,256]{2,1,0:T(8,128)} %bitcast.98), calls=%async_computation.4 | async-start | bytes 524288 | tf_op jit(solution)/shard_map/all_to_all | solution.py:622
  166.5 3.5 %second.1 = (f32[64,1536]{1,0:T(8,128)}, bf16[64,1536]{1,0:T(8,128)(2,1)}, bf16[64,1536]{1,0:T(8,128)(2,1)}, bf16[64,1536]{1,0:T(8,128)(2,1)}) custom-call(s32[2]{0:T(128)} %pad_add_fusion.refs_8_.coord_ref.refs_0_, bf16[4,64,1536]{2,1,0:T(8,128)(2,1)} %get-tuple-element.72.refs_8_.refs_0_, bf16[4,64,1536]{2,1,0:T(8,128)(2,1)} %copy-done.7, ...), custom_call_target="tpu_custom_call" | custom-call | bytes 4718592 | tf_op jit(solution)/shard_map/second/pallas_call | solution.py:604
  (113 shorter events, 51.6 us)
Async XLA Ops:
  3.7 48.6 %all-to-all-start = ((bf16[8,48,2048]{2,1,0:T(8,128)(2,1)}), bf16[8,48,2048]{2,1,0:T(8,128)(2,1)S(1)}, u32[]{:S(2)}, u32[]{:S(2)}) async-start(bf16[8,48,2048]{2,1,0:T(8,128)(2,1)} %bitcast.96), calls=%async_computation | async-start | bytes 3145728 | tf_op jit(solution)/shard_map/all_to_all | solution.py:359
  34.3 13.3 %collective-permute-start = (bf16[1024,128]{1,0:T(8,128)(2,1)S(1)}, bf16[1024,128]{1,0:T(8,128)(2,1)S(1)}, u32[]{:S(2)}, u32[]{:S(2)}) collective-permute-start(bf16[1024,128]{1,0:T(8,128)(2,1)S(1)} %bitcast.97), channel_id=1, source_target_pairs={{0,8},{8,0},{1,9},{9,1},{2,10},{10,2},{3,11},{11,3},{4,12},{12,4},... | collective-permute-start | bytes 786440 | tf_op jit(solution)/shard_map/weights_only/ppermute | solution.py:43
  61.3 33.8 %collective-permute-start.4 = (f32[384,768]{1,0:T(8,128)}, f32[384,768]{1,0:T(8,128)S(1)}, u32[]{:S(2)}, u32[]{:S(2)}) collective-permute-start(f32[384,768]{1,0:T(8,128)} %get-tuple-element.53.one_ref), channel_id=1, source_target_pairs={{0,8},{8,0},{1,9},{9,1},{2,10},{10,2},{3,11},{11,3},{4,12},{12,4},... | collective-permute-start | bytes 3538952 | tf_op jit(solution)/shard_map/turned/ppermute | solution.py:43
  61.4 33.7 %collective-permute-start.5 = (f32[384,768]{1,0:T(8,128)}, f32[384,768]{1,0:T(8,128)}, u32[]{:S(2)}, u32[]{:S(2)}) collective-permute-start(f32[384,768]{1,0:T(8,128)} %get-tuple-element.54.two_ref), channel_id=1, source_target_pairs={{0,8},{8,0},{1,9},{9,1},{2,10},{10,2},{3,11},{11,3},{4,12},{12,4},... | collective-permute-start | bytes 3538952 | tf_op jit(solution)/shard_map/turned/ppermute | solution.py:43
  61.9 16.5 %all-to-all-start.1 = ((bf16[8,64,256]{2,1,0:T(8,128)(2,1)}), bf16[8,64,256]{2,1,0:T(8,128)(2,1)}, u32[]{:S(2)}, u32[]{:S(2)}) async-start(bf16[8,64,256]{2,1,0:T(8,128)(2,1)} %get-tuple-element.47), calls=%async_computation.1 | async-start | bytes 524288 | tf_op jit(solution)/shard_map/all_to_all | solution.py:359
  69.8 16.1 %collective-permute-start.1 = (bf16[16,64,384]{2,1,0:T(8,128)(2,1)}, bf16[16,64,384]{2,1,0:T(8,128)(2,1)S(1)}, u32[]{:S(2)}, u32[]{:S(2)}) collective-permute-start(bf16[16,64,384]{2,1,0:T(8,128)(2,1)} %get-tuple-element.51.refs_7_), channel_id=1, source_target_pairs={{0,8},{8,0},{1,9},{9,1},{2,10},{10,2},{3,11},{11,3},{4,12},{12,4},... | collective-permute-start | bytes 2359304 | tf_op jit(solution)/shard_map/turned/ppermute | solution.py:43
  72.0 13.9 %collective-permute-start.3 = (bf16[384,768]{1,0:T(8,128)(2,1)}, bf16[384,768]{1,0:T(8,128)(2,1)}, u32[]{:S(2)}, u32[]{:S(2)}) collective-permute-start(bf16[384,768]{1,0:T(8,128)(2,1)} %get-tuple-element.49.token.act_ref), channel_id=1, source_target_pairs={{0,8},{8,0},{1,9},{9,1},{2,10},{10,2},{3,11},{11,3},{4,12},{12,4},... | collective-permute-start | bytes 1769480 | tf_op jit(solution)/shard_map/turned/ppermute | solution.py:43
  80.9 14.2 %all-to-all-start.2 = ((bf16[8,48,256]{2,1,0:T(8,128)(2,1)}), bf16[8,48,256]{2,1,0:T(8,128)(2,1)S(1)}, u32[]{:S(2)}, u32[]{:S(2)}) async-start(bf16[8,48,256]{2,1,0:T(8,128)(2,1)} %bitcast.99), calls=%async_computation.2 | async-start | bytes 393216 | tf_op jit(solution)/shard_map/all_to_all | solution.py:359
  84.3 1.6 collective-permute-start.2
  103.1 47.0 %all-to-all-start.3 = ((bf16[8,48,2048]{2,1,0:T(8,128)(2,1)}), bf16[8,48,2048]{2,1,0:T(8,128)(2,1)S(1)}, u32[]{:S(2)}, u32[]{:S(2)}) async-start(bf16[8,48,2048]{2,1,0:T(8,128)(2,1)} %bitcast.95), calls=%async_computation.3 | async-start | bytes 3145728 | tf_op jit(solution)/shard_map/all_to_all | solution.py:359
  106.8 1.7 collective-permute-start.6
  116.1 21.3 %collective-permute-start.13 = (bf16[4,64,1536]{2,1,0:T(8,128)(2,1)}, bf16[4,64,1536]{2,1,0:T(8,128)(2,1)S(1)}, u32[]{:S(2)}, u32[]{:S(2)}) collective-permute-start(bf16[4,64,1536]{2,1,0:T(8,128)(2,1)} %get-tuple-element.73), channel_id=1, source_target_pairs={{0,128},{64,192},{128,0},{192,64},{1,129},{65,193},{129,1},{193,65... | collective-permute-start | bytes 2359304 | tf_op jit(solution)/shard_map/ppermute | solution.py:534
  117.3 28.8 %collective-permute-start.7 = (bf16[4,64,1024]{2,1,0:T(8,128)(2,1)}, bf16[4,64,1024]{2,1,0:T(8,128)(2,1)S(1)}, u32[]{:S(2)}, u32[]{:S(2)}) collective-permute-start(bf16[4,64,1024]{2,1,0:T(8,128)(2,1)} %get-tuple-element.62), channel_id=1, source_target_pairs={{0,32},{16,48},{32,0},{48,16},{1,33},{17,49},{33,1},{49,17},{2,34}... | collective-permute-start | bytes 1572872 | tf_op jit(solution)/shard_map/ppermute | solution.py:534
  126.4 19.8 %collective-permute-start.9 = (bf16[4,64,1024]{2,1,0:T(8,128)(2,1)}, bf16[4,64,1024]{2,1,0:T(8,128)(2,1)S(1)}, u32[]{:S(2)}, u32[]{:S(2)}) collective-permute-start(bf16[4,64,1024]{2,1,0:T(8,128)(2,1)} %get-tuple-element.63), channel_id=1, source_target_pairs={{0,48},{16,0},{32,16},{48,32},{1,49},{17,1},{33,17},{49,33},{2,50}... | collective-permute-start | bytes 1572872 | tf_op jit(solution)/shard_map/ppermute | solution.py:534
  127.6 18.6 %collective-permute-start.8 = (bf16[4,64,1024]{2,1,0:T(8,128)(2,1)}, bf16[4,64,1024]{2,1,0:T(8,128)(2,1)S(1)}, u32[]{:S(2)}, u32[]{:S(2)}) collective-permute-start(bf16[4,64,1024]{2,1,0:T(8,128)(2,1)} %get-tuple-element.60.token), channel_id=1, source_target_pairs={{0,16},{16,32},{32,48},{48,0},{1,17},{17,33},{33,49},{49,1},{2,18}... | collective-permute-start | bytes 1572872 | tf_op jit(solution)/shard_map/ppermute | solution.py:534
  144.1 20.4 %collective-permute-start.14 = (bf16[4,64,1536]{2,1,0:T(8,128)(2,1)}, bf16[4,64,1536]{2,1,0:T(8,128)(2,1)S(1)}, u32[]{:S(2)}, u32[]{:S(2)}) collective-permute-start(bf16[4,64,1536]{2,1,0:T(8,128)(2,1)} %get-tuple-element.74), channel_id=1, source_target_pairs={{0,64},{64,128},{128,192},{192,0},{1,65},{65,129},{129,193},{193,1... | collective-permute-start | bytes 2359304 | tf_op jit(solution)/shard_map/ppermute | solution.py:534
  146.2 20.4 %collective-permute-start.15 = (bf16[4,64,1536]{2,1,0:T(8,128)(2,1)}, bf16[4,64,1536]{2,1,0:T(8,128)(2,1)}, u32[]{:S(2)}, u32[]{:S(2)}) collective-permute-start(bf16[4,64,1536]{2,1,0:T(8,128)(2,1)} %get-tuple-element.75), channel_id=1, source_target_pairs={{0,192},{64,0},{128,64},{192,128},{1,193},{65,1},{129,65},{193,129... | collective-permute-start | bytes 2359304 | tf_op jit(solution)/shard_map/ppermute | solution.py:534
  154.0 28.9 %all-to-all-start.4 = ((f32[32,8,256]{2,1,0:T(8,128)}), f32[32,8,256]{2,1,0:T(8,128)S(1)}, u32[]{:S(2)}, u32[]{:S(2)}) async-start(f32[32,8,256]{2,1,0:T(8,128)} %bitcast.98), calls=%async_computation.4 | async-start | bytes 524288 | tf_op jit(solution)/shard_map/all_to_all | solution.py:622
  164.3 12.7 %collective-permute-start.10 = (bf16[64,768]{1,0:T(8,128)(2,1)S(1)}, bf16[64,768]{1,0:T(8,128)(2,1)S(1)}, u32[]{:S(2)}, u32[]{:S(2)}) collective-permute-start(bf16[64,768]{1,0:T(8,128)(2,1)S(1)} %copy-done.29), channel_id=1, source_target_pairs={{0,64},{64,128},{128,192},{192,0},{1,65},{65,129},{129,193},{193,1... | collective-permute-start | bytes 294920 | tf_op jit(solution)/shard_map/ppermute | solution.py:49
  170.0 12.8 %collective-permute-start.16 = (bf16[64,1536]{1,0:T(8,128)(2,1)}, bf16[64,1536]{1,0:T(8,128)(2,1)S(1)}, u32[]{:S(2)}, u32[]{:S(2)}) collective-permute-start(bf16[64,1536]{1,0:T(8,128)(2,1)} %get-tuple-element.77), channel_id=1, source_target_pairs={{0,16},{16,32},{32,48},{48,0},{1,17},{17,33},{33,49},{49,1},{2,18}... | collective-permute-start | bytes 589832 | tf_op jit(solution)/shard_map/ppermute | solution.py:49
  170.1 12.8 %collective-permute-start.17 = (bf16[64,1536]{1,0:T(8,128)(2,1)}, bf16[64,1536]{1,0:T(8,128)(2,1)S(1)}, u32[]{:S(2)}, u32[]{:S(2)}) collective-permute-start(bf16[64,1536]{1,0:T(8,128)(2,1)} %get-tuple-element.78), channel_id=1, source_target_pairs={{0,32},{16,48},{32,0},{48,16},{1,33},{17,49},{33,1},{49,17},{2,34}... | collective-permute-start | bytes 589832 | tf_op jit(solution)/shard_map/ppermute | solution.py:49
  172.8 10.1 %collective-permute-start.18 = (bf16[64,1536]{1,0:T(8,128)(2,1)}, bf16[64,1536]{1,0:T(8,128)(2,1)S(1)}, u32[]{:S(2)}, u32[]{:S(2)}) collective-permute-start(bf16[64,1536]{1,0:T(8,128)(2,1)} %get-tuple-element.79), channel_id=1, source_target_pairs={{0,48},{16,0},{32,16},{48,32},{1,49},{17,1},{33,17},{49,33},{2,50}... | collective-permute-start | bytes 589832 | tf_op jit(solution)/shard_map/ppermute | solution.py:49
  174.2 6.1 %collective-permute-start.11 = (bf16[64,768]{1,0:T(8,128)(2,1)S(1)}, bf16[64,768]{1,0:T(8,128)(2,1)S(1)}, u32[]{:S(2)}, u32[]{:S(2)}) collective-permute-start(bf16[64,768]{1,0:T(8,128)(2,1)S(1)} %copy-done.28), channel_id=1, source_target_pairs={{0,128},{64,192},{128,0},{192,64},{1,129},{65,193},{129,1},{193,65... | collective-permute-start | bytes 294920 | tf_op jit(solution)/shard_map/ppermute | solution.py:49
  176.9 5.9 %collective-permute-start.12 = (bf16[64,768]{1,0:T(8,128)(2,1)S(1)}, bf16[64,768]{1,0:T(8,128)(2,1)S(1)}, u32[]{:S(2)}, u32[]{:S(2)}) collective-permute-start(bf16[64,768]{1,0:T(8,128)(2,1)S(1)} %copy-done.27), channel_id=1, source_target_pairs={{0,192},{64,0},{128,64},{192,128},{1,193},{65,1},{129,65},{193,129... | collective-permute-start | bytes 294920 | tf_op jit(solution)/shard_map/ppermute | solution.py:49
  (30 other events, 172.1 us)

commit v3 on v2

--- a/solution.py
+++ b/solution.py
@@ -14,7 +14,7 @@
 F32 = jnp.float32
 STAT_ROWS = 16
 MIB = 1024 * 1024
-VMEM_BYTES = 56 * MIB
+VMEM_BYTES = 62 * MIB
 
 
 def dot(left, right, left_dim=1, right_dim=0):
@@ -96,8 +96,8 @@
     sig = jax.nn.sigmoid(gate)
     act = (gate * sig * up).astype(BF16)
     act_ref[...] = act
-    one_ref[...] = up * sig * (1.0 + gate * (1.0 - sig))
-    two_ref[...] = gate * sig
+    one_ref[...] = (up * sig * (1.0 + gate * (1.0 - sig))).astype(BF16)
+    two_ref[...] = (gate * sig).astype(BF16)
     part = dot(act, mix_ref[...])
 
     @pl.when(step == 0)
@@ -181,8 +181,8 @@
     @pl.when(pl.program_id(0) == 0)
     def _():
         act_grad = dot(grad_ref[...], mix_ref[...], 1, 1)
-        pair_ref[:, :ff] = (act_grad * one_ref[...]).astype(BF16)
-        pair_ref[:, ff:] = (act_grad * two_ref[...]).astype(BF16)
+        pair_ref[:, :ff] = (act_grad * one_ref[...].astype(F32)).astype(BF16)
+        pair_ref[:, ff:] = (act_grad * two_ref[...].astype(F32)).astype(BF16)
 
     input_ref[...] = (
         dot(pair_ref[:, :ff], gate_ref[...], 1, 1) + dot(pair_ref[:, ff:], up_ref[...], 1, 1)
@@ -190,20 +190,20 @@
 
 
 def far_kernel(
-    coord_ref, rows_x, rows_x2, resid_x, resid_x2, down_x, rows_y, rows_y2, value_y, pair_ref,
+    coord_ref, rows_x, rows_x2, resid_x, resid_x2, down_x, value_x, rows_y, rows_y2, value_y, pair_ref,
     grad_ref, grad2_ref, row_grad, row_grad2, mix_ref, one2_ref, two2_ref, act_ref, act2_ref,
     first_ref, second_ref, pair2_ref, inner_ref,
 ):
     ff = act_ref.shape[1]
     act_grad = dot(row_grad2[...], mix_ref[...], 1, 1)
-    pair2_ref[:, :ff] = (act_grad * one2_ref[...]).astype(BF16)
-    pair2_ref[:, ff:] = (act_grad * two2_ref[...]).astype(BF16)
+    pair2_ref[:, :ff] = (act_grad * one2_ref[...].astype(F32)).astype(BF16)
+    pair2_ref[:, ff:] = (act_grad * two2_ref[...].astype(F32)).astype(BF16)
     inner_ref[...] = (
         dot(act_ref[...], row_grad[...], 0, 0) + dot(act2_ref[...], row_grad2[...], 0, 0)
     ).astype(BF16)
     gates, ups = slice(None, ff), slice(ff, None)
     x_kernel(
-        1, coord_ref, rows_x, rows_x2, resid_x, resid_x2, down_x, pair_ref.at[:, gates],
+        1, coord_ref, rows_x, rows_x2, resid_x, resid_x2, down_x, value_x, pair_ref.at[:, gates],
         pair2_ref.at[:, gates], inner_ref, grad_ref, grad2_ref, first_ref,
     )
     y_kernel(
@@ -213,14 +213,14 @@
 
 
 def own_kernel(
-    coord_ref, rows_x, rows_x2, resid_x, resid_x2, down_x, rows_y, rows_y2, value_y, pair_ref,
-    pair2_ref, inner_ref, grad_ref, grad2_ref, token, first_ref, second_ref,
+    coord_ref, rows_x, rows_x2, resid_x, resid_x2, down_x, value_x, rows_y, rows_y2, value_y, pair_ref,
+    pair2_ref, inner_ref, grad_ref, grad2_ref, *refs,
 ):
-    del token
+    first_ref, second_ref = refs[-2:]
     ff = inner_ref.shape[0]
     gates, ups = slice(None, ff), slice(ff, None)
     x_kernel(
-        1, coord_ref, rows_x, rows_x2, resid_x, resid_x2, down_x, pair_ref.at[:, gates],
+        1, coord_ref, rows_x, rows_x2, resid_x, resid_x2, down_x, value_x, pair_ref.at[:, gates],
         pair2_ref.at[:, gates], inner_ref, grad_ref, grad2_ref, first_ref,
     )
     y_kernel(
@@ -247,15 +247,18 @@
 
 
 def x_kernel(
-    count, coord_ref, rows_x, rows_x2, resid_x, resid_x2, down_x, pair_ref, pair2_ref, inner_ref,
-    grad_ref, grad2_ref, *outs,
+    count, coord_ref, rows_x, rows_x2, resid_x, resid_x2, down_x, value_x, pair_ref, pair2_ref,
+    inner_ref, grad_ref, grad2_ref, *outs,
 ):
     del coord_ref
     outs = outs[-count:]
     write(outs, 0, dot(flat(rows_x), pair_ref[...]) + dot(flat(rows_x2), pair2_ref[...]))
+    ff = inner_ref.shape[0]
+    cut = ff // 6
+    write(outs, ff, dot(flat(value_x), inner_ref[:cut, :], 1, 1))
     write(
         outs,
-        pair_ref.shape[1],
+        ff + cut,
         dot(flat(resid_x), grad_ref[...])
         + dot(flat(resid_x2), grad2_ref[...])
         + dot(flat(down_x), inner_ref[...]),
@@ -268,39 +271,49 @@
     del coord_ref
     outs = outs[-count:]
     write(outs, 0, dot(flat(rows_y), pair_ref[...]) + dot(flat(rows_y2), pair2_ref[...]))
-    write(outs, pair_ref.shape[1], dot(flat(value_y), inner_ref[...], 1, 1))
+    ff = inner_ref.shape[0]
+    write(outs, ff, dot(flat(value_y), inner_ref[ff // 6 :, :], 1, 1))
+
+
+def pass_kernel(head_ref, token, out_ref):
+    del token
+    out_ref[...] = head_ref[...]
+
+
+def summed_at(refs, index, columns):
+    total = refs[0][index, :, columns].astype(F32)
+    for ref in refs[1:]:
+        total = total + ref[index, :, columns].astype(F32)
+    return total
 
 
 def first_kernel(coord_ref, *refs):
-    full, head_ref, outs = refs[-1], refs[-6], refs[-5:-1]
-    columns = outs[0].shape[1]
-    full[...] = summed(refs[:4])
-    head_ref[...] = full[:, :, columns:]
+    parts, (head_ref, *outs) = refs[:4], refs[-5:]
+    side, columns = len(outs), outs[0].shape[1]
+    for y in range(side):
+        head_ref[y] = summed_at(parts, y, slice(columns, None))
     for shift, out in enumerate(outs):
-        at = lax.rem(coord_ref[1] + shift, full.shape[0])
-        out[...] = full[at, :, :columns].astype(out.dtype)
+        y = lax.rem(coord_ref[1] + shift, side)
+        out[...] = summed_at(parts, y, slice(None, columns)).astype(out.dtype)
 
 
 def second_kernel(coord_ref, *refs):
-    full, outs = refs[-1], refs[-5:-1]
-    full[...] = summed(refs[:4])
+    parts, outs = refs[:4], refs[-4:]
     for shift, out in enumerate(outs):
-        out[...] = full[lax.rem(coord_ref[0] + shift, full.shape[0])].astype(out.dtype)
-
-
-def hidden_kernel(placed_ref, rows_ref, head_ref, out_ref, pass_ref):
-    out_ref[...] = dot(placed_ref[...], rows_ref[...], 0, 0).astype(BF16)
-    pass_ref[...] = head_ref[...]
+        x = lax.rem(coord_ref[0] + shift, len(outs))
+        out[...] = summed_at(parts, x, slice(None)).astype(out.dtype)
 
 
 def last_kernel(side_x, side_y, head_ref, *refs):
     firsts, seconds = refs[:side_y], refs[side_y : side_y + side_x]
     gate_ref, up_ref, down_ref, value_ref = refs[side_y + side_x :]
     ff = gate_ref.shape[1]
-    gate_ref[...] = summed(firsts)
-    second = summed(seconds)
+    first, second = summed(firsts), summed(seconds)
+    cut = first.shape[1] - ff
+    gate_ref[...] = first[:, :ff]
     up_ref[...] = second[:, :ff]
-    down_ref[...] = second[:, ff:]
+    down_ref[:, :cut] = first[:, ff:]
+    down_ref[:, cut:] = second[:, ff:]
     value_ref[...] = jnp.sum(head_ref[...], axis=0)
 
 
@@ -408,8 +421,8 @@
         ],
         out_shape=(
             sds((slot_total, ff), BF16),
-            sds((slot_total, ff), F32),
-            sds((slot_total, ff), F32),
+            sds((slot_total, ff), BF16),
+            sds((slot_total, ff), BF16),
             sds((groups, cap + STAT_ROWS, bins), BF16),
         ),
         scratch_shapes=[pltpu.VMEM((slot_total, bins), F32)],
@@ -491,7 +504,9 @@
     back_grad = exchange_rows(input_grad)
 
     half = width // 2
-    first_block, second_block = (side_y, own_rows, ff + bins), (side_x, own_rows, 2 * ff)
+    cut = ff // 6
+    first_columns, second_columns = ff + cut + bins, 2 * ff - cut
+    first_block, second_block = (side_y, own_rows, first_columns), (side_x, own_rows, second_columns)
 
     def parts(kernel, shifts, blocked, shared, outs, name):
         def shift_of(step):
@@ -533,7 +548,9 @@
         size = lax.axis_size(axis_name)
         return lax.ppermute(array, axis_name, [(k, (k + shift) % size) for k in range(size)])
 
-    x_rows = [("x", r) for r in (rows_mine, rows_peer, resid_mine, resid_peer, down_mine)]
+    x_rows = [
+        ("x", r) for r in (rows_mine, rows_peer, resid_mine, resid_peer, down_mine, value_mine)
+    ]
     y_rows = [("y", r) for r in (rows_mine, rows_peer, value_mine)]
     first_out, second_out = sds(first_block, BF16), sds(second_block, BF16)
     first_far, second_far, pair_peer, inner = parts(
@@ -567,35 +584,34 @@
         "x_near",
     )
     firsts += [step_on(first_up, "x", 1), step_on(first_down, "x", 3)]
+    second_up, second_down = parts(
+        lambda *refs: y_kernel(2, *refs),
+        (1, 3),
+        y_rows,
+        [
+            (up_spec, pair), (up_spec, pair_peer), (None, inner), (anywhere, first_up),
+        ],
+        [second_out] * 2,
+        "y_near",
+    )
     first_own, second_own = parts(
         own_kernel,
         (0,),
         x_rows + y_rows,
         [
             (None, pair), (None, pair_peer), (None, inner), (None, logit_grad), (None, grad_peer),
-            (anywhere, first_up),
+            (anywhere, second_up), (anywhere, seconds[0]), (anywhere, firsts[0]),
         ],
         [first_out, second_out],
         "own",
     )
-    second_up, second_down = parts(
-        lambda *refs: y_kernel(2, *refs),
-        (1, 3),
-        y_rows,
-        [
-            (up_spec, pair), (up_spec, pair_peer), (None, inner), (anywhere, seconds[0]),
-            (anywhere, second_own),
-        ],
-        [second_out] * 2,
-        "y_near",
-    )
     seconds += [step_on(second_up, "y", 1), step_on(second_down, "y", 3)]
 
     head, *firsts = pl.pallas_call(
         first_kernel,
         in_specs=[smem] + [vmem] * 4,
-        out_shape=(sds((side_y, own_rows, bins), F32),) + per_shift(side_y, (own_rows, ff)),
-        scratch_shapes=[pltpu.VMEM(first_block, F32)],
+        out_shape=(sds((side_y, own_rows, bins), F32),)
+        + per_shift(side_y, (own_rows, first_columns - bins)),
         compiler_params=params(),
         cost_estimate=cost(0, 12 * side_y * own_rows * ff),
         name="first",
@@ -604,20 +620,22 @@
     seconds = pl.pallas_call(
         second_kernel,
         in_specs=[smem] + [vmem] * 4,
-        out_shape=per_shift(side_x, (own_rows, 2 * ff)),
-        scratch_shapes=[pltpu.VMEM(second_block, F32)],
+        out_shape=per_shift(side_x, (own_rows, second_columns)),
         compiler_params=params(),
         cost_estimate=cost(0, 24 * side_y * own_rows * ff),
         name="second",
     )(coords, second_own, *seconds)
     second_came = send(seconds, "x")
-    grad_hidden, head = pl.pallas_call(
-        hidden_kernel,
-        out_shape=(sds((tok_rows, width), BF16), sds(head.shape, F32)),
-        compiler_params=params(),
-        cost_estimate=cost(2 * tok_rows * slot_total * width, 2 * width * (slot_total + tok_rows)),
-        name="hidden",
-    )(placed_any, back_grad, head)
+    with jax.named_scope("hidden"):
+        grad_hidden = dot(placed_any, back_grad, 0, 0).astype(BF16)
+    head = pl.pallas_call(
+        pass_kernel,
+        in_specs=[vmem, anywhere],
+        out_shape=sds(head.shape, F32),
+        compiler_params=params(),
+        cost_estimate=cost(0, 8 * side_y * own_rows * bins),
+        name="pass",
+    )(head, back_grad)
     shares = head.reshape(side_y * groups, own_rows // groups, bins)
     shares = lax.all_to_all(shares, ("y", "expert"), 0, 0, tiled=True)
     grad_gate, grad_up, grad_down, grad_value = pl.pallas_call(

time: 187 us -> 181 us (0.968)
  waiting for transfers between devices: 32.9 us -> 25.2 us
  starting transfers between devices: 47 us -> 51 us
  matrix products: 2.71 us -> 6.54 us
  local copies, waits for them, and re-layouts: 19.6 us -> 15.8 us
  Pallas kernels: 59.4 us -> 57.5 us
    dot_general x2 -> x3, matrix products: 2.71 us -> 6.54 us  [dot(): lax.dot_general(left, right, (((left_dim,), (right_dim,)), ((), ())), pre...]
    unnamed x64 -> x44, local copies, waits for them, and re-layouts: 14.4 us -> 10.6 us
    all_to_all x4, waiting for transfers between devices: 19 us -> 15.9 us  [exchange(): return lax.all_to_all(blocks, 'expert', 0, 0, tiled=True)]
    all_to_all x4, starting transfers between devices: 19.8 us -> 22.8 us  [exchange(): return lax.all_to_all(blocks, 'expert', 0, 0, tiled=True)]
    ppermute x6, waiting for transfers between devices: 5.79 us -> 2.92 us  [step_on(): lax.ppermute(array, axis_name, [(k, (k + shift) % size) for k in range(si...]
  transfers between devices with their start and end apart: 24 -> 24, of which waited for: 9 -> 9; matrix products, arithmetic and copies ran while one was open for 10% -> 11% of each run, Pallas kernels for 21% -> 21%
where the time goes in v3:
time: 181 us; the launch traced here: 180 us
  Pallas kernels  57.5 us (32%)
  starting transfers between devices  51 us (28%)
  waiting for transfers between devices  25.2 us (14%)
  blocking collectives  21 us (12%)
  local copies, waits for them, and re-layouts  15.8 us (9%)
  matrix products  6.54 us (4%)
  other arithmetic  2.58 us (1%)
    pallas_call x4, Pallas kernels, parts(): pl.pallas_call(kernel, grid_spec=pltpu.PrefetchScalarGridSpec(num_scalar_...  24.5 us
    all_to_all x4, starting transfers between devices, exchange(): return lax.all_to_all(blocks, 'expert', 0, 0, tiled=True)  22.8 us
    psum x3, blocking collectives, per_device(): sums = lax.psum(sums, axis_name)  21 us
    all_to_all x4, waiting for transfers between devices, exchange(): return lax.all_to_all(blocks, 'expert', 0, 0, tiled=True)  15.9 us
    unnamed x44, local copies, waits for them, and re-layouts  10.6 us
    all_to_all x1, starting transfers between devices, per_device(): shares = lax.all_to_all(shares, ('y', 'expert'), 0, 0, tiled=True)  9.89 us
    ppermute x6, starting transfers between devices, send(): lax.ppermute(arrays[shift], axis_name, [(k, (k + shift) % size) for k in...  8.49 us
    ppermute x6, starting transfers between devices, step_on(): lax.ppermute(array, axis_name, [(k, (k + shift) % size) for k in range(si...  8.47 us
  transfers between devices with their start and end apart: 24, of which 9 were waited for; matrix products, arithmetic and copies ran while one was open for 11% of the time, Pallas kernels for 21%

profile of v3, /device:TPU:24, one launch (start us, length us, event | category | flops | bytes accessed | tf_op | source)
XLA Modules:
  0.0 180.4 jit_solution(7031992982109939704)
XLA Ops:
  0.6 3.1 %slots.1 = (bf16[384,2048]{1,0:T(8,128)(2,1)}, s32[2,128]{1,0:T(2,128)}, bf16[384,128]{1,0:T(8,128)(2,1)}) custom-call(s32[2,128]{1,0:T(2,128)} %bitcast.106, bf16[128,2048]{1,0:T(8,128)(2,1)} %refs_1_.1), custom_call_target="tpu_custom_call" | custom-call | flops 201326592 | bytes 2097152 | tf_op jit(solution)/shard_map/slots/pallas_call | solution.py:377
  3.7 8.6 %all-to-all-start = ((bf16[8,48,2048]{2,1,0:T(8,128)(2,1)}), bf16[8,48,2048]{2,1,0:T(8,128)(2,1)}, u32[]{:S(2)}, u32[]{:S(2)}) async-start(bf16[8,48,2048]{2,1,0:T(8,128)(2,1)} %bitcast.98), calls=%async_computation | async-start | bytes 3145728 | tf_op jit(solution)/shard_map/all_to_all | solution.py:372
  14.3 10.5 %psum.21 = f32[2]{0:T(128)S(1)} all-reduce(f32[2]{0:T(128)S(1)} %pad_maximum_fusion), channel_id=1, replica_groups=mesh['y'=4,'x'=4,'core'=2,'expert'=8] {'x'}, use_global_device_ids=true, to_apply=%region_2.0 | all-reduce | flops 2 | bytes 16 | tf_op jit(solution)/shard_map/moments/psum | solution.py:393
  24.7 7.5 %psum.22 = f32[2]{0:T(128)S(1)} all-reduce(f32[2]{0:T(128)S(1)} %psum.21), channel_id=1, replica_groups=mesh['y'=4,'x'=4,'core'=2,'expert'=8] {'y'}, use_global_device_ids=true, to_apply=%region_3.0 | all-reduce | flops 2 | bytes 16 | tf_op jit(solution)/shard_map/moments/psum | solution.py:393
  33.2 3.1 %psum.23.refs_4_ = f32[2]{0:T(128)} all-reduce(f32[2]{0:T(128)S(1)} %psum.22), channel_id=1, replica_groups=mesh['y'=4,'x'=4,'core'=2,'expert'=8] {'core'}, use_global_device_ids=true, to_apply=%region_4.0 | all-reduce | flops 2 | bytes 16 | tf_op jit(solution)/shard_map/moments/psum | solution.py:393
  36.4 4.7 %copy.23 = bf16[1,768,2048]{1,2,0:T(8,128)(2,1)} copy(bf16[1,768,2048]{2,1,0:T(8,128)(2,1)} %param.18) | data formatting | bytes 6291456 | tf_op args[8]
  41.9 2.9 %constant_dynamic-slice_fusion.2 = bf16[16,1,64,768]{3,2,1,0:T(8,128)(2,1)} fusion(bf16[16,2,64,768]{3,2,1,0:T(8,128)(2,1)} %bitcast.85, s32[]{:T(128)S(6)} %select_n.11), kind=kLoop, calls=%fused_computation.6 | loop fusion | bytes 3145732 | tf_op jit(solution)/shard_map/weights_only/jit(dynamic_index_in_dim)/dynamic_slice | solution.py:39
  46.5 5.9 %all-to-all-done = bf16[8,48,2048]{2,1,0:T(8,128)(2,1)} async-done(((bf16[8,48,2048]{2,1,0:T(8,128)(2,1)}), bf16[8,48,2048]{2,1,0:T(8,128)(2,1)}, u32[]{:S(2)}, u32[]{:S(2)}) %all-to-all-start) | async-done | bytes 1572896 | tf_op jit(solution)/shard_map/all_to_all | solution.py:372
  52.4 7.5 %front.1 = (bf16[384,768]{1,0:T(8,128)(2,1)}, bf16[384,768]{1,0:T(8,128)(2,1)}, bf16[384,768]{1,0:T(8,128)(2,1)}, bf16[8,64,256]{2,1,0:T(8,128)(2,1)}) custom-call(bf16[384,2048]{1,0:T(8,128)(2,1)} %bitcast.2.refs_0_.rows_ref, bf16[2048,768]{1,0:T(8,128)(2,1)} %bitcast.81, bf16[2048,768]{1,0:T(8,128)(2,1)} %bitcast.83, ...), custom_call_target="tpu_custom_call" | custom-call | flops 2415919104 | bytes 6291456 | tf_op jit(solution)/shard_map/front/pallas_call | solution.py:405
  59.9 4.2 %all-to-all-start.1 = ((bf16[8,64,256]{2,1,0:T(8,128)(2,1)}), bf16[8,64,256]{2,1,0:T(8,128)(2,1)}, u32[]{:S(2)}, u32[]{:S(2)}) async-start(bf16[8,64,256]{2,1,0:T(8,128)(2,1)} %get-tuple-element.45), calls=%async_computation.1 | async-start | bytes 524288 | tf_op jit(solution)/shard_map/all_to_all | solution.py:372
  64.0 3.9 %turn.1 = (bf16[16,64,384]{2,1,0:T(8,128)(2,1)}, bf16[16,64,384]{2,1,0:T(8,128)(2,1)}) custom-call(s32[1]{0:T(128)} %bitcast.19.core_ref, bf16[384,2048]{1,0:T(8,128)(2,1)} %bitcast.2.refs_0_.rows_ref, bf16[384,768]{1,0:T(8,128)(2,1)} %get-tuple-element.47.token.act_ref), custom_call_target="tpu_custom_call" | custom-call | bytes 3145728 | tf_op jit(solution)/shard_map/turned/turn/pallas_call | solution.py:436
  77.0 5.6 %all-to-all-start.2 = ((bf16[8,48,256]{2,1,0:T(8,128)(2,1)}), bf16[8,48,256]{2,1,0:T(8,128)(2,1)S(1)}, u32[]{:S(2)}, u32[]{:S(2)}) async-start(bf16[8,48,256]{2,1,0:T(8,128)(2,1)} %bitcast.101), calls=%async_computation.2 | async-start | bytes 393216 | tf_op jit(solution)/shard_map/all_to_all | solution.py:372
  84.8 8.5 %all-to-all-done.2 = bf16[8,48,256]{2,1,0:T(8,128)(2,1)S(1)} async-done(((bf16[8,48,256]{2,1,0:T(8,128)(2,1)}), bf16[8,48,256]{2,1,0:T(8,128)(2,1)S(1)}, u32[]{:S(2)}, u32[]{:S(2)}) %all-to-all-start.2) | async-done | bytes 196640 | tf_op jit(solution)/shard_map/all_to_all | solution.py:372
  94.0 6.5 %back.1 = (bf16[384,2048]{1,0:T(8,128)(2,1)}, bf16[384,1536]{1,0:T(8,128)(2,1)}) custom-call(bf16[384,256]{1,0:T(8,128)(2,1)} %bitcast.94, bf16[768,256]{1,0:T(8,128)(2,1)} %fusion.2.refs_3_.mix_ref, bf16[384,768]{1,0:T(8,128)(2,1)} %get-tuple-element.51.one_ref, bf16[384,768]{1,0:T(8,128)(2,1)} %get-tuple-element.52.two_ref, bf16[2048,768]{1,0:T(8,128)(2,1)} %bitcast.82, ...), custom_call_target="tpu_custom_call" | custom-call | flops 2415919104 | bytes 6291456 | tf_op jit(solution)/shard_map/back/pallas_call | solution.py:478
  100.5 4.4 %all-to-all-start.3 = ((bf16[8,48,2048]{2,1,0:T(8,128)(2,1)}), bf16[8,48,2048]{2,1,0:T(8,128)(2,1)}, u32[]{:S(2)}, u32[]{:S(2)}) async-start(bf16[8,48,2048]{2,1,0:T(8,128)(2,1)} %bitcast.97), calls=%async_computation.3 | async-start | bytes 3145728 | tf_op jit(solution)/shard_map/all_to_all | solution.py:372
  107.4 6.8 %far.1 = (bf16[4,64,1152]{2,1,0:T(8,128)(2,1)}, bf16[4,64,1408]{2,1,0:T(8,128)(2,1)}, bf16[384,1536]{1,0:T(8,128)(2,1)}, bf16[768,256]{1,0:T(8,128)(2,1)}) custom-call(s32[2]{0:T(128)} %pad_add_fusion.refs_8_.coord_ref.refs_0_, bf16[4,4,64,384]{3,2,1,0:T(8,128)(2,1)} %bitcast.61, bf16[4,4,64,384]{3,2,1,0:T(8,128)(2,1)} %bitcast.68, ...), custom_call_target="tpu_custom_call" | custom-call | flops 301989888 | bytes 3145728 | tf_op jit(solution)/shard_map/far/pallas_call | solution.py:528
  114.2 3.0 %collective-permute-start.8 = (bf16[4,64,1152]{2,1,0:T(8,128)(2,1)}, bf16[4,64,1152]{2,1,0:T(8,128)(2,1)}, u32[]{:S(2)}, u32[]{:S(2)}) collective-permute-start(bf16[4,64,1152]{2,1,0:T(8,128)(2,1)} %get-tuple-element.62), channel_id=1, source_target_pairs={{0,32},{16,48},{32,0},{48,16},{1,33},{17,49},{33,1},{49,17},{2,34}... | collective-permute-start | bytes 1769480 | tf_op jit(solution)/shard_map/ppermute | solution.py:549
  118.4 6.7 %x_near.1 = (bf16[4,64,1152]{2,1,0:T(8,128)(2,1)}, bf16[4,64,1152]{2,1,0:T(8,128)(2,1)}) custom-call(s32[2]{0:T(128)} %pad_add_fusion.refs_8_.coord_ref.refs_0_, bf16[4,4,64,384]{3,2,1,0:T(8,128)(2,1)} %bitcast.63, bf16[4,4,64,384]{3,2,1,0:T(8,128)(2,1)} %bitcast.70, bf16[4,4,64,128]{3,2,1,0:T(8,128)(2,1)} %bitcast.88, bf16[4,4,64,128]{3,2,1,0:T(8,128)(2,1)} %bitcast.91, ...), custom_call_target="tpu_custom_call" | custom-call | flops 603979776 | bytes 6291456 | tf_op jit(solution)/shard_map/x_near/pallas_call | solution.py:528
  127.1 5.8 %y_near.1 = (bf16[4,64,1408]{2,1,0:T(8,128)(2,1)}, bf16[4,64,1408]{2,1,0:T(8,128)(2,1)}) custom-call(s32[2]{0:T(128)} %pad_add_fusion.refs_8_.coord_ref.refs_0_, bf16[4,4,64,384]{3,2,1,0:T(8,128)(2,1)} %bitcast.64, bf16[4,4,64,384]{3,2,1,0:T(8,128)(2,1)} %bitcast.71, bf16[4,4,64,256]{3,2,1,0:T(8,128)(2,1)} %bitcast.78, ...), custom_call_target="tpu_custom_call" | custom-call | flops 603979776 | bytes 6291456 | tf_op jit(solution)/shard_map/y_near/pallas_call | solution.py:528
  137.7 5.2 %own.1 = (bf16[4,64,1152]{2,1,0:T(8,128)(2,1)}, bf16[4,64,1408]{2,1,0:T(8,128)(2,1)}) custom-call(s32[2]{0:T(128)} %pad_add_fusion.refs_8_.coord_ref.refs_0_, bf16[4,4,64,384]{3,2,1,0:T(8,128)(2,1)} %bitcast.65, bf16[4,4,64,384]{3,2,1,0:T(8,128)(2,1)} %bitcast.72, bf16[4,4,64,128]{3,2,1,0:T(8,128)(2,1)} %bitcast.89, bf16[4,4,64,128]{3,2,1,0:T(8,128)(2,1)} %bitcast.92, ...), custom_call_target="tpu_custom_call" | custom-call | flops 301989888 | bytes 3145728 | tf_op jit(solution)/shard_map/own/pallas_call | solution.py:528
  148.5 9.9 %all-to-all-start.4 = ((f32[32,8,256]{2,1,0:T(8,128)}), f32[32,8,256]{2,1,0:T(8,128)S(1)}, u32[]{:S(2)}, u32[]{:S(2)}) async-start(f32[32,8,256]{2,1,0:T(8,128)} %bitcast.99), calls=%async_computation.4 | async-start | bytes 524288 | tf_op jit(solution)/shard_map/all_to_all | solution.py:640
  159.3 2.9 %second.1 = (f32[64,1408]{1,0:T(8,128)}, bf16[64,1408]{1,0:T(8,128)(2,1)}, bf16[64,1408]{1,0:T(8,128)(2,1)}, bf16[64,1408]{1,0:T(8,128)(2,1)}) custom-call(s32[2]{0:T(128)} %pad_add_fusion.refs_8_.coord_ref.refs_0_, bf16[4,64,1408]{2,1,0:T(8,128)(2,1)} %get-tuple-element.70.refs_0_, bf16[4,64,1408]{2,1,0:T(8,128)(2,1)} %copy-done.4, ...), custom_call_target="tpu_custom_call" | custom-call | bytes 4718592 | tf_op jit(solution)/shard_map/second/pallas_call | solution.py:620
  167.6 2.7 %collective-permute-start.12 = (bf16[64,896]{1,0:T(8,128)(2,1)}, bf16[64,896]{1,0:T(8,128)(2,1)S(1)}, u32[]{:S(2)}, u32[]{:S(2)}) collective-permute-start(bf16[64,896]{1,0:T(8,128)(2,1)} %get-tuple-element.68), channel_id=1, source_target_pairs={{0,128},{64,192},{128,0},{192,64},{1,129},{65,193},{129,1},{193,65... | collective-permute-start | bytes 344072 | tf_op jit(solution)/shard_map/ppermute | solution.py:49
  170.4 2.8 %convolution_convert_fusion = bf16[128,2048]{1,0:T(8,128)(2,1)} fusion(bf16[384,128]{1,0:T(8,128)(2,1)} %get-tuple-element.43, bf16[384,2048]{1,0:T(8,128)(2,1)} %bitcast.27.token), kind=kOutput, calls=%fused_computation.2 | convolution fusion | flops 201588736 | bytes 2195456 | tf_op jit(solution)/shard_map/hidden/dot_general | solution.py:21
  (94 shorter events, 47.0 us)
Async XLA Ops:
  3.7 48.7 %all-to-all-start = ((bf16[8,48,2048]{2,1,0:T(8,128)(2,1)}), bf16[8,48,2048]{2,1,0:T(8,128)(2,1)}, u32[]{:S(2)}, u32[]{:S(2)}) async-start(bf16[8,48,2048]{2,1,0:T(8,128)(2,1)} %bitcast.98), calls=%async_computation | async-start | bytes 3145728 | tf_op jit(solution)/shard_map/all_to_all | solution.py:372
  33.2 13.2 %collective-permute-start = (bf16[1024,128]{1,0:T(8,128)(2,1)S(1)}, bf16[1024,128]{1,0:T(8,128)(2,1)S(1)}, u32[]{:S(2)}, u32[]{:S(2)}) collective-permute-start(bf16[1024,128]{1,0:T(8,128)(2,1)S(1)} %bitcast.100), channel_id=1, source_target_pairs={{0,8},{8,0},{1,9},{9,1},{2,10},{10,2},{3,11},{11,3},{4,12},{12,4},... | collective-permute-start | bytes 786440 | tf_op jit(solution)/shard_map/weights_only/ppermute | solution.py:43
  59.9 14.7 %all-to-all-start.1 = ((bf16[8,64,256]{2,1,0:T(8,128)(2,1)}), bf16[8,64,256]{2,1,0:T(8,128)(2,1)}, u32[]{:S(2)}, u32[]{:S(2)}) async-start(bf16[8,64,256]{2,1,0:T(8,128)(2,1)} %get-tuple-element.45), calls=%async_computation.1 | async-start | bytes 524288 | tf_op jit(solution)/shard_map/all_to_all | solution.py:372
  68.0 16.8 %collective-permute-start.1 = (bf16[16,64,384]{2,1,0:T(8,128)(2,1)}, bf16[16,64,384]{2,1,0:T(8,128)(2,1)S(1)}, u32[]{:S(2)}, u32[]{:S(2)}) collective-permute-start(bf16[16,64,384]{2,1,0:T(8,128)(2,1)} %get-tuple-element.49.refs_7_), channel_id=1, source_target_pairs={{0,8},{8,0},{1,9},{9,1},{2,10},{10,2},{3,11},{11,3},{4,12},{12,4},... | collective-permute-start | bytes 2359304 | tf_op jit(solution)/shard_map/turned/ppermute | solution.py:43
  70.1 14.1 %collective-permute-start.3 = (bf16[384,768]{1,0:T(8,128)(2,1)}, bf16[384,768]{1,0:T(8,128)(2,1)}, u32[]{:S(2)}, u32[]{:S(2)}) collective-permute-start(bf16[384,768]{1,0:T(8,128)(2,1)} %get-tuple-element.47.token.act_ref), channel_id=1, source_target_pairs={{0,8},{8,0},{1,9},{9,1},{2,10},{10,2},{3,11},{11,3},{4,12},{12,4},... | collective-permute-start | bytes 1769480 | tf_op jit(solution)/shard_map/turned/ppermute | solution.py:43
  70.6 13.6 %collective-permute-start.4 = (bf16[384,768]{1,0:T(8,128)(2,1)}, bf16[384,768]{1,0:T(8,128)(2,1)}, u32[]{:S(2)}, u32[]{:S(2)}) collective-permute-start(bf16[384,768]{1,0:T(8,128)(2,1)} %get-tuple-element.51.one_ref), channel_id=1, source_target_pairs={{0,8},{8,0},{1,9},{9,1},{2,10},{10,2},{3,11},{11,3},{4,12},{12,4},... | collective-permute-start | bytes 1769480 | tf_op jit(solution)/shard_map/turned/ppermute | solution.py:43
  70.6 13.6 %collective-permute-start.5 = (bf16[384,768]{1,0:T(8,128)(2,1)}, bf16[384,768]{1,0:T(8,128)(2,1)}, u32[]{:S(2)}, u32[]{:S(2)}) collective-permute-start(bf16[384,768]{1,0:T(8,128)(2,1)} %get-tuple-element.52.two_ref), channel_id=1, source_target_pairs={{0,8},{8,0},{1,9},{9,1},{2,10},{10,2},{3,11},{11,3},{4,12},{12,4},... | collective-permute-start | bytes 1769480 | tf_op jit(solution)/shard_map/turned/ppermute | solution.py:43
  77.0 16.3 %all-to-all-start.2 = ((bf16[8,48,256]{2,1,0:T(8,128)(2,1)}), bf16[8,48,256]{2,1,0:T(8,128)(2,1)S(1)}, u32[]{:S(2)}, u32[]{:S(2)}) async-start(bf16[8,48,256]{2,1,0:T(8,128)(2,1)} %bitcast.101), calls=%async_computation.2 | async-start | bytes 393216 | tf_op jit(solution)/shard_map/all_to_all | solution.py:372
  82.7 1.5 collective-permute-start.2
  100.5 46.2 %all-to-all-start.3 = ((bf16[8,48,2048]{2,1,0:T(8,128)(2,1)}), bf16[8,48,2048]{2,1,0:T(8,128)(2,1)}, u32[]{:S(2)}, u32[]{:S(2)}) async-start(bf16[8,48,2048]{2,1,0:T(8,128)(2,1)} %bitcast.97), calls=%async_computation.3 | async-start | bytes 3145728 | tf_op jit(solution)/shard_map/all_to_all | solution.py:372
  105.0 1.7 collective-permute-start.6
  114.2 20.9 %collective-permute-start.8 = (bf16[4,64,1152]{2,1,0:T(8,128)(2,1)}, bf16[4,64,1152]{2,1,0:T(8,128)(2,1)}, u32[]{:S(2)}, u32[]{:S(2)}) collective-permute-start(bf16[4,64,1152]{2,1,0:T(8,128)(2,1)} %get-tuple-element.62), channel_id=1, source_target_pairs={{0,32},{16,48},{32,0},{48,16},{1,33},{17,49},{33,1},{49,17},{2,34}... | collective-permute-start | bytes 1769480 | tf_op jit(solution)/shard_map/ppermute | solution.py:549
  117.2 19.6 %collective-permute-start.7 = (bf16[4,64,1408]{2,1,0:T(8,128)(2,1)}, bf16[4,64,1408]{2,1,0:T(8,128)(2,1)S(1)}, u32[]{:S(2)}, u32[]{:S(2)}) collective-permute-start(bf16[4,64,1408]{2,1,0:T(8,128)(2,1)} %get-tuple-element.61), channel_id=1, source_target_pairs={{0,128},{64,192},{128,0},{192,64},{1,129},{65,193},{129,1},{193,65... | collective-permute-start | bytes 2162696 | tf_op jit(solution)/shard_map/ppermute | solution.py:549
  125.1 19.0 %collective-permute-start.10 = (bf16[4,64,1152]{2,1,0:T(8,128)(2,1)}, bf16[4,64,1152]{2,1,0:T(8,128)(2,1)}, u32[]{:S(2)}, u32[]{:S(2)}) collective-permute-start(bf16[4,64,1152]{2,1,0:T(8,128)(2,1)} %get-tuple-element.64), channel_id=1, source_target_pairs={{0,48},{16,0},{32,16},{48,32},{1,49},{17,1},{33,17},{49,33},{2,50}... | collective-permute-start | bytes 1769480 | tf_op jit(solution)/shard_map/ppermute | solution.py:549
  126.3 17.9 %collective-permute-start.9 = (bf16[4,64,1152]{2,1,0:T(8,128)(2,1)}, bf16[4,64,1152]{2,1,0:T(8,128)(2,1)}, u32[]{:S(2)}, u32[]{:S(2)}) collective-permute-start(bf16[4,64,1152]{2,1,0:T(8,128)(2,1)} %get-tuple-element.59.refs_7_), channel_id=1, source_target_pairs={{0,16},{16,32},{32,48},{48,0},{1,17},{17,33},{33,49},{49,1},{2,18}... | collective-permute-start | bytes 1769480 | tf_op jit(solution)/shard_map/ppermute | solution.py:549
  132.9 26.3 %collective-permute-start.14 = (bf16[4,64,1408]{2,1,0:T(8,128)(2,1)}, bf16[4,64,1408]{2,1,0:T(8,128)(2,1)}, u32[]{:S(2)}, u32[]{:S(2)}) collective-permute-start(bf16[4,64,1408]{2,1,0:T(8,128)(2,1)} %get-tuple-element.60.refs_0_), channel_id=1, source_target_pairs={{0,64},{64,128},{128,192},{192,0},{1,65},{65,129},{129,193},{193,1... | collective-permute-start | bytes 2162696 | tf_op jit(solution)/shard_map/ppermute | solution.py:549
  135.1 24.1 %collective-permute-start.15 = (bf16[4,64,1408]{2,1,0:T(8,128)(2,1)}, bf16[4,64,1408]{2,1,0:T(8,128)(2,1)}, u32[]{:S(2)}, u32[]{:S(2)}) collective-permute-start(bf16[4,64,1408]{2,1,0:T(8,128)(2,1)} %get-tuple-element.71), channel_id=1, source_target_pairs={{0,192},{64,0},{128,64},{192,128},{1,193},{65,1},{129,65},{193,129... | collective-permute-start | bytes 2162696 | tf_op jit(solution)/shard_map/ppermute | solution.py:549
  148.5 28.8 %all-to-all-start.4 = ((f32[32,8,256]{2,1,0:T(8,128)}), f32[32,8,256]{2,1,0:T(8,128)S(1)}, u32[]{:S(2)}, u32[]{:S(2)}) async-start(f32[32,8,256]{2,1,0:T(8,128)} %bitcast.99), calls=%async_computation.4 | async-start | bytes 524288 | tf_op jit(solution)/shard_map/all_to_all | solution.py:640
  158.3 12.0 %collective-permute-start.11 = (bf16[64,896]{1,0:T(8,128)(2,1)}, bf16[64,896]{1,0:T(8,128)(2,1)S(1)}, u32[]{:S(2)}, u32[]{:S(2)}) collective-permute-start(bf16[64,896]{1,0:T(8,128)(2,1)} %get-tuple-element.67), channel_id=1, source_target_pairs={{0,64},{64,128},{128,192},{192,0},{1,65},{65,129},{129,193},{193,1... | collective-permute-start | bytes 344072 | tf_op jit(solution)/shard_map/ppermute | solution.py:49
  162.1 14.4 %collective-permute-start.16 = (bf16[64,1408]{1,0:T(8,128)(2,1)}, bf16[64,1408]{1,0:T(8,128)(2,1)S(1)}, u32[]{:S(2)}, u32[]{:S(2)}) collective-permute-start(bf16[64,1408]{1,0:T(8,128)(2,1)} %get-tuple-element.73), channel_id=1, source_target_pairs={{0,16},{16,32},{32,48},{48,0},{1,17},{17,33},{33,49},{49,1},{2,18}... | collective-permute-start | bytes 540680 | tf_op jit(solution)/shard_map/ppermute | solution.py:49
  163.5 13.0 %collective-permute-start.17 = (bf16[64,1408]{1,0:T(8,128)(2,1)}, bf16[64,1408]{1,0:T(8,128)(2,1)S(1)}, u32[]{:S(2)}, u32[]{:S(2)}) collective-permute-start(bf16[64,1408]{1,0:T(8,128)(2,1)} %get-tuple-element.74), channel_id=1, source_target_pairs={{0,32},{16,48},{32,0},{48,16},{1,33},{17,49},{33,1},{49,17},{2,34}... | collective-permute-start | bytes 540680 | tf_op jit(solution)/shard_map/ppermute | solution.py:49
  166.2 11.0 %collective-permute-start.18 = (bf16[64,1408]{1,0:T(8,128)(2,1)}, bf16[64,1408]{1,0:T(8,128)(2,1)S(1)}, u32[]{:S(2)}, u32[]{:S(2)}) collective-permute-start(bf16[64,1408]{1,0:T(8,128)(2,1)} %get-tuple-element.75), channel_id=1, source_target_pairs={{0,48},{16,0},{32,16},{48,32},{1,49},{17,1},{33,17},{49,33},{2,50}... | collective-permute-start | bytes 540680 | tf_op jit(solution)/shard_map/ppermute | solution.py:49
  167.6 7.3 %collective-permute-start.12 = (bf16[64,896]{1,0:T(8,128)(2,1)}, bf16[64,896]{1,0:T(8,128)(2,1)S(1)}, u32[]{:S(2)}, u32[]{:S(2)}) collective-permute-start(bf16[64,896]{1,0:T(8,128)(2,1)} %get-tuple-element.68), channel_id=1, source_target_pairs={{0,128},{64,192},{128,0},{192,64},{1,129},{65,193},{129,1},{193,65... | collective-permute-start | bytes 344072 | tf_op jit(solution)/shard_map/ppermute | solution.py:49
  170.3 6.2 %collective-permute-start.13 = (bf16[64,896]{1,0:T(8,128)(2,1)}, bf16[64,896]{1,0:T(8,128)(2,1)S(1)}, u32[]{:S(2)}, u32[]{:S(2)}) collective-permute-start(bf16[64,896]{1,0:T(8,128)(2,1)} %get-tuple-element.69), channel_id=1, source_target_pairs={{0,192},{64,0},{128,64},{192,128},{1,193},{65,1},{129,65},{193,129... | collective-permute-start | bytes 344072 | tf_op jit(solution)/shard_map/ppermute | solution.py:49
  (20 other events, 134.3 us)

commit v4 on v3

--- a/solution.py
+++ b/solution.py
@@ -276,8 +276,7 @@
 
 
 def pass_kernel(head_ref, token, out_ref):
-    del token
-    out_ref[...] = head_ref[...]
+    del head_ref, token, out_ref
 
 
 def summed_at(refs, index, columns):
@@ -630,8 +629,10 @@
         grad_hidden = dot(placed_any, back_grad, 0, 0).astype(BF16)
     head = pl.pallas_call(
         pass_kernel,
-        in_specs=[vmem, anywhere],
+        in_specs=[anywhere] * 2,
+        out_specs=anywhere,
         out_shape=sds(head.shape, F32),
+        input_output_aliases={0: 0},
         compiler_params=params(),
         cost_estimate=cost(0, 8 * side_y * own_rows * bins),
         name="pass",

time: 181 us -> 180 us (level)
  transfers between devices with their start and end apart: 24 -> 24, of which waited for: 9 -> 9; matrix products, arithmetic and copies ran while one was open for 11% -> 12% of each run, Pallas kernels for 21% -> 20%
where the time goes in v4:
time: 180 us; the launch traced here: 179 us
  Pallas kernels  55.8 us (31%)
  starting transfers between devices  51.1 us (28%)
  waiting for transfers between devices  25.2 us (14%)
  blocking collectives  21 us (12%)
  local copies, waits for them, and re-layouts  15.8 us (9%)
  matrix products  6.54 us (4%)
  other arithmetic  2.58 us (1%)
    pallas_call x4, Pallas kernels, parts(): pl.pallas_call(kernel, grid_spec=pltpu.PrefetchScalarGridSpec(num_scalar_...  24.5 us
    all_to_all x4, starting transfers between devices, exchange(): return lax.all_to_all(blocks, 'expert', 0, 0, tiled=True)  22.8 us
    psum x3, blocking collectives, per_device(): sums = lax.psum(sums, axis_name)  21 us
    all_to_all x4, waiting for transfers between devices, exchange(): return lax.all_to_all(blocks, 'expert', 0, 0, tiled=True)  15.9 us
    unnamed x44, local copies, waits for them, and re-layouts  10.6 us
    all_to_all x1, starting transfers between devices, per_device(): shares = lax.all_to_all(shares, ('y', 'expert'), 0, 0, tiled=True)  10 us
    ppermute x6, starting transfers between devices, send(): lax.ppermute(arrays[shift], axis_name, [(k, (k + shift) % size) for k in...  8.49 us
    ppermute x6, starting transfers between devices, step_on(): lax.ppermute(array, axis_name, [(k, (k + shift) % size) for k in range(si...  8.47 us
  transfers between devices with their start and end apart: 24, of which 9 were waited for; matrix products, arithmetic and copies ran while one was open for 12% of the time, Pallas kernels for 20%

profile of v4, /device:TPU:24, one launch (start us, length us, event | category | flops | bytes accessed | tf_op | source)
XLA Modules:
  0.0 178.8 jit_solution(16729604017815833011)
XLA Ops:
  0.6 3.1 %slots.1 = (bf16[384,2048]{1,0:T(8,128)(2,1)}, s32[2,128]{1,0:T(2,128)}, bf16[384,128]{1,0:T(8,128)(2,1)}) custom-call(s32[2,128]{1,0:T(2,128)} %bitcast.106, bf16[128,2048]{1,0:T(8,128)(2,1)} %refs_1_.1), custom_call_target="tpu_custom_call" | custom-call | flops 201326592 | bytes 2097152 | tf_op jit(solution)/shard_map/slots/pallas_call | solution.py:376
  3.7 8.6 %all-to-all-start = ((bf16[8,48,2048]{2,1,0:T(8,128)(2,1)}), bf16[8,48,2048]{2,1,0:T(8,128)(2,1)}, u32[]{:S(2)}, u32[]{:S(2)}) async-start(bf16[8,48,2048]{2,1,0:T(8,128)(2,1)} %bitcast.98), calls=%async_computation | async-start | bytes 3145728 | tf_op jit(solution)/shard_map/all_to_all | solution.py:371
  14.3 10.5 %psum.21 = f32[2]{0:T(128)S(1)} all-reduce(f32[2]{0:T(128)S(1)} %pad_maximum_fusion), channel_id=1, replica_groups=mesh['y'=4,'x'=4,'core'=2,'expert'=8] {'x'}, use_global_device_ids=true, to_apply=%region_2.0 | all-reduce | flops 2 | bytes 16 | tf_op jit(solution)/shard_map/moments/psum | solution.py:392
  24.7 7.5 %psum.22 = f32[2]{0:T(128)S(1)} all-reduce(f32[2]{0:T(128)S(1)} %psum.21), channel_id=1, replica_groups=mesh['y'=4,'x'=4,'core'=2,'expert'=8] {'y'}, use_global_device_ids=true, to_apply=%region_3.0 | all-reduce | flops 2 | bytes 16 | tf_op jit(solution)/shard_map/moments/psum | solution.py:392
  33.2 3.1 %psum.23.refs_4_ = f32[2]{0:T(128)} all-reduce(f32[2]{0:T(128)S(1)} %psum.22), channel_id=1, replica_groups=mesh['y'=4,'x'=4,'core'=2,'expert'=8] {'core'}, use_global_device_ids=true, to_apply=%region_4.0 | all-reduce | flops 2 | bytes 16 | tf_op jit(solution)/shard_map/moments/psum | solution.py:392
  36.4 4.7 %copy.24 = bf16[1,768,2048]{1,2,0:T(8,128)(2,1)} copy(bf16[1,768,2048]{2,1,0:T(8,128)(2,1)} %param.18) | data formatting | bytes 6291456 | tf_op args[8]
  41.9 2.9 %constant_dynamic-slice_fusion.2 = bf16[16,1,64,768]{3,2,1,0:T(8,128)(2,1)} fusion(bf16[16,2,64,768]{3,2,1,0:T(8,128)(2,1)} %bitcast.85, s32[]{:T(128)S(6)} %select_n.11), kind=kLoop, calls=%fused_computation.6 | loop fusion | bytes 3145732 | tf_op jit(solution)/shard_map/weights_only/jit(dynamic_index_in_dim)/dynamic_slice | solution.py:39
  46.5 5.9 %all-to-all-done = bf16[8,48,2048]{2,1,0:T(8,128)(2,1)} async-done(((bf16[8,48,2048]{2,1,0:T(8,128)(2,1)}), bf16[8,48,2048]{2,1,0:T(8,128)(2,1)}, u32[]{:S(2)}, u32[]{:S(2)}) %all-to-all-start) | async-done | bytes 1572896 | tf_op jit(solution)/shard_map/all_to_all | solution.py:371
  52.4 7.5 %front.1 = (bf16[384,768]{1,0:T(8,128)(2,1)}, bf16[384,768]{1,0:T(8,128)(2,1)}, bf16[384,768]{1,0:T(8,128)(2,1)}, bf16[8,64,256]{2,1,0:T(8,128)(2,1)}) custom-call(bf16[384,2048]{1,0:T(8,128)(2,1)} %bitcast.2.refs_0_.rows_ref, bf16[2048,768]{1,0:T(8,128)(2,1)} %bitcast.81, bf16[2048,768]{1,0:T(8,128)(2,1)} %bitcast.83, ...), custom_call_target="tpu_custom_call" | custom-call | flops 2415919104 | bytes 6291456 | tf_op jit(solution)/shard_map/front/pallas_call | solution.py:404
  59.9 4.2 %all-to-all-start.1 = ((bf16[8,64,256]{2,1,0:T(8,128)(2,1)}), bf16[8,64,256]{2,1,0:T(8,128)(2,1)}, u32[]{:S(2)}, u32[]{:S(2)}) async-start(bf16[8,64,256]{2,1,0:T(8,128)(2,1)} %get-tuple-element.45), calls=%async_computation.1 | async-start | bytes 524288 | tf_op jit(solution)/shard_map/all_to_all | solution.py:371
  64.0 3.9 %turn.1 = (bf16[16,64,384]{2,1,0:T(8,128)(2,1)}, bf16[16,64,384]{2,1,0:T(8,128)(2,1)}) custom-call(s32[1]{0:T(128)} %bitcast.19.core_ref, bf16[384,2048]{1,0:T(8,128)(2,1)} %bitcast.2.refs_0_.rows_ref, bf16[384,768]{1,0:T(8,128)(2,1)} %get-tuple-element.47.token.act_ref), custom_call_target="tpu_custom_call" | custom-call | bytes 3145728 | tf_op jit(solution)/shard_map/turned/turn/pallas_call | solution.py:435
  77.0 5.6 %all-to-all-start.2 = ((bf16[8,48,256]{2,1,0:T(8,128)(2,1)}), bf16[8,48,256]{2,1,0:T(8,128)(2,1)S(1)}, u32[]{:S(2)}, u32[]{:S(2)}) async-start(bf16[8,48,256]{2,1,0:T(8,128)(2,1)} %bitcast.101), calls=%async_computation.2 | async-start | bytes 393216 | tf_op jit(solution)/shard_map/all_to_all | solution.py:371
  84.8 8.5 %all-to-all-done.2 = bf16[8,48,256]{2,1,0:T(8,128)(2,1)S(1)} async-done(((bf16[8,48,256]{2,1,0:T(8,128)(2,1)}), bf16[8,48,256]{2,1,0:T(8,128)(2,1)S(1)}, u32[]{:S(2)}, u32[]{:S(2)}) %all-to-all-start.2) | async-done | bytes 196640 | tf_op jit(solution)/shard_map/all_to_all | solution.py:371
  94.0 6.5 %back.1 = (bf16[384,2048]{1,0:T(8,128)(2,1)}, bf16[384,1536]{1,0:T(8,128)(2,1)}) custom-call(bf16[384,256]{1,0:T(8,128)(2,1)} %bitcast.94, bf16[768,256]{1,0:T(8,128)(2,1)} %fusion.2.refs_3_.mix_ref, bf16[384,768]{1,0:T(8,128)(2,1)} %get-tuple-element.51.one_ref, bf16[384,768]{1,0:T(8,128)(2,1)} %get-tuple-element.52.two_ref, bf16[2048,768]{1,0:T(8,128)(2,1)} %bitcast.82, ...), custom_call_target="tpu_custom_call" | custom-call | flops 2415919104 | bytes 6291456 | tf_op jit(solution)/shard_map/back/pallas_call | solution.py:477
  100.5 4.4 %all-to-all-start.3 = ((bf16[8,48,2048]{2,1,0:T(8,128)(2,1)}), bf16[8,48,2048]{2,1,0:T(8,128)(2,1)}, u32[]{:S(2)}, u32[]{:S(2)}) async-start(bf16[8,48,2048]{2,1,0:T(8,128)(2,1)} %bitcast.97), calls=%async_computation.3 | async-start | bytes 3145728 | tf_op jit(solution)/shard_map/all_to_all | solution.py:371
  107.4 6.8 %far.1 = (bf16[4,64,1152]{2,1,0:T(8,128)(2,1)}, bf16[4,64,1408]{2,1,0:T(8,128)(2,1)}, bf16[384,1536]{1,0:T(8,128)(2,1)}, bf16[768,256]{1,0:T(8,128)(2,1)}) custom-call(s32[2]{0:T(128)} %pad_add_fusion.refs_8_.coord_ref.refs_0_, bf16[4,4,64,384]{3,2,1,0:T(8,128)(2,1)} %bitcast.61, bf16[4,4,64,384]{3,2,1,0:T(8,128)(2,1)} %bitcast.68, ...), custom_call_target="tpu_custom_call" | custom-call | flops 301989888 | bytes 3145728 | tf_op jit(solution)/shard_map/far/pallas_call | solution.py:527
  114.2 3.0 %collective-permute-start.8 = (bf16[4,64,1152]{2,1,0:T(8,128)(2,1)}, bf16[4,64,1152]{2,1,0:T(8,128)(2,1)}, u32[]{:S(2)}, u32[]{:S(2)}) collective-permute-start(bf16[4,64,1152]{2,1,0:T(8,128)(2,1)} %get-tuple-element.62), channel_id=1, source_target_pairs={{0,32},{16,48},{32,0},{48,16},{1,33},{17,49},{33,1},{49,17},{2,34}... | collective-permute-start | bytes 1769480 | tf_op jit(solution)/shard_map/ppermute | solution.py:548
  118.4 6.7 %x_near.1 = (bf16[4,64,1152]{2,1,0:T(8,128)(2,1)}, bf16[4,64,1152]{2,1,0:T(8,128)(2,1)}) custom-call(s32[2]{0:T(128)} %pad_add_fusion.refs_8_.coord_ref.refs_0_, bf16[4,4,64,384]{3,2,1,0:T(8,128)(2,1)} %bitcast.63, bf16[4,4,64,384]{3,2,1,0:T(8,128)(2,1)} %bitcast.70, bf16[4,4,64,128]{3,2,1,0:T(8,128)(2,1)} %bitcast.88, bf16[4,4,64,128]{3,2,1,0:T(8,128)(2,1)} %bitcast.91, ...), custom_call_target="tpu_custom_call" | custom-call | flops 603979776 | bytes 6291456 | tf_op jit(solution)/shard_map/x_near/pallas_call | solution.py:527
  127.1 5.8 %y_near.1 = (bf16[4,64,1408]{2,1,0:T(8,128)(2,1)}, bf16[4,64,1408]{2,1,0:T(8,128)(2,1)}) custom-call(s32[2]{0:T(128)} %pad_add_fusion.refs_8_.coord_ref.refs_0_, bf16[4,4,64,384]{3,2,1,0:T(8,128)(2,1)} %bitcast.64, bf16[4,4,64,384]{3,2,1,0:T(8,128)(2,1)} %bitcast.71, bf16[4,4,64,256]{3,2,1,0:T(8,128)(2,1)} %bitcast.78, ...), custom_call_target="tpu_custom_call" | custom-call | flops 603979776 | bytes 6291456 | tf_op jit(solution)/shard_map/y_near/pallas_call | solution.py:527
  137.7 5.2 %own.1 = (bf16[4,64,1152]{2,1,0:T(8,128)(2,1)}, bf16[4,64,1408]{2,1,0:T(8,128)(2,1)}) custom-call(s32[2]{0:T(128)} %pad_add_fusion.refs_8_.coord_ref.refs_0_, bf16[4,4,64,384]{3,2,1,0:T(8,128)(2,1)} %bitcast.65, bf16[4,4,64,384]{3,2,1,0:T(8,128)(2,1)} %bitcast.72, bf16[4,4,64,128]{3,2,1,0:T(8,128)(2,1)} %bitcast.89, bf16[4,4,64,128]{3,2,1,0:T(8,128)(2,1)} %bitcast.92, ...), custom_call_target="tpu_custom_call" | custom-call | flops 301989888 | bytes 3145728 | tf_op jit(solution)/shard_map/own/pallas_call | solution.py:527
  146.8 10.0 %all-to-all-start.4 = ((f32[32,8,256]{2,1,0:T(8,128)}), f32[32,8,256]{2,1,0:T(8,128)S(1)}, u32[]{:S(2)}, u32[]{:S(2)}) async-start(f32[32,8,256]{2,1,0:T(8,128)} %bitcast.99), calls=%async_computation.4 | async-start | bytes 524288 | tf_op jit(solution)/shard_map/all_to_all | solution.py:641
  157.7 2.9 %second.1 = (f32[64,1408]{1,0:T(8,128)}, bf16[64,1408]{1,0:T(8,128)(2,1)}, bf16[64,1408]{1,0:T(8,128)(2,1)}, bf16[64,1408]{1,0:T(8,128)(2,1)}) custom-call(s32[2]{0:T(128)} %pad_add_fusion.refs_8_.coord_ref.refs_0_, bf16[4,64,1408]{2,1,0:T(8,128)(2,1)} %get-tuple-element.70.refs_0_, bf16[4,64,1408]{2,1,0:T(8,128)(2,1)} %copy-done.4, ...), custom_call_target="tpu_custom_call" | custom-call | bytes 4718592 | tf_op jit(solution)/shard_map/second/pallas_call | solution.py:619
  166.1 2.7 %collective-permute-start.12 = (bf16[64,896]{1,0:T(8,128)(2,1)}, bf16[64,896]{1,0:T(8,128)(2,1)S(1)}, u32[]{:S(2)}, u32[]{:S(2)}) collective-permute-start(bf16[64,896]{1,0:T(8,128)(2,1)} %get-tuple-element.68), channel_id=1, source_target_pairs={{0,128},{64,192},{128,0},{192,64},{1,129},{65,193},{129,1},{193,65... | collective-permute-start | bytes 344072 | tf_op jit(solution)/shard_map/ppermute | solution.py:49
  168.8 2.8 %convolution_convert_fusion = bf16[128,2048]{1,0:T(8,128)(2,1)} fusion(bf16[384,128]{1,0:T(8,128)(2,1)} %get-tuple-element.43, bf16[384,2048]{1,0:T(8,128)(2,1)} %bitcast.27.token), kind=kOutput, calls=%fused_computation.2 | convolution fusion | flops 201588736 | bytes 2195456 | tf_op jit(solution)/shard_map/hidden/dot_general | solution.py:21
  (94 shorter events, 45.3 us)
Async XLA Ops:
  3.7 48.7 %all-to-all-start = ((bf16[8,48,2048]{2,1,0:T(8,128)(2,1)}), bf16[8,48,2048]{2,1,0:T(8,128)(2,1)}, u32[]{:S(2)}, u32[]{:S(2)}) async-start(bf16[8,48,2048]{2,1,0:T(8,128)(2,1)} %bitcast.98), calls=%async_computation | async-start | bytes 3145728 | tf_op jit(solution)/shard_map/all_to_all | solution.py:371
  33.2 13.2 %collective-permute-start = (bf16[1024,128]{1,0:T(8,128)(2,1)S(1)}, bf16[1024,128]{1,0:T(8,128)(2,1)S(1)}, u32[]{:S(2)}, u32[]{:S(2)}) collective-permute-start(bf16[1024,128]{1,0:T(8,128)(2,1)S(1)} %bitcast.100), channel_id=1, source_target_pairs={{0,8},{8,0},{1,9},{9,1},{2,10},{10,2},{3,11},{11,3},{4,12},{12,4},... | collective-permute-start | bytes 786440 | tf_op jit(solution)/shard_map/weights_only/ppermute | solution.py:43
  59.9 14.7 %all-to-all-start.1 = ((bf16[8,64,256]{2,1,0:T(8,128)(2,1)}), bf16[8,64,256]{2,1,0:T(8,128)(2,1)}, u32[]{:S(2)}, u32[]{:S(2)}) async-start(bf16[8,64,256]{2,1,0:T(8,128)(2,1)} %get-tuple-element.45), calls=%async_computation.1 | async-start | bytes 524288 | tf_op jit(solution)/shard_map/all_to_all | solution.py:371
  68.0 16.8 %collective-permute-start.1 = (bf16[16,64,384]{2,1,0:T(8,128)(2,1)}, bf16[16,64,384]{2,1,0:T(8,128)(2,1)S(1)}, u32[]{:S(2)}, u32[]{:S(2)}) collective-permute-start(bf16[16,64,384]{2,1,0:T(8,128)(2,1)} %get-tuple-element.49.refs_7_), channel_id=1, source_target_pairs={{0,8},{8,0},{1,9},{9,1},{2,10},{10,2},{3,11},{11,3},{4,12},{12,4},... | collective-permute-start | bytes 2359304 | tf_op jit(solution)/shard_map/turned/ppermute | solution.py:43
  70.1 14.1 %collective-permute-start.3 = (bf16[384,768]{1,0:T(8,128)(2,1)}, bf16[384,768]{1,0:T(8,128)(2,1)}, u32[]{:S(2)}, u32[]{:S(2)}) collective-permute-start(bf16[384,768]{1,0:T(8,128)(2,1)} %get-tuple-element.47.token.act_ref), channel_id=1, source_target_pairs={{0,8},{8,0},{1,9},{9,1},{2,10},{10,2},{3,11},{11,3},{4,12},{12,4},... | collective-permute-start | bytes 1769480 | tf_op jit(solution)/shard_map/turned/ppermute | solution.py:43
  70.6 13.6 %collective-permute-start.4 = (bf16[384,768]{1,0:T(8,128)(2,1)}, bf16[384,768]{1,0:T(8,128)(2,1)}, u32[]{:S(2)}, u32[]{:S(2)}) collective-permute-start(bf16[384,768]{1,0:T(8,128)(2,1)} %get-tuple-element.51.one_ref), channel_id=1, source_target_pairs={{0,8},{8,0},{1,9},{9,1},{2,10},{10,2},{3,11},{11,3},{4,12},{12,4},... | collective-permute-start | bytes 1769480 | tf_op jit(solution)/shard_map/turned/ppermute | solution.py:43
  70.6 13.6 %collective-permute-start.5 = (bf16[384,768]{1,0:T(8,128)(2,1)}, bf16[384,768]{1,0:T(8,128)(2,1)}, u32[]{:S(2)}, u32[]{:S(2)}) collective-permute-start(bf16[384,768]{1,0:T(8,128)(2,1)} %get-tuple-element.52.two_ref), channel_id=1, source_target_pairs={{0,8},{8,0},{1,9},{9,1},{2,10},{10,2},{3,11},{11,3},{4,12},{12,4},... | collective-permute-start | bytes 1769480 | tf_op jit(solution)/shard_map/turned/ppermute | solution.py:43
  77.0 16.3 %all-to-all-start.2 = ((bf16[8,48,256]{2,1,0:T(8,128)(2,1)}), bf16[8,48,256]{2,1,0:T(8,128)(2,1)S(1)}, u32[]{:S(2)}, u32[]{:S(2)}) async-start(bf16[8,48,256]{2,1,0:T(8,128)(2,1)} %bitcast.101), calls=%async_computation.2 | async-start | bytes 393216 | tf_op jit(solution)/shard_map/all_to_all | solution.py:371
  82.7 1.5 collective-permute-start.2
  100.5 46.2 %all-to-all-start.3 = ((bf16[8,48,2048]{2,1,0:T(8,128)(2,1)}), bf16[8,48,2048]{2,1,0:T(8,128)(2,1)}, u32[]{:S(2)}, u32[]{:S(2)}) async-start(bf16[8,48,2048]{2,1,0:T(8,128)(2,1)} %bitcast.97), calls=%async_computation.3 | async-start | bytes 3145728 | tf_op jit(solution)/shard_map/all_to_all | solution.py:371
  105.0 1.7 collective-permute-start.6
  114.2 20.9 %collective-permute-start.8 = (bf16[4,64,1152]{2,1,0:T(8,128)(2,1)}, bf16[4,64,1152]{2,1,0:T(8,128)(2,1)}, u32[]{:S(2)}, u32[]{:S(2)}) collective-permute-start(bf16[4,64,1152]{2,1,0:T(8,128)(2,1)} %get-tuple-element.62), channel_id=1, source_target_pairs={{0,32},{16,48},{32,0},{48,16},{1,33},{17,49},{33,1},{49,17},{2,34}... | collective-permute-start | bytes 1769480 | tf_op jit(solution)/shard_map/ppermute | solution.py:548
  117.2 19.6 %collective-permute-start.7 = (bf16[4,64,1408]{2,1,0:T(8,128)(2,1)}, bf16[4,64,1408]{2,1,0:T(8,128)(2,1)S(1)}, u32[]{:S(2)}, u32[]{:S(2)}) collective-permute-start(bf16[4,64,1408]{2,1,0:T(8,128)(2,1)} %get-tuple-element.61), channel_id=1, source_target_pairs={{0,128},{64,192},{128,0},{192,64},{1,129},{65,193},{129,1},{193,65... | collective-permute-start | bytes 2162696 | tf_op jit(solution)/shard_map/ppermute | solution.py:548
  125.1 19.0 %collective-permute-start.10 = (bf16[4,64,1152]{2,1,0:T(8,128)(2,1)}, bf16[4,64,1152]{2,1,0:T(8,128)(2,1)}, u32[]{:S(2)}, u32[]{:S(2)}) collective-permute-start(bf16[4,64,1152]{2,1,0:T(8,128)(2,1)} %get-tuple-element.64), channel_id=1, source_target_pairs={{0,48},{16,0},{32,16},{48,32},{1,49},{17,1},{33,17},{49,33},{2,50}... | collective-permute-start | bytes 1769480 | tf_op jit(solution)/shard_map/ppermute | solution.py:548
  126.3 17.9 %collective-permute-start.9 = (bf16[4,64,1152]{2,1,0:T(8,128)(2,1)}, bf16[4,64,1152]{2,1,0:T(8,128)(2,1)}, u32[]{:S(2)}, u32[]{:S(2)}) collective-permute-start(bf16[4,64,1152]{2,1,0:T(8,128)(2,1)} %get-tuple-element.59.refs_7_), channel_id=1, source_target_pairs={{0,16},{16,32},{32,48},{48,0},{1,17},{17,33},{33,49},{49,1},{2,18}... | collective-permute-start | bytes 1769480 | tf_op jit(solution)/shard_map/ppermute | solution.py:548
  132.9 24.8 %collective-permute-start.14 = (bf16[4,64,1408]{2,1,0:T(8,128)(2,1)}, bf16[4,64,1408]{2,1,0:T(8,128)(2,1)}, u32[]{:S(2)}, u32[]{:S(2)}) collective-permute-start(bf16[4,64,1408]{2,1,0:T(8,128)(2,1)} %get-tuple-element.60.refs_0_), channel_id=1, source_target_pairs={{0,64},{64,128},{128,192},{192,0},{1,65},{65,129},{129,193},{193,1... | collective-permute-start | bytes 2162696 | tf_op jit(solution)/shard_map/ppermute | solution.py:548
  135.1 22.6 %collective-permute-start.15 = (bf16[4,64,1408]{2,1,0:T(8,128)(2,1)}, bf16[4,64,1408]{2,1,0:T(8,128)(2,1)}, u32[]{:S(2)}, u32[]{:S(2)}) collective-permute-start(bf16[4,64,1408]{2,1,0:T(8,128)(2,1)} %get-tuple-element.71), channel_id=1, source_target_pairs={{0,192},{64,0},{128,64},{192,128},{1,193},{65,1},{129,65},{193,129... | collective-permute-start | bytes 2162696 | tf_op jit(solution)/shard_map/ppermute | solution.py:548
  146.8 28.9 %all-to-all-start.4 = ((f32[32,8,256]{2,1,0:T(8,128)}), f32[32,8,256]{2,1,0:T(8,128)S(1)}, u32[]{:S(2)}, u32[]{:S(2)}) async-start(f32[32,8,256]{2,1,0:T(8,128)} %bitcast.99), calls=%async_computation.4 | async-start | bytes 524288 | tf_op jit(solution)/shard_map/all_to_all | solution.py:641
  156.8 12.0 %collective-permute-start.11 = (bf16[64,896]{1,0:T(8,128)(2,1)}, bf16[64,896]{1,0:T(8,128)(2,1)S(1)}, u32[]{:S(2)}, u32[]{:S(2)}) collective-permute-start(bf16[64,896]{1,0:T(8,128)(2,1)} %get-tuple-element.67), channel_id=1, source_target_pairs={{0,64},{64,128},{128,192},{192,0},{1,65},{65,129},{129,193},{193,1... | collective-permute-start | bytes 344072 | tf_op jit(solution)/shard_map/ppermute | solution.py:49
  160.6 14.4 %collective-permute-start.16 = (bf16[64,1408]{1,0:T(8,128)(2,1)}, bf16[64,1408]{1,0:T(8,128)(2,1)S(1)}, u32[]{:S(2)}, u32[]{:S(2)}) collective-permute-start(bf16[64,1408]{1,0:T(8,128)(2,1)} %get-tuple-element.73), channel_id=1, source_target_pairs={{0,16},{16,32},{32,48},{48,0},{1,17},{17,33},{33,49},{49,1},{2,18}... | collective-permute-start | bytes 540680 | tf_op jit(solution)/shard_map/ppermute | solution.py:49
  162.0 13.0 %collective-permute-start.17 = (bf16[64,1408]{1,0:T(8,128)(2,1)}, bf16[64,1408]{1,0:T(8,128)(2,1)S(1)}, u32[]{:S(2)}, u32[]{:S(2)}) collective-permute-start(bf16[64,1408]{1,0:T(8,128)(2,1)} %get-tuple-element.74), channel_id=1, source_target_pairs={{0,32},{16,48},{32,0},{48,16},{1,33},{17,49},{33,1},{49,17},{2,34}... | collective-permute-start | bytes 540680 | tf_op jit(solution)/shard_map/ppermute | solution.py:49
  164.7 11.0 %collective-permute-start.18 = (bf16[64,1408]{1,0:T(8,128)(2,1)}, bf16[64,1408]{1,0:T(8,128)(2,1)S(1)}, u32[]{:S(2)}, u32[]{:S(2)}) collective-permute-start(bf16[64,1408]{1,0:T(8,128)(2,1)} %get-tuple-element.75), channel_id=1, source_target_pairs={{0,48},{16,0},{32,16},{48,32},{1,49},{17,1},{33,17},{49,33},{2,50}... | collective-permute-start | bytes 540680 | tf_op jit(solution)/shard_map/ppermute | solution.py:49
  166.1 7.3 %collective-permute-start.12 = (bf16[64,896]{1,0:T(8,128)(2,1)}, bf16[64,896]{1,0:T(8,128)(2,1)S(1)}, u32[]{:S(2)}, u32[]{:S(2)}) collective-permute-start(bf16[64,896]{1,0:T(8,128)(2,1)} %get-tuple-element.68), channel_id=1, source_target_pairs={{0,128},{64,192},{128,0},{192,64},{1,129},{65,193},{129,1},{193,65... | collective-permute-start | bytes 344072 | tf_op jit(solution)/shard_map/ppermute | solution.py:49
  168.8 6.2 %collective-permute-start.13 = (bf16[64,896]{1,0:T(8,128)(2,1)}, bf16[64,896]{1,0:T(8,128)(2,1)S(1)}, u32[]{:S(2)}, u32[]{:S(2)}) collective-permute-start(bf16[64,896]{1,0:T(8,128)(2,1)} %get-tuple-element.69), channel_id=1, source_target_pairs={{0,192},{64,0},{128,64},{192,128},{1,193},{65,1},{129,65},{193,129... | collective-permute-start | bytes 344072 | tf_op jit(solution)/shard_map/ppermute | solution.py:49
  (20 other events, 132.6 us)
